TPU v7x, 256 devices: a whole 4x4x8 slice. The times are simulated.
256 devices in a mesh: sensor: 8 (over z), slab: 32 (over y, x, core).
Axes of the slice: x: 4, y: 4, z: 8, core: 2. Of those that a mesh axis runs over, the one named last changes fastest.
Arguments:
- volume: bfloat16 [32, 256, 4, 512], P('sensor', 'slab'), may hold values from -6 to 6
- measured: bfloat16 [512, 4, 128], P(('sensor', 'slab')), may hold values from -6 to 6
- blocks: bfloat16 [512, 160, 64, 128], P('sensor', 'slab'), may hold values from -0.0625 to 0.0625
- voxel_ids: int32 [512, 160], P('sensor', 'slab'), may hold values from 0 to 2047
- counts: int32 [512, 32], P('sensor', 'slab'), may hold values from 0 to 5, as said below
- exponents: int32 [512, 160], P('sensor', 'slab'), may hold values from -1 to 1
- conv_in: float32 [32, 2, 27], replicated, may hold values from -0.875 to 0.875
- conv_bias: float32 [32], replicated, may hold values from -3 to 3
- conv_out: float32 [32], replicated, may hold values from -1 to 1
Outputs:
- updated: float32 [32, 256, 4, 512], P('sensor', 'slab')
Inputs may be any that keep to these rules, and one draw needn't show every extreme that they name: `counts`: every sample block has 5 live slots in at least one slab.
All inputs are finite; a program needn't handle non-finite values.
Results may differ from a plain program's by a relative error of at most 0.006.
Values may be sent and summed in bfloat16 or wider, within the bound.
No kernel may reach another device: no remote copies, remote signals or barrier semaphores. Data moves between devices by JAX's collectives and lax.ppermute only.
A program may use at most 128 MiB of HBM per device.

v0:
```python
import functools

import jax
import jax.numpy as jnp
import numpy as np
from jax import lax
from jax.experimental import pallas as pl
from jax.experimental.pallas import tpu as pltpu
from jax.sharding import PartitionSpec as P

F32 = jnp.float32
BF16 = jnp.bfloat16
I32 = jnp.int32

JB = 64
KS = 5
SLOTS = JB * KS
NB = 4
TB = 128
OWN = 256
SHARD_ROWS = OWN + 16
CHAN = 32
TAPS = 192
SPLIT = 144


def vmem():
    return pl.BlockSpec(memory_space=pltpu.VMEM)


def smem():
    return pl.BlockSpec(memory_space=pltpu.SMEM)


def params(mib):
    return pltpu.CompilerParams(vmem_limit_bytes=mib * 1024 * 1024)


def cost(us):
    return pl.CostEstimate(flops=0, bytes_accessed=int(us * 3.0e6), transcendentals=0)


def lower_half(rows):
    return lax.broadcasted_iota(I32, (rows, 128), 1) < 64


def swapped(tile):
    return pltpu.roll(tile, 64, axis=1)


def pair_halves(first, second, low):
    return jnp.where(low, first, swapped(second)), jnp.where(low, swapped(first), second)


def prep_kernel(volume_ref, ids_ref, out_ref, rows):
    for i in range(32):
        image = volume_ref[i // 8, i % 8].astype(F32)
        for q in range(4):
            rows[q, 4 * i : 4 * i + 4, :] = image[:, 128 * q : 128 * q + 128]
    low = lower_half(32)
    for m in range(2):
        for q in range(4):
            one = rows[q, pl.ds(2 * m, 32, stride=4), :]
            two = rows[q, pl.ds(2 * m + 1, 32, stride=4), :]
            even, odd = pair_halves(one, two, low)
            out_ref[64 * q : 64 * q + 32, 128 * m : 128 * m + 128] = even.astype(BF16)
            out_ref[64 * q + 32 : 64 * q + 64, 128 * m : 128 * m + 128] = odd.astype(BF16)
    out_ref[OWN:SHARD_ROWS, :] = ids_ref[...]


def prep(volume, id_rows):
    return pl.pallas_call(
        prep_kernel,
        out_shape=jax.ShapeDtypeStruct((SHARD_ROWS, 256), BF16),
        in_specs=[vmem(), vmem()],
        out_specs=vmem(),
        scratch_shapes=[pltpu.VMEM((4, 128, 128), F32)],
        compiler_params=params(8),
        cost_estimate=cost(1.0),
        name="images_to_rows",
    )(volume, id_rows)


def add_gathered(acc, keys, weights, base, shard):
    lane = lax.broadcasted_iota(I32, (SLOTS, OWN), 1)
    hot = jnp.where(lane == keys - base, weights, 0.0).astype(BF16)
    return acc + jnp.dot(hot, shard, preferred_element_type=F32)


def gather_kernel(base_ref, keys_ref, weights_ref, *refs):
    shards, out_ref = refs[:-1], refs[-1]
    acc = jnp.zeros((SLOTS, 256), F32)
    for i, shard in enumerate(shards):
        acc = add_gathered(acc, keys_ref[...], weights_ref[...], base_ref[i], shard[0:OWN, :])
    out_ref[...] = acc


def gather_first(base, keys, weights, shards):
    return pl.pallas_call(
        gather_kernel,
        out_shape=jax.ShapeDtypeStruct((SLOTS, 256), F32),
        in_specs=[smem()] + [vmem()] * (2 + len(shards)),
        out_specs=vmem(),
        compiler_params=params(16),
        cost_estimate=cost(2.0),
        name="gather_first",
    )(base, keys, weights, *shards)


CHUNKS = 8


def start_blocks(blocks_ref, held, sems):
    step = JB // CHUNKS
    copies = [
        pltpu.make_async_copy(
            blocks_ref.at[pl.ds(c * step, step)], held.at[pl.ds(c * step, step)], sems.at[c]
        )
        for c in range(CHUNKS)
    ]
    for copy in copies:
        copy.start()
    return copies


def project_kernel(
    base_ref,
    slab_ref,
    keys_ref,
    weights_ref,
    before_ref,
    three_ref,
    minus_ref,
    half_a_ref,
    half_b_ref,
    measured_ref,
    blocks_ref,
    out_ref,
    held,
    far,
    lhs,
    total,
    sems,
):
    copies = start_blocks(blocks_ref, held, sems)
    far[0:SPLIT, :] = half_a_ref[...]
    far[SPLIT:SHARD_ROWS, :] = half_b_ref[...]
    acc = before_ref[...]
    keys, weights = keys_ref[...], weights_ref[...]
    for i, shard in enumerate((three_ref, minus_ref, far)):
        acc = add_gathered(acc, keys, weights, base_ref[5 + i], shard[0:OWN, :])
    low = lower_half(JB)
    for m in range(2):
        cols = slice(128 * m, 128 * m + 128)
        for q in range(3):
            one = acc[2 * q * JB : (2 * q + 1) * JB, cols]
            if q < 2:
                two = acc[(2 * q + 1) * JB : (2 * q + 2) * JB, cols]
                even, odd = pair_halves(one, two, low)
            else:
                even, odd = one, swapped(one)
            lhs[q, pl.ds(2 * m, JB, stride=4), :] = even
            lhs[q, pl.ds(2 * m + 1, JB, stride=4), :] = odd
    upper = lax.broadcasted_iota(I32, (8, TB), 0) < 4
    for c in range(CHUNKS):
        copies[c].wait()
        for p in range(c * (JB // CHUNKS) // 2, (c + 1) * (JB // CHUNKS) // 2):
            at = slice(8 * p, 8 * p + 8)
            left = jnp.concatenate([lhs[0, at], lhs[1, at], lhs[2, at, 0:64]], axis=1).astype(BF16)
            both = jnp.concatenate([held[2 * p], held[2 * p + 1]], axis=1)
            got = jnp.dot(left, both, preferred_element_type=F32)
            total[8 * p : 8 * p + 8, :] = jnp.where(upper, got[:, :TB], got[:, TB:])
    mine = pl.ds(pl.multiple_of(slab_ref[0] * 8, 8), 8)
    total[mine, :] = total[mine, :] - measured_ref[...]
    out_ref[...] = total[...].astype(BF16)


def project(base, slab, keys, weights, before, rest, measured, blocks):
    return pl.pallas_call(
        project_kernel,
        out_shape=jax.ShapeDtypeStruct((JB * NB, TB), BF16),
        in_specs=[smem(), smem()]
        + [vmem()] * 8
        + [pl.BlockSpec(memory_space=pl.ANY)],
        out_specs=vmem(),
        scratch_shapes=[
            pltpu.VMEM((JB, KS * 64, TB), BF16),
            pltpu.VMEM((SHARD_ROWS, 256), BF16),
            pltpu.VMEM((3, JB * NB, 128), F32),
            pltpu.VMEM((JB * NB, TB), F32),
            pltpu.SemaphoreType.DMA((CHUNKS,)),
        ],
        compiler_params=params(24),
        cost_estimate=cost(4.0),
        name="project",
    )(base, slab, keys, weights, before, *rest, measured, blocks)


def adjoint_kernel(
    own_ref, one_ref, two_ref, three_ref, weights_ref, blocks_ref, out_ref, held, resid, back, sems
):
    copies = start_blocks(blocks_ref, held, sems)
    back[2] = jnp.zeros((JB * NB, 128), F32)
    total = own_ref[...].astype(F32) + one_ref[...].astype(F32)
    total = total + two_ref[...].astype(F32) + three_ref[...].astype(F32)
    resid[...] = total.astype(BF16).astype(F32)
    upper = lax.broadcasted_iota(I32, (8, KS * 64), 0) < 4
    dims = (((1,), (1,)), ((), ()))
    for c in range(CHUNKS):
        copies[c].wait()
        for p in range(c * (JB // CHUNKS) // 2, (c + 1) * (JB // CHUNKS) // 2):
            left = resid[8 * p : 8 * p + 8, :].astype(BF16)
            a = lax.dot_general(left, held[2 * p], dims, preferred_element_type=F32)
            b = lax.dot_general(left, held[2 * p + 1], dims, preferred_element_type=F32)
            got = jnp.where(upper, a, b)
            at = slice(8 * p, 8 * p + 8)
            back[0, at, :] = got[:, 0:128]
            back[1, at, :] = got[:, 128:256]
            back[2, at, 0:64] = got[:, 256 : KS * 64]
    low = lower_half(JB)
    for m in range(2):
        for q in range(3):
            one = back[q, pl.ds(2 * m, JB, stride=4), :]
            two = back[q, pl.ds(2 * m + 1, JB, stride=4), :]
            even, odd = pair_halves(one, two, low)
            for k, part in ((2 * q, even), (2 * q + 1, odd)):
                if k < KS:
                    scaled = part * weights_ref[k * JB : (k + 1) * JB, :]
                    out_ref[k * JB : (k + 1) * JB, 128 * m : 128 * m + 128] = scaled.astype(BF16)


def adjoint(parts, weights, blocks):
    return pl.pallas_call(
        adjoint_kernel,
        out_shape=jax.ShapeDtypeStruct((SLOTS, 256), BF16),
        in_specs=[vmem()] * 5 + [pl.BlockSpec(memory_space=pl.ANY)],
        out_specs=vmem(),
        scratch_shapes=[
            pltpu.VMEM((JB, KS * 64, TB), BF16),
            pltpu.VMEM((JB * NB, TB), F32),
            pltpu.VMEM((3, JB * NB, 128), F32),
            pltpu.SemaphoreType.DMA((CHUNKS,)),
        ],
        compiler_params=params(24),
        cost_estimate=cost(4.0),
        name="adjoint",
    )(*parts, weights, blocks)


def rows_to_planes(rows, out_ref):
    low = lower_half(48)
    for m in range(2):
        for q in range(4):
            one = rows[96 * q : 96 * q + 48, 128 * m : 128 * m + 128]
            two = rows[96 * q + 48 : 96 * q + 96, 128 * m : 128 * m + 128]
            even, odd = pair_halves(one, two, low)
            out_ref[2 * m, q] = even
            out_ref[2 * m + 1, q] = odd


def edge_rows(planes_ref, place, z):
    for n in range(NB):
        for q in range(4):
            rows = planes_ref[n, q, pl.ds(z, 6, stride=8), :]
            place[n * 6 : n * 6 + 6, 128 * q : 128 * q + 128] = rows


def images_kernel(
    pos_ref,
    own_ref,
    plus_ref,
    minus_ref,
    *refs,
):
    others, (planes_ref, low_ref, high_ref, index_ref, rows) = refs[:-5], refs[-5:]
    sensor, last = pos_ref[0], pos_ref[1]
    keep_low = jnp.where(sensor > 0, 1.0, 0.0).astype(F32)
    keep_high = jnp.where(sensor < last, 1.0, 0.0).astype(F32)
    for h in range(8):
        block = slice(32 * h, 32 * h + 32)
        rows[48 * h : 48 * h + 8, :] = plus_ref[block, :].astype(F32)[24:32] * keep_low
        rows[48 * h + 8 : 48 * h + 40, :] = own_ref[block, :].astype(F32)
        rows[48 * h + 40 : 48 * h + 48, :] = minus_ref[block, :].astype(F32)[0:8] * keep_high
    rows_to_planes(rows, planes_ref)
    edge_rows(planes_ref, low_ref, 0)
    edge_rows(planes_ref, high_ref, 7)
    sources = [own_ref, plus_ref, minus_ref, *others[:-1]]
    for g in range(8):
        if g < 7:
            coded = sources[g][OWN:SHARD_ROWS, :].astype(F32)
        else:
            coded = others[-1][OWN - SPLIT : SHARD_ROWS - SPLIT, :].astype(F32)
        ids = (coded[0:2] * 16.0 + coded[2:4]).astype(I32)
        x = (ids >> 6) - 4 * sensor + 1
        row = (ids & 7) * 48 + x * 8 + ((ids >> 3) & 7)
        index_ref[g] = jnp.where((x >= 0) & (x < 6), row, -1)


def images(pos, shards):
    return pl.pallas_call(
        images_kernel,
        out_shape=[
            jax.ShapeDtypeStruct((NB, 4, 48, 128), F32),
            jax.ShapeDtypeStruct((24, 512), F32),
            jax.ShapeDtypeStruct((24, 512), F32),
            jax.ShapeDtypeStruct((8, 2, 256), I32),
        ],
        in_specs=[smem()] + [vmem()] * len(shards),
        out_specs=[vmem()] * 4,
        scratch_shapes=[pltpu.VMEM((384, 256), F32)],
        compiler_params=params(16),
        cost_estimate=cost(2.0),
        name="images_to_planes",
    )(pos, *shards)


def add_scattered(acc, index, contrib):
    first = lax.broadcasted_iota(I32, (384, 256), 0)
    second = lax.broadcasted_iota(I32, (384, SLOTS - 256), 0)
    hot = jnp.where(first == index[0:1, :], 1.0, 0.0).astype(BF16)
    more = jnp.where(second == index[1:2, 0 : SLOTS - 256], 1.0, 0.0).astype(BF16)
    acc = acc + jnp.dot(hot, contrib[0:256, :], preferred_element_type=F32)
    return acc + jnp.dot(more, contrib[256:SLOTS, :], preferred_element_type=F32)


def scatter_kernel(index_ref, *refs):
    contribs, out_ref = refs[:-1], refs[-1]
    acc = jnp.zeros((384, 256), F32)
    for i, contrib in enumerate(contribs):
        acc = add_scattered(acc, index_ref[i], contrib)
    out_ref[...] = acc


def scatter_first(index, contribs):
    return pl.pallas_call(
        scatter_kernel,
        out_shape=jax.ShapeDtypeStruct((384, 256), F32),
        in_specs=[vmem()] * (1 + len(contribs)),
        out_specs=vmem(),
        compiler_params=params(16),
        cost_estimate=cost(2.0),
        name="scatter_first",
    )(index, *contribs)


def gradient_kernel(
    index_ref,
    before_ref,
    three_ref,
    minus_ref,
    half_a_ref,
    half_b_ref,
    image_low_ref,
    image_high_ref,
    planes_ref,
    low_ref,
    high_ref,
    far,
    rows,
    edge,
):
    far[0 : SLOTS // 2, :] = half_a_ref[...]
    far[SLOTS // 2 : SLOTS, :] = half_b_ref[...]
    acc = before_ref[...]
    for i, contrib in enumerate((three_ref, minus_ref, far)):
        acc = add_scattered(acc, index_ref[5 + i], contrib)
    rows[...] = acc
    rows_to_planes(rows, planes_ref)
    edge[0:24, :] = image_low_ref[...]
    edge_rows(planes_ref, edge.at[pl.ds(24, 24)], 0)
    low_ref[...] = edge[...].astype(BF16)
    edge[0:24, :] = image_high_ref[...]
    edge_rows(planes_ref, edge.at[pl.ds(24, 24)], 7)
    high_ref[...] = edge[...].astype(BF16)


def gradient_planes(index, before, rest, image_low, image_high):
    return pl.pallas_call(
        gradient_kernel,
        out_shape=[
            jax.ShapeDtypeStruct((NB, 4, 48, 128), F32),
            jax.ShapeDtypeStruct((48, 512), BF16),
            jax.ShapeDtypeStruct((48, 512), BF16),
        ],
        in_specs=[vmem()] * 8,
        out_specs=[vmem()] * 3,
        scratch_shapes=[
            pltpu.VMEM((SLOTS, 256), BF16),
            pltpu.VMEM((384, 256), F32),
            pltpu.VMEM((48, 512), F32),
        ],
        compiler_params=params(16),
        cost_estimate=cost(2.0),
        name="gradient_planes",
    )(index, before, *rest, image_low, image_high)


def shifted_rows(rows, e):
    if e == 1:
        return rows
    y = lax.broadcasted_iota(I32, rows.shape, 1)
    if e == 0:
        return jnp.where(y == 0, 0.0, pltpu.roll(rows, 1, axis=1))
    return jnp.where(y == 511, 0.0, pltpu.roll(rows, 511, axis=1))


def conv_kernel(
    image_ref, grad_ref, low_ref, high_ref, matrix_ref, out_w_ref, out_ref, body, ends, done
):
    for kind, (ref, start) in enumerate(((low_ref, 0), (high_ref, 0), (low_ref, 24), (high_ref, 24))):
        rows = ref[...].astype(F32)[start : start + 24]
        for e in range(3):
            moved = shifted_rows(rows, e)
            for q in range(4):
                ends[q, pl.ds(kind + 4 * e, 24, stride=16), :] = moved[:, 128 * q : 128 * q + 128]
    for q in range(4):
        ends[q, pl.ds(12, 24, stride=16), :] = jnp.ones((24, 128), F32)
        for r in range(13, 16):
            ends[q, pl.ds(r, 24, stride=16), :] = jnp.zeros((24, 128), F32)
    for n in range(NB):
        for x in range(6):
            rows = jnp.concatenate(
                [
                    jnp.concatenate([ref[n, q, 8 * x : 8 * x + 8, :] for q in range(4)], axis=1)
                    for ref in (image_ref, grad_ref)
                ],
                axis=0,
            )
            for e in range(3):
                body[e, n * 6 + x] = shifted_rows(rows, e).astype(BF16)

    def one_x(x, carry):
        for n in range(NB):
            for half in range(2):
                cols = slice(256 * half, 256 * half + 256)
                tiles = [body[e, n * 6 + x + a, :, cols] for a in range(3) for e in range(3)]
                for a in range(3):
                    at = pl.multiple_of((n * 6 + x + a) * 16, 16)
                    pair = [ends[2 * half + q, pl.ds(at, 16), :] for q in range(2)]
                    tiles.append(jnp.concatenate(pair, axis=1).astype(BF16))
                stack = jnp.concatenate(tiles, axis=0)
                hidden = jnp.dot(matrix_ref[0], stack, preferred_element_type=F32)
                hidden = hidden + jnp.dot(matrix_ref[1], stack, preferred_element_type=F32)
                at = pl.multiple_of(8 * x + 8, 8)
                pair = [image_ref[n, 2 * half + q, pl.ds(at, 8), :] for q in range(2)]
                total = jnp.concatenate(pair, axis=1)
                for c in range(CHAN):
                    total = total + jnp.maximum(hidden[8 * c : 8 * c + 8], 0.0) * out_w_ref[c]
                for q in range(2):
                    part = total[:, 128 * q : 128 * q + 128]
                    done[2 * half + q, pl.ds(n, 8, stride=4), :] = part
        for z in range(8):
            for q in range(4):
                out_ref[x, z, :, 128 * q : 128 * q + 128] = done[q, 4 * z : 4 * z + 4, :]
        return carry

    lax.fori_loop(0, 4, one_x, 0)


def convolve(image, grad, low, high, matrix, out_w):
    return pl.pallas_call(
        conv_kernel,
        out_shape=jax.ShapeDtypeStruct((4, 8, NB, 512), F32),
        in_specs=[vmem()] * 5 + [smem()],
        out_specs=vmem(),
        scratch_shapes=[
            pltpu.VMEM((3, 24, 16, 512), BF16),
            pltpu.VMEM((4, 384, 128), F32),
            pltpu.VMEM((4, 32, 128), F32),
        ],
        compiler_params=params(32),
        cost_estimate=cost(5.0),
        name="convolutions",
    )(image, grad, low, high, matrix, out_w)


def tap_choice():
    choice = np.zeros((55, 8, TAPS), np.float32)
    for z in range(8):
        for a in range(3):
            for e in range(3):
                for i in range(2):
                    for plane in range(-1, 9):
                        b = plane - z + 1
                        if not 0 <= b <= 2:
                            continue
                        if 0 <= plane < 8:
                            column = (a * 3 + e) * 16 + i * 8 + plane
                        else:
                            column = 144 + a * 16 + i * 2 + (plane > 0) + 4 * e
                        choice[i * 27 + (a * 3 + b) * 3 + e, z, column] = 1.0
        choice[54, z, 144 + 12] = 1.0
    return choice


def conv_matrix(conv_in, conv_bias):
    table = jnp.concatenate([conv_in.reshape(CHAN, 54), conv_bias[:, None]], axis=1)
    high = lax.reduce_precision(table, 8, 7)
    parts = jnp.concatenate([high, table - high], axis=0).astype(BF16)
    choice = jnp.asarray(tap_choice().reshape(55, 8 * TAPS), BF16)
    spread = jnp.dot(parts, choice, preferred_element_type=F32).astype(BF16)
    return spread.reshape(2, CHAN * 8, TAPS)


def ring(distance, count):
    return [(i, (i + distance) % count) for i in range(count)]


def slab_perm(dy, dx, core):
    def index(y, x, c):
        return (y % 4 * 4 + x % 4) * 2 + c

    return [
        (index(y, x, c), index(y + dy, x + dx, c ^ core))
        for y in range(4)
        for x in range(4)
        for c in range(2)
    ]


def from_sensor(block, distance):
    return lax.ppermute(block, "sensor", ring(distance, 8))


def spread_near(block):
    return [from_sensor(block, d) for d in (1, -1, 2, -2)]


def spread_far(near, split):
    plus, minus = near[2], near[3]
    return [
        from_sensor(plus, 1),
        from_sensor(minus, -1),
        from_sensor(plus[:split], 2),
        from_sensor(minus[split:], -2),
    ]


def slab_sum_parts(partial):
    other = lax.ppermute(partial, "slab", slab_perm(0, 0, 1))
    total = partial.astype(F32) + other.astype(F32)
    total = total.astype(BF16)
    moved = [lax.ppermute(total, "slab", slab_perm(0, d, 0)) for d in (1, 3, 2)]
    row = total.astype(F32) + moved[0].astype(F32) + moved[1].astype(F32) + moved[2].astype(F32)
    row = row.astype(BF16)
    return [row] + [lax.ppermute(row, "slab", slab_perm(d, 0, 0)) for d in (1, 3, 2)]


def slot_weights(live_slots, exponents):
    slot_iota = lax.broadcasted_iota(I32, exponents.shape, 1)
    scaled = jnp.exp2(exponents.astype(F32))
    return jnp.where(slot_iota < live_slots[:, None], scaled, jnp.zeros_like(scaled))


def on_device(volume, measured, blocks, voxel_ids, counts, exponents, conv_in, conv_bias, conv_out):
    sensor = lax.axis_index("sensor").astype(I32)
    slab = lax.axis_index("slab").astype(I32)
    steps = jnp.array([0, -1, 1, -2, 2, -3, 3, 4], I32)
    base = ((sensor + steps) % 8) * OWN
    pos = jnp.stack([sensor, jnp.full_like(sensor, 7)])
    ids = voxel_ids.T.reshape(SLOTS)
    padded = jnp.pad(ids, (0, 512 - SLOTS), constant_values=4080).reshape(2, 256)
    id_rows = jnp.concatenate([padded >> 4, padded & 15, jnp.zeros((12, 256), I32)], axis=0)
    keys = (ids & ~255) | ((ids & 7) << 5) | ((ids >> 3) & 31)
    keys = keys.reshape(SLOTS, 1)
    weights = slot_weights(counts[:, 0], exponents).T.reshape(SLOTS, 1)
    stacked = blocks.reshape(JB, KS * 64, TB)

    shard = prep(volume, id_rows.astype(BF16))
    near = spread_near(shard)
    far = spread_far(near, SPLIT)
    before = gather_first(base, keys, weights, [shard, *near])
    partial = project(
        base, slab.reshape(1), keys, weights, before, far,
        measured.reshape(8, TB).astype(F32), stacked,
    )
    parts = slab_sum_parts(partial)
    matrix = conv_matrix(conv_in, conv_bias)
    image, image_low, image_high, index = images(
        pos, [shard, *near, far[0], far[1], far[3]]
    )
    contrib = adjoint(parts, weights, stacked)
    near_c = spread_near(contrib)
    far_c = spread_far(near_c, SLOTS // 2)
    sums = scatter_first(index, [contrib, *near_c])
    grad, low_out, high_out = gradient_planes(index, sums, far_c, image_low, image_high)
    forward = [(i, i + 1) for i in range(31)]
    backward = [(i + 1, i) for i in range(31)]
    low_in = lax.ppermute(high_out, "slab", forward)
    high_in = lax.ppermute(low_out, "slab", backward)
    return convolve(image, grad, low_in, high_in, matrix, conv_out)


def solution(mesh):
    in_specs = (
        P("sensor", "slab", None, None),
        P(("sensor", "slab"), None, None),
        P("sensor", "slab", None, None),
        P("sensor", "slab"),
        P("sensor", "slab"),
        P("sensor", "slab"),
        P(),
        P(),
        P(),
    )
    out_specs = P("sensor", "slab", None, None)
    return jax.shard_map(
        on_device, mesh=mesh, in_specs=in_specs, out_specs=out_specs, check_vma=False
    )
```

profile of v0, /device:TPU:7, one launch (start us, length us, event | category | flops | bytes accessed | tf_op | source)
XLA Modules:
  0.0 99.1 jit_solution(10837278469871989597)
XLA Ops:
  2.0 1.7 %collective-permute-start = (bf16[272,256]{1,0:T(8,128)(2,1)S(1)}, bf16[272,256]{1,0:T(8,128)(2,1)S(1)}, u32[]{:S(2)}, u32[]{:S(2)}) collective-permute-start(bf16[272,256]{1,0:T(8,128)(2,1)S(1)} %images_to_rows.1.own_ref.refs_0_), channel_id=1, source_target_pairs={{0,32},{32,64},{64,96},{96,128},{128,160},{160,192},{192,224},{224... | collective-permute-start | bytes 417800 | tf_op jit(solution)/shard_map/ppermute | solution.py:522
  3.7 4.0 %collective-permute-start.1 = (bf16[272,256]{1,0:T(8,128)(2,1)S(1)}, bf16[272,256]{1,0:T(8,128)(2,1)S(1)}, u32[]{:S(2)}, u32[]{:S(2)}) collective-permute-start(bf16[272,256]{1,0:T(8,128)(2,1)S(1)} %images_to_rows.1.own_ref.refs_0_), channel_id=1, source_target_pairs={{0,224},{32,0},{64,32},{96,64},{128,96},{160,128},{192,160},{224,1... | collective-permute-start | bytes 417800 | tf_op jit(solution)/shard_map/ppermute | solution.py:522
  7.8 3.6 %collective-permute-start.3 = (bf16[272,256]{1,0:T(8,128)(2,1)S(1)}, bf16[272,256]{1,0:T(8,128)(2,1)S(1)}, u32[]{:S(2)}, u32[]{:S(2)}) collective-permute-start(bf16[272,256]{1,0:T(8,128)(2,1)S(1)} %images_to_rows.1.own_ref.refs_0_), channel_id=1, source_target_pairs={{0,192},{32,224},{64,0},{96,32},{128,64},{160,96},{192,128},{224,1... | collective-permute-start | bytes 417800 | tf_op jit(solution)/shard_map/ppermute | solution.py:522
  12.7 5.7 %collective-permute-done.3.refs_1_.refs_4_ = bf16[272,256]{1,0:T(8,128)(2,1)S(1)} collective-permute-done((bf16[272,256]{1,0:T(8,128)(2,1)S(1)}, bf16[272,256]{1,0:T(8,128)(2,1)S(1)}, u32[]{:S(2)}, u32[]{:S(2)}) %collective-permute-start.3) | collective-permute-done | bytes 139296 | tf_op jit(solution)/shard_map/ppermute | solution.py:522
  18.4 2.6 %collective-permute-start.6 = (bf16[128,256]{1,0:T(8,128)(2,1)S(1)}, bf16[128,256]{1,0:T(8,128)(2,1)S(1)}, u32[]{:S(2)}, u32[]{:S(2)}) collective-permute-start(bf16[128,256]{1,0:T(8,128)(2,1)S(1)} %slice.16), channel_id=1, source_target_pairs={{0,192},{32,224},{64,0},{96,32},{128,64},{160,96},{192,128},{224,1... | collective-permute-start | bytes 196616 | tf_op jit(solution)/shard_map/ppermute | solution.py:522
  21.9 2.7 %collective-permute-start.5 = (bf16[272,256]{1,0:T(8,128)(2,1)S(1)}, bf16[272,256]{1,0:T(8,128)(2,1)S(1)}, u32[]{:S(2)}, u32[]{:S(2)}) collective-permute-start(bf16[272,256]{1,0:T(8,128)(2,1)S(1)} %collective-permute-done.3.refs_1_.refs_4_), channel_id=1, source_target_pairs={{0,224},{32,0},{64,32},{96,64},{128,96},{160,128},{192,160},{224,1... | collective-permute-start | bytes 417800 | tf_op jit(solution)/shard_map/ppermute | solution.py:522
  26.2 1.0 %gather_first.1.before_ref = f32[320,256]{1,0:T(8,128)S(1)} custom-call(s32[8]{0:T(128)S(1)} %fusion.5.base_ref, s32[320,1]{1,0:T(8,128)S(1)} %or.27.keys_ref, f32[320,1]{1,0:T(8,128)S(1)} %reshape.88.weights_ref, bf16[272,256]{1,0:T(8,128)(2,1)S(1)} %images_to_rows.1.own_ref.refs_0_, bf16[272,256]{1,0:T(8,128)(2,1)S(1)} %collective-permute-done.plus_ref.refs_1_, ...), custom_call_target="tpu_custom_call" | custom-call | bytes 6000000 | tf_op jit(solution)/shard_map/gather_first/pallas_call | solution.py:99
  27.3 2.2 %collective-permute-done.4.refs_2_.three_ref = bf16[272,256]{1,0:T(8,128)(2,1)S(1)} collective-permute-done((bf16[272,256]{1,0:T(8,128)(2,1)S(1)}, bf16[272,256]{1,0:T(8,128)(2,1)S(1)}, u32[]{:S(2)}, u32[]{:S(2)}) %collective-permute-start.4) | collective-permute-done | bytes 139296 | tf_op jit(solution)/shard_map/ppermute | solution.py:522
  29.5 2.5 %copy-done = bf16[64,5,64,128]{3,2,1,0:T(8,128)(2,1)S(1)} copy-done((bf16[64,5,64,128]{3,2,1,0:T(8,128)(2,1)S(1)}, bf16[64,5,64,128]{3,2,1,0:T(8,128)(2,1)}, u32[]{:S(2)}) %copy-start) | copy-done | bytes 5242904
  32.0 4.6 %project.1 = bf16[256,128]{1,0:T(8,128)(2,1)S(1)} custom-call(s32[8]{0:T(128)S(1)} %fusion.5.base_ref, s32[1]{0:T(128)} %bitcast.2.slab_ref, s32[320,1]{1,0:T(8,128)S(1)} %or.27.keys_ref, f32[320,1]{1,0:T(8,128)S(1)} %reshape.88.weights_ref, f32[320,256]{1,0:T(8,128)S(1)} %gather_first.1.before_ref, ...), custom_call_target="tpu_custom_call" | custom-call | bytes 12000000 | tf_op jit(solution)/shard_map/project/pallas_call | solution.py:179
  36.6 1.3 %collective-permute-start.8 = (bf16[256,128]{1,0:T(8,128)(2,1)S(1)}, bf16[256,128]{1,0:T(8,128)(2,1)S(1)}, u32[]{:S(2)}, u32[]{:S(2)}) collective-permute-start(bf16[256,128]{1,0:T(8,128)(2,1)S(1)} %project.1), channel_id=1, source_target_pairs={{0,1},{1,0},{2,3},{3,2},{4,5},{5,4},{6,7},{7,6},{8,9},{9,8},{10,11... | collective-permute-start | bytes 196616 | tf_op jit(solution)/shard_map/ppermute | solution.py:540
  38.9 1.2 %collective-permute-start.11 = (bf16[256,128]{1,0:T(8,128)(2,1)S(1)}, bf16[256,128]{1,0:T(8,128)(2,1)S(1)}, u32[]{:S(2)}, u32[]{:S(2)}) collective-permute-start(bf16[256,128]{1,0:T(8,128)(2,1)S(1)} %add_convert_fusion.1), channel_id=1, source_target_pairs={{0,4},{1,5},{2,6},{3,7},{4,0},{5,1},{6,2},{7,3},{8,12},{9,13},{10,... | collective-permute-start | bytes 196616 | tf_op jit(solution)/shard_map/ppermute | solution.py:543
  40.1 2.7 %collective-permute-start.9 = (bf16[256,128]{1,0:T(8,128)(2,1)S(1)}, bf16[256,128]{1,0:T(8,128)(2,1)S(1)}, u32[]{:S(2)}, u32[]{:S(2)}) collective-permute-start(bf16[256,128]{1,0:T(8,128)(2,1)S(1)} %add_convert_fusion.1), channel_id=1, source_target_pairs={{0,2},{1,3},{2,4},{3,5},{4,6},{5,7},{6,0},{7,1},{8,10},{9,11},{10,... | collective-permute-start | bytes 196616 | tf_op jit(solution)/shard_map/ppermute | solution.py:543
  43.6 2.1 %collective-permute-done.10 = bf16[256,128]{1,0:T(8,128)(2,1)S(1)} collective-permute-done((bf16[256,128]{1,0:T(8,128)(2,1)S(1)}, bf16[256,128]{1,0:T(8,128)(2,1)S(1)}, u32[]{:S(2)}, u32[]{:S(2)}) %collective-permute-start.10) | collective-permute-done | bytes 65568 | tf_op jit(solution)/shard_map/ppermute | solution.py:543
  45.7 1.4 %collective-permute-start.12 = (bf16[256,128]{1,0:T(8,128)(2,1)S(1)}, bf16[256,128]{1,0:T(8,128)(2,1)S(1)}, u32[]{:S(2)}, u32[]{:S(2)}) collective-permute-start(bf16[256,128]{1,0:T(8,128)(2,1)S(1)} %add_convert_fusion.own_ref), channel_id=1, source_target_pairs={{0,8},{1,9},{2,10},{3,11},{4,12},{5,13},{6,14},{7,15},{8,16},{9,17... | collective-permute-start | bytes 196616 | tf_op jit(solution)/shard_map/ppermute | solution.py:546
  47.1 1.7 %collective-permute-start.13 = (bf16[256,128]{1,0:T(8,128)(2,1)S(1)}, bf16[256,128]{1,0:T(8,128)(2,1)S(1)}, u32[]{:S(2)}, u32[]{:S(2)}) collective-permute-start(bf16[256,128]{1,0:T(8,128)(2,1)S(1)} %add_convert_fusion.own_ref), channel_id=1, source_target_pairs={{0,24},{1,25},{2,26},{3,27},{4,28},{5,29},{6,30},{7,31},{8,0},{9,1... | collective-permute-start | bytes 196616 | tf_op jit(solution)/shard_map/ppermute | solution.py:546
  48.8 1.4 %collective-permute-start.14 = (bf16[256,128]{1,0:T(8,128)(2,1)S(1)}, bf16[256,128]{1,0:T(8,128)(2,1)S(1)}, u32[]{:S(2)}, u32[]{:S(2)}) collective-permute-start(bf16[256,128]{1,0:T(8,128)(2,1)S(1)} %add_convert_fusion.own_ref), channel_id=1, source_target_pairs={{0,16},{1,17},{2,18},{3,19},{4,20},{5,21},{6,22},{7,23},{8,24},{9,... | collective-permute-start | bytes 196616 | tf_op jit(solution)/shard_map/ppermute | solution.py:546
  50.2 3.2 %collective-permute-done.14.three_ref = bf16[256,128]{1,0:T(8,128)(2,1)S(1)} collective-permute-done((bf16[256,128]{1,0:T(8,128)(2,1)S(1)}, bf16[256,128]{1,0:T(8,128)(2,1)S(1)}, u32[]{:S(2)}, u32[]{:S(2)}) %collective-permute-start.14) | collective-permute-done | bytes 65568 | tf_op jit(solution)/shard_map/ppermute | solution.py:546
  53.4 4.4 %adjoint.1.refs_0_ = bf16[320,256]{1,0:T(8,128)(2,1)S(1)} custom-call(bf16[256,128]{1,0:T(8,128)(2,1)S(1)} %add_convert_fusion.own_ref, bf16[256,128]{1,0:T(8,128)(2,1)S(1)} %collective-permute-done.12.one_ref, bf16[256,128]{1,0:T(8,128)(2,1)S(1)} %collective-permute-done.13.two_ref, bf16[256,128]{1,0:T(8,128)(2,1)S(1)} %collective-permute-done.14.three_ref, ...), custom_call_target="tpu_custom_call" | custom-call | bytes 12000000 | tf_op jit(solution)/shard_map/adjoint/pallas_call | solution.py:233
  57.8 1.3 %collective-permute-start.17 = (bf16[320,256]{1,0:T(8,128)(2,1)S(1)}, bf16[320,256]{1,0:T(8,128)(2,1)S(1)}, u32[]{:S(2)}, u32[]{:S(2)}) collective-permute-start(bf16[320,256]{1,0:T(8,128)(2,1)S(1)} %adjoint.1.refs_0_), channel_id=1, source_target_pairs={{0,64},{32,96},{64,128},{96,160},{128,192},{160,224},{192,0},{224,... | collective-permute-start | bytes 491528 | tf_op jit(solution)/shard_map/ppermute | solution.py:522
  59.1 2.4 %collective-permute-start.18 = (bf16[320,256]{1,0:T(8,128)(2,1)S(1)}, bf16[320,256]{1,0:T(8,128)(2,1)S(1)}, u32[]{:S(2)}, u32[]{:S(2)}) collective-permute-start(bf16[320,256]{1,0:T(8,128)(2,1)S(1)} %adjoint.1.refs_0_), channel_id=1, source_target_pairs={{0,192},{32,224},{64,0},{96,32},{128,64},{160,96},{192,128},{224,1... | collective-permute-start | bytes 491528 | tf_op jit(solution)/shard_map/ppermute | solution.py:522
  61.5 1.7 %collective-permute-start.15 = (bf16[320,256]{1,0:T(8,128)(2,1)S(1)}, bf16[320,256]{1,0:T(8,128)(2,1)S(1)}, u32[]{:S(2)}, u32[]{:S(2)}) collective-permute-start(bf16[320,256]{1,0:T(8,128)(2,1)S(1)} %adjoint.1.refs_0_), channel_id=1, source_target_pairs={{0,32},{32,64},{64,96},{96,128},{128,160},{160,192},{192,224},{224... | collective-permute-start | bytes 491528 | tf_op jit(solution)/shard_map/ppermute | solution.py:522
  64.4 1.8 %collective-permute-done.17.refs_3_ = bf16[320,256]{1,0:T(8,128)(2,1)S(1)} collective-permute-done((bf16[320,256]{1,0:T(8,128)(2,1)S(1)}, bf16[320,256]{1,0:T(8,128)(2,1)S(1)}, u32[]{:S(2)}, u32[]{:S(2)}) %collective-permute-start.17) | collective-permute-done | bytes 163872 | tf_op jit(solution)/shard_map/ppermute | solution.py:522
  66.2 1.5 %collective-permute-start.19 = (bf16[320,256]{1,0:T(8,128)(2,1)S(1)}, bf16[320,256]{1,0:T(8,128)(2,1)S(1)}, u32[]{:S(2)}, u32[]{:S(2)}) collective-permute-start(bf16[320,256]{1,0:T(8,128)(2,1)S(1)} %collective-permute-done.17.refs_3_), channel_id=1, source_target_pairs={{0,32},{32,64},{64,96},{96,128},{128,160},{160,192},{192,224},{224... | collective-permute-start | bytes 491528 | tf_op jit(solution)/shard_map/ppermute | solution.py:522
  67.8 1.7 %collective-permute-start.20 = (bf16[320,256]{1,0:T(8,128)(2,1)S(1)}, bf16[320,256]{1,0:T(8,128)(2,1)S(1)}, u32[]{:S(2)}, u32[]{:S(2)}) collective-permute-start(bf16[320,256]{1,0:T(8,128)(2,1)S(1)} %collective-permute-done.18.refs_4_), channel_id=1, source_target_pairs={{0,224},{32,0},{64,32},{96,64},{128,96},{160,128},{192,160},{224,1... | collective-permute-start | bytes 491528 | tf_op jit(solution)/shard_map/ppermute | solution.py:522
  69.5 1.5 %collective-permute-start.21 = (bf16[160,256]{1,0:T(8,128)(2,1)S(1)}, bf16[160,256]{1,0:T(8,128)(2,1)S(1)}, u32[]{:S(2)}, u32[]{:S(2)}) collective-permute-start(bf16[160,256]{1,0:T(8,128)(2,1)S(1)} %slice.18), channel_id=1, source_target_pairs={{0,64},{32,96},{64,128},{96,160},{128,192},{160,224},{192,0},{224,... | collective-permute-start | bytes 245768 | tf_op jit(solution)/shard_map/ppermute | solution.py:522
  71.7 1.6 %collective-permute-start.22 = (bf16[160,256]{1,0:T(8,128)(2,1)S(1)}, bf16[160,256]{1,0:T(8,128)(2,1)S(1)}, u32[]{:S(2)}, u32[]{:S(2)}) collective-permute-start(bf16[160,256]{1,0:T(8,128)(2,1)S(1)} %slice.19), channel_id=1, source_target_pairs={{0,192},{32,224},{64,0},{96,32},{128,64},{160,96},{192,128},{224,1... | collective-permute-start | bytes 245768 | tf_op jit(solution)/shard_map/ppermute | solution.py:522
  74.8 2.6 %collective-permute-done.21.half_a_ref = bf16[160,256]{1,0:T(8,128)(2,1)S(1)} collective-permute-done((bf16[160,256]{1,0:T(8,128)(2,1)S(1)}, bf16[160,256]{1,0:T(8,128)(2,1)S(1)}, u32[]{:S(2)}, u32[]{:S(2)}) %collective-permute-start.21) | collective-permute-done | bytes 81952 | tf_op jit(solution)/shard_map/ppermute | solution.py:522
  78.0 8.9 %collective-permute-start.23 = (bf16[48,512]{1,0:T(8,128)(2,1)S(1)}, bf16[48,512]{1,0:T(8,128)(2,1)S(1)}, u32[]{:S(2)}, u32[]{:S(2)}) collective-permute-start(bf16[48,512]{1,0:T(8,128)(2,1)S(1)} %get-tuple-element.17), channel_id=1, source_target_pairs={{0,1},{1,2},{2,3},{3,4},{4,5},{5,6},{6,7},{7,8},{8,9},{9,10},{10,1... | collective-permute-start | bytes 147464 | tf_op jit(solution)/shard_map/ppermute | solution.py:589
  86.8 1.9 %collective-permute-start.24 = (bf16[48,512]{1,0:T(8,128)(2,1)S(1)}, bf16[48,512]{1,0:T(8,128)(2,1)S(1)}, u32[]{:S(2)}, u32[]{:S(2)}) collective-permute-start(bf16[48,512]{1,0:T(8,128)(2,1)S(1)} %get-tuple-element.18), channel_id=1, source_target_pairs={{1,0},{2,1},{3,2},{4,3},{5,4},{6,5},{7,6},{8,7},{9,8},{10,9},{11,1... | collective-permute-start | bytes 147464 | tf_op jit(solution)/shard_map/ppermute | solution.py:590
  89.2 5.1 %collective-permute-done.24.high_ref = bf16[48,512]{1,0:T(8,128)(2,1)S(1)} collective-permute-done((bf16[48,512]{1,0:T(8,128)(2,1)S(1)}, bf16[48,512]{1,0:T(8,128)(2,1)S(1)}, u32[]{:S(2)}, u32[]{:S(2)}) %collective-permute-start.24) | collective-permute-done | bytes 49184 | tf_op jit(solution)/shard_map/ppermute | solution.py:590
  94.4 4.7 %convolutions.1 = f32[4,8,4,512]{3,2,1,0:T(4,128)} custom-call(f32[4,4,48,128]{3,2,1,0:T(8,128)S(1)} %get-tuple-element.12.image_ref, f32[4,4,48,128]{3,2,1,0:T(8,128)S(1)} %get-tuple-element.16.grad_ref, bf16[48,512]{1,0:T(8,128)(2,1)S(1)} %collective-permute-done.23.low_ref, bf16[48,512]{1,0:T(8,128)(2,1)S(1)} %collective-permute-done.24.high_ref, ...), custom_call_target="tpu_custom_call" | custom-call | bytes 15000000 | tf_op jit(solution)/shard_map/convolutions/pallas_call | solution.py:461
  (66 shorter events, 12.3 us)
Async XLA Ops:
  1.0 0.9 copy-start.2
  2.0 19.9 %collective-permute-start = (bf16[272,256]{1,0:T(8,128)(2,1)S(1)}, bf16[272,256]{1,0:T(8,128)(2,1)S(1)}, u32[]{:S(2)}, u32[]{:S(2)}) collective-permute-start(bf16[272,256]{1,0:T(8,128)(2,1)S(1)} %images_to_rows.1.own_ref.refs_0_), channel_id=1, source_target_pairs={{0,32},{32,64},{64,96},{96,128},{128,160},{160,192},{192,224},{224... | collective-permute-start | bytes 417800 | tf_op jit(solution)/shard_map/ppermute | solution.py:522
  3.7 22.5 %collective-permute-start.1 = (bf16[272,256]{1,0:T(8,128)(2,1)S(1)}, bf16[272,256]{1,0:T(8,128)(2,1)S(1)}, u32[]{:S(2)}, u32[]{:S(2)}) collective-permute-start(bf16[272,256]{1,0:T(8,128)(2,1)S(1)} %images_to_rows.1.own_ref.refs_0_), channel_id=1, source_target_pairs={{0,224},{32,0},{64,32},{96,64},{128,96},{160,128},{192,160},{224,1... | collective-permute-start | bytes 417800 | tf_op jit(solution)/shard_map/ppermute | solution.py:522
  7.8 13.2 %collective-permute-start.2 = (bf16[272,256]{1,0:T(8,128)(2,1)S(1)}, bf16[272,256]{1,0:T(8,128)(2,1)S(1)}, u32[]{:S(2)}, u32[]{:S(2)}) collective-permute-start(bf16[272,256]{1,0:T(8,128)(2,1)S(1)} %images_to_rows.1.own_ref.refs_0_), channel_id=1, source_target_pairs={{0,64},{32,96},{64,128},{96,160},{128,192},{160,224},{192,0},{224,... | collective-permute-start | bytes 417800 | tf_op jit(solution)/shard_map/ppermute | solution.py:522
  7.8 10.7 %collective-permute-start.3 = (bf16[272,256]{1,0:T(8,128)(2,1)S(1)}, bf16[272,256]{1,0:T(8,128)(2,1)S(1)}, u32[]{:S(2)}, u32[]{:S(2)}) collective-permute-start(bf16[272,256]{1,0:T(8,128)(2,1)S(1)} %images_to_rows.1.own_ref.refs_0_), channel_id=1, source_target_pairs={{0,192},{32,224},{64,0},{96,32},{128,64},{160,96},{192,128},{224,1... | collective-permute-start | bytes 417800 | tf_op jit(solution)/shard_map/ppermute | solution.py:522
  18.4 8.8 %collective-permute-start.6 = (bf16[128,256]{1,0:T(8,128)(2,1)S(1)}, bf16[128,256]{1,0:T(8,128)(2,1)S(1)}, u32[]{:S(2)}, u32[]{:S(2)}) collective-permute-start(bf16[128,256]{1,0:T(8,128)(2,1)S(1)} %slice.16), channel_id=1, source_target_pairs={{0,192},{32,224},{64,0},{96,32},{128,64},{160,96},{192,128},{224,1... | collective-permute-start | bytes 196616 | tf_op jit(solution)/shard_map/ppermute | solution.py:522
  21.0 6.3 %collective-permute-start.7 = (bf16[144,256]{1,0:T(8,128)(2,1)S(1)}, bf16[144,256]{1,0:T(8,128)(2,1)S(1)}, u32[]{:S(2)}, u32[]{:S(2)}) collective-permute-start(bf16[144,256]{1,0:T(8,128)(2,1)S(1)} %slice.17), channel_id=1, source_target_pairs={{0,64},{32,96},{64,128},{96,160},{128,192},{160,224},{192,0},{224,... | collective-permute-start | bytes 221192 | tf_op jit(solution)/shard_map/ppermute | solution.py:522
  21.9 7.6 %collective-permute-start.4 = (bf16[272,256]{1,0:T(8,128)(2,1)S(1)}, bf16[272,256]{1,0:T(8,128)(2,1)S(1)}, u32[]{:S(2)}, u32[]{:S(2)}) collective-permute-start(bf16[272,256]{1,0:T(8,128)(2,1)S(1)} %collective-permute-done.2.refs_0_.refs_3_), channel_id=1, source_target_pairs={{0,32},{32,64},{64,96},{96,128},{128,160},{160,192},{192,224},{224... | collective-permute-start | bytes 417800 | tf_op jit(solution)/shard_map/ppermute | solution.py:522
  21.9 7.6 %collective-permute-start.5 = (bf16[272,256]{1,0:T(8,128)(2,1)S(1)}, bf16[272,256]{1,0:T(8,128)(2,1)S(1)}, u32[]{:S(2)}, u32[]{:S(2)}) collective-permute-start(bf16[272,256]{1,0:T(8,128)(2,1)S(1)} %collective-permute-done.3.refs_1_.refs_4_), channel_id=1, source_target_pairs={{0,224},{32,0},{64,32},{96,64},{128,96},{160,128},{192,160},{224,1... | collective-permute-start | bytes 417800 | tf_op jit(solution)/shard_map/ppermute | solution.py:522
  29.5 2.5 %copy-start = (bf16[64,5,64,128]{3,2,1,0:T(8,128)(2,1)S(1)}, bf16[64,5,64,128]{3,2,1,0:T(8,128)(2,1)}, u32[]{:S(2)}) copy-start(bf16[64,5,64,128]{3,2,1,0:T(8,128)(2,1)} %param.13) | copy-start | bytes 15728644
  32.0 21.4 %copy-start.1 = (bf16[64,5,64,128]{3,2,1,0:T(8,128)(2,1)S(1)}, bf16[64,5,64,128]{3,2,1,0:T(8,128)(2,1)}, u32[]{:S(2)}) copy-start(bf16[64,5,64,128]{3,2,1,0:T(8,128)(2,1)} %param.13) | copy-start | bytes 15728644
  32.0 31.2 %copy-start.6 = (f32[32]{0:T(128)S(1)}, f32[32]{0:T(128)}, u32[]{:S(2)}) copy-start(f32[32]{0:T(128)} %param.18) | copy-start | bytes 388
  32.0 31.3 %copy-start.5 = (f32[32,2,27]{0,1,2:T(2,128)S(1)}, f32[32,2,27]{0,1,2:T(2,128)}, u32[]{:S(2)}) copy-start(f32[32,2,27]{0,1,2:T(2,128)} %param.17) | copy-start | bytes 20740
  36.6 52.2 %copy-start.4 = (bf16[55,1536]{1,0:T(8,128)(2,1)S(1)}, bf16[55,1536]{1,0:T(8,128)(2,1)}, u32[]{:S(2)}) copy-start(bf16[55,1536]{1,0:T(8,128)(2,1)} %constant.55.clone) | copy-start | bytes 506884
  36.6 2.2 %collective-permute-start.8 = (bf16[256,128]{1,0:T(8,128)(2,1)S(1)}, bf16[256,128]{1,0:T(8,128)(2,1)S(1)}, u32[]{:S(2)}, u32[]{:S(2)}) collective-permute-start(bf16[256,128]{1,0:T(8,128)(2,1)S(1)} %project.1), channel_id=1, source_target_pairs={{0,1},{1,0},{2,3},{3,2},{4,5},{5,4},{6,7},{7,6},{8,9},{9,8},{10,11... | collective-permute-start | bytes 196616 | tf_op jit(solution)/shard_map/ppermute | solution.py:540
  38.9 4.7 %collective-permute-start.11 = (bf16[256,128]{1,0:T(8,128)(2,1)S(1)}, bf16[256,128]{1,0:T(8,128)(2,1)S(1)}, u32[]{:S(2)}, u32[]{:S(2)}) collective-permute-start(bf16[256,128]{1,0:T(8,128)(2,1)S(1)} %add_convert_fusion.1), channel_id=1, source_target_pairs={{0,4},{1,5},{2,6},{3,7},{4,0},{5,1},{6,2},{7,3},{8,12},{9,13},{10,... | collective-permute-start | bytes 196616 | tf_op jit(solution)/shard_map/ppermute | solution.py:543
  40.1 5.6 %collective-permute-start.10 = (bf16[256,128]{1,0:T(8,128)(2,1)S(1)}, bf16[256,128]{1,0:T(8,128)(2,1)S(1)}, u32[]{:S(2)}, u32[]{:S(2)}) collective-permute-start(bf16[256,128]{1,0:T(8,128)(2,1)S(1)} %add_convert_fusion.1), channel_id=1, source_target_pairs={{0,6},{1,7},{2,0},{3,1},{4,2},{5,3},{6,4},{7,5},{8,14},{9,15},{10,... | collective-permute-start | bytes 196616 | tf_op jit(solution)/shard_map/ppermute | solution.py:543
  40.1 5.6 %collective-permute-start.9 = (bf16[256,128]{1,0:T(8,128)(2,1)S(1)}, bf16[256,128]{1,0:T(8,128)(2,1)S(1)}, u32[]{:S(2)}, u32[]{:S(2)}) collective-permute-start(bf16[256,128]{1,0:T(8,128)(2,1)S(1)} %add_convert_fusion.1), channel_id=1, source_target_pairs={{0,2},{1,3},{2,4},{3,5},{4,6},{5,7},{6,0},{7,1},{8,10},{9,11},{10,... | collective-permute-start | bytes 196616 | tf_op jit(solution)/shard_map/ppermute | solution.py:543
  45.7 48.7 %copy-start.3 = (f32[32]{0:T(128)S(1)}, f32[32]{0:T(128)}, u32[]{:S(2)}) copy-start(f32[32]{0:T(128)} %out_w_ref.1) | copy-start | bytes 388
  45.7 4.5 %collective-permute-start.12 = (bf16[256,128]{1,0:T(8,128)(2,1)S(1)}, bf16[256,128]{1,0:T(8,128)(2,1)S(1)}, u32[]{:S(2)}, u32[]{:S(2)}) collective-permute-start(bf16[256,128]{1,0:T(8,128)(2,1)S(1)} %add_convert_fusion.own_ref), channel_id=1, source_target_pairs={{0,8},{1,9},{2,10},{3,11},{4,12},{5,13},{6,14},{7,15},{8,16},{9,17... | collective-permute-start | bytes 196616 | tf_op jit(solution)/shard_map/ppermute | solution.py:546
  47.1 3.1 %collective-permute-start.13 = (bf16[256,128]{1,0:T(8,128)(2,1)S(1)}, bf16[256,128]{1,0:T(8,128)(2,1)S(1)}, u32[]{:S(2)}, u32[]{:S(2)}) collective-permute-start(bf16[256,128]{1,0:T(8,128)(2,1)S(1)} %add_convert_fusion.own_ref), channel_id=1, source_target_pairs={{0,24},{1,25},{2,26},{3,27},{4,28},{5,29},{6,30},{7,31},{8,0},{9,1... | collective-permute-start | bytes 196616 | tf_op jit(solution)/shard_map/ppermute | solution.py:546
  48.8 4.6 %collective-permute-start.14 = (bf16[256,128]{1,0:T(8,128)(2,1)S(1)}, bf16[256,128]{1,0:T(8,128)(2,1)S(1)}, u32[]{:S(2)}, u32[]{:S(2)}) collective-permute-start(bf16[256,128]{1,0:T(8,128)(2,1)S(1)} %add_convert_fusion.own_ref), channel_id=1, source_target_pairs={{0,16},{1,17},{2,18},{3,19},{4,20},{5,21},{6,22},{7,23},{8,24},{9,... | collective-permute-start | bytes 196616 | tf_op jit(solution)/shard_map/ppermute | solution.py:546
  57.8 8.4 %collective-permute-start.17 = (bf16[320,256]{1,0:T(8,128)(2,1)S(1)}, bf16[320,256]{1,0:T(8,128)(2,1)S(1)}, u32[]{:S(2)}, u32[]{:S(2)}) collective-permute-start(bf16[320,256]{1,0:T(8,128)(2,1)S(1)} %adjoint.1.refs_0_), channel_id=1, source_target_pairs={{0,64},{32,96},{64,128},{96,160},{128,192},{160,224},{192,0},{224,... | collective-permute-start | bytes 491528 | tf_op jit(solution)/shard_map/ppermute | solution.py:522
  59.1 8.7 %collective-permute-start.18 = (bf16[320,256]{1,0:T(8,128)(2,1)S(1)}, bf16[320,256]{1,0:T(8,128)(2,1)S(1)}, u32[]{:S(2)}, u32[]{:S(2)}) collective-permute-start(bf16[320,256]{1,0:T(8,128)(2,1)S(1)} %adjoint.1.refs_0_), channel_id=1, source_target_pairs={{0,192},{32,224},{64,0},{96,32},{128,64},{160,96},{192,128},{224,1... | collective-permute-start | bytes 491528 | tf_op jit(solution)/shard_map/ppermute | solution.py:522
  61.5 10.2 %collective-permute-start.15 = (bf16[320,256]{1,0:T(8,128)(2,1)S(1)}, bf16[320,256]{1,0:T(8,128)(2,1)S(1)}, u32[]{:S(2)}, u32[]{:S(2)}) collective-permute-start(bf16[320,256]{1,0:T(8,128)(2,1)S(1)} %adjoint.1.refs_0_), channel_id=1, source_target_pairs={{0,32},{32,64},{64,96},{96,128},{128,160},{160,192},{192,224},{224... | collective-permute-start | bytes 491528 | tf_op jit(solution)/shard_map/ppermute | solution.py:522
  63.4 10.7 %collective-permute-start.16 = (bf16[320,256]{1,0:T(8,128)(2,1)S(1)}, bf16[320,256]{1,0:T(8,128)(2,1)S(1)}, u32[]{:S(2)}, u32[]{:S(2)}) collective-permute-start(bf16[320,256]{1,0:T(8,128)(2,1)S(1)} %adjoint.1.refs_0_), channel_id=1, source_target_pairs={{0,224},{32,0},{64,32},{96,64},{128,96},{160,128},{192,160},{224,1... | collective-permute-start | bytes 491528 | tf_op jit(solution)/shard_map/ppermute | solution.py:522
  66.2 11.1 %collective-permute-start.19 = (bf16[320,256]{1,0:T(8,128)(2,1)S(1)}, bf16[320,256]{1,0:T(8,128)(2,1)S(1)}, u32[]{:S(2)}, u32[]{:S(2)}) collective-permute-start(bf16[320,256]{1,0:T(8,128)(2,1)S(1)} %collective-permute-done.17.refs_3_), channel_id=1, source_target_pairs={{0,32},{32,64},{64,96},{96,128},{128,160},{160,192},{192,224},{224... | collective-permute-start | bytes 491528 | tf_op jit(solution)/shard_map/ppermute | solution.py:522
  67.8 9.6 %collective-permute-start.20 = (bf16[320,256]{1,0:T(8,128)(2,1)S(1)}, bf16[320,256]{1,0:T(8,128)(2,1)S(1)}, u32[]{:S(2)}, u32[]{:S(2)}) collective-permute-start(bf16[320,256]{1,0:T(8,128)(2,1)S(1)} %collective-permute-done.18.refs_4_), channel_id=1, source_target_pairs={{0,224},{32,0},{64,32},{96,64},{128,96},{160,128},{192,160},{224,1... | collective-permute-start | bytes 491528 | tf_op jit(solution)/shard_map/ppermute | solution.py:522
  69.5 7.8 %collective-permute-start.21 = (bf16[160,256]{1,0:T(8,128)(2,1)S(1)}, bf16[160,256]{1,0:T(8,128)(2,1)S(1)}, u32[]{:S(2)}, u32[]{:S(2)}) collective-permute-start(bf16[160,256]{1,0:T(8,128)(2,1)S(1)} %slice.18), channel_id=1, source_target_pairs={{0,64},{32,96},{64,128},{96,160},{128,192},{160,224},{192,0},{224,... | collective-permute-start | bytes 245768 | tf_op jit(solution)/shard_map/ppermute | solution.py:522
  71.7 5.7 %collective-permute-start.22 = (bf16[160,256]{1,0:T(8,128)(2,1)S(1)}, bf16[160,256]{1,0:T(8,128)(2,1)S(1)}, u32[]{:S(2)}, u32[]{:S(2)}) collective-permute-start(bf16[160,256]{1,0:T(8,128)(2,1)S(1)} %slice.19), channel_id=1, source_target_pairs={{0,192},{32,224},{64,0},{96,32},{128,64},{160,96},{192,128},{224,1... | collective-permute-start | bytes 245768 | tf_op jit(solution)/shard_map/ppermute | solution.py:522
  78.0 11.2 %collective-permute-start.23 = (bf16[48,512]{1,0:T(8,128)(2,1)S(1)}, bf16[48,512]{1,0:T(8,128)(2,1)S(1)}, u32[]{:S(2)}, u32[]{:S(2)}) collective-permute-start(bf16[48,512]{1,0:T(8,128)(2,1)S(1)} %get-tuple-element.17), channel_id=1, source_target_pairs={{0,1},{1,2},{2,3},{3,4},{4,5},{5,6},{6,7},{7,8},{8,9},{9,10},{10,1... | collective-permute-start | bytes 147464 | tf_op jit(solution)/shard_map/ppermute | solution.py:589
  86.8 7.5 %collective-permute-start.24 = (bf16[48,512]{1,0:T(8,128)(2,1)S(1)}, bf16[48,512]{1,0:T(8,128)(2,1)S(1)}, u32[]{:S(2)}, u32[]{:S(2)}) collective-permute-start(bf16[48,512]{1,0:T(8,128)(2,1)S(1)} %get-tuple-element.18), channel_id=1, source_target_pairs={{1,0},{2,1},{3,2},{4,3},{5,4},{6,5},{7,6},{8,7},{9,8},{10,9},{11,1... | collective-permute-start | bytes 147464 | tf_op jit(solution)/shard_map/ppermute | solution.py:590
where the time goes:
time: 99.5 us; the launch traced here: 99.1 us
  starting transfers between devices  48.5 us (49%)
  waiting for transfers between devices  25.2 us (25%)
  Pallas kernels  16.8 us (17%)
  local copies, waits for them, and re-layouts  5.11 us (5%)
  other arithmetic  3.04 us (3%)
    ppermute x16, starting transfers between devices, from_sensor(): return lax.ppermute(block, 'sensor', ring(distance, 8))  28 us
    ppermute x16, waiting for transfers between devices, from_sensor(): return lax.ppermute(block, 'sensor', ring(distance, 8))  13 us
    ppermute x1, starting transfers between devices, on_device(): low_in = lax.ppermute(high_out, 'slab', forward)  8.86 us
    ppermute x1, waiting for transfers between devices, on_device(): high_in = lax.ppermute(low_out, 'slab', backward)  5.15 us
    pallas_call x1, Pallas kernels, convolve(): pl.pallas_call(conv_kernel, out_shape=jax.ShapeDtypeStruct((4, 8, NB, 512...  4.75 us
    pallas_call x1, Pallas kernels, project(): pl.pallas_call(project_kernel, out_shape=jax.ShapeDtypeStruct((JB * NB, T...  4.57 us
    ppermute x3, starting transfers between devices, slab_sum_parts(): lax.ppermute(row, 'slab', slab_perm(d, 0, 0))  4.46 us
    pallas_call x1, Pallas kernels, adjoint(): pl.pallas_call(adjoint_kernel, out_shape=jax.ShapeDtypeStruct((SLOTS, 256...  4.4 us
  transfers between devices with their start and end apart: 25, of which 10 were waited for; matrix products, arithmetic and copies ran while one was open for 4% of the time, Pallas kernels for 2%

commit v1 on v0

v1 whole, which is shorter than its diff:
```python
import functools

import jax
import jax.numpy as jnp
import numpy as np
from jax import lax
from jax.experimental import pallas as pl
from jax.experimental.pallas import tpu as pltpu
from jax.sharding import PartitionSpec as P

F32 = jnp.float32
BF16 = jnp.bfloat16
I32 = jnp.int32

JB = 64
KS = 5
SLOTS = JB * KS
NB = 4
TB = 128
OWN = 256
SENT = SLOTS + 16
SENT_SPLIT = 176
CHAN = 32
TAPS = 192


def vmem():
    return pl.BlockSpec(memory_space=pltpu.VMEM)


def smem():
    return pl.BlockSpec(memory_space=pltpu.SMEM)


def params(mib):
    return pltpu.CompilerParams(vmem_limit_bytes=mib * 1024 * 1024)


def cost(us):
    return pl.CostEstimate(flops=0, bytes_accessed=int(us * 3.0e6), transcendentals=0)


def lower_half(rows):
    return lax.broadcasted_iota(I32, (rows, 128), 1) < 64


def swapped(tile):
    return pltpu.roll(tile, 64, axis=1)


def pair_halves(first, second, low):
    return jnp.where(low, first, swapped(second)), jnp.where(low, swapped(first), second)


def planes_to_rows(volume_refs, rows, out_ref):
    i = 0
    for volume_ref in volume_refs:
        for x in range(volume_ref.shape[0]):
            for z in range(8):
                image = volume_ref[x, z].astype(F32)
                for q in range(4):
                    rows[q, 4 * i : 4 * i + 4, :] = image[:, 128 * q : 128 * q + 128]
                i += 1
    low = lower_half(32)
    for m in range(2):
        for q in range(4):
            one = rows[q, pl.ds(2 * m, 32, stride=4), :]
            two = rows[q, pl.ds(2 * m + 1, 32, stride=4), :]
            even, odd = pair_halves(one, two, low)
            out_ref[64 * q : 64 * q + 32, 128 * m : 128 * m + 128] = even.astype(BF16)
            out_ref[64 * q + 32 : 64 * q + 64, 128 * m : 128 * m + 128] = odd.astype(BF16)


def add_gathered(acc, keys, weights, base, shard):
    lane = lax.broadcasted_iota(I32, (SLOTS, OWN), 1)
    hot = jnp.where(lane == keys - base, weights, 0.0).astype(BF16)
    return acc + jnp.dot(hot, shard, preferred_element_type=F32)


def gather_kernel(
    base_ref, keys_ref, weights_ref, own_ref, plus_ref, minus_ref, two_ref, back_ref,
    out_ref, own_rows, plus_rows, minus_rows, rows, shard,
):
    acc = jnp.zeros((SLOTS, 256), F32)
    keys, weights = keys_ref[...], weights_ref[...]
    shards = (own_rows, plus_rows, minus_rows, shard.at[0], shard.at[1])
    for i, ref in enumerate((own_ref, plus_ref, minus_ref, two_ref, back_ref)):
        planes_to_rows([ref], rows.at[i], shards[i])
        acc = add_gathered(acc, keys, weights, base_ref[i], shards[i][...])
    out_ref[...] = acc


def gather_first(base, keys, weights, shards):
    return pl.pallas_call(
        gather_kernel,
        out_shape=[jax.ShapeDtypeStruct((SLOTS, 256), F32)]
        + [jax.ShapeDtypeStruct((OWN, 256), BF16)] * 3,
        in_specs=[smem()] + [vmem()] * (2 + len(shards)),
        out_specs=[vmem()] * 4,
        scratch_shapes=[
            pltpu.VMEM((5, 4, 128, 128), F32),
            pltpu.VMEM((2, OWN, 256), BF16),
        ],
        compiler_params=params(16),
        cost_estimate=cost(1.5),
        name="gather_first",
    )(base, keys, weights, *shards)


CHUNKS = 8


def hold_kernel(blocks_ref, after_ref, held_ref, sems):
    step = JB // CHUNKS
    copies = [
        pltpu.make_async_copy(
            blocks_ref.at[pl.ds(c * step, step)], held_ref.at[pl.ds(c * step, step)], sems.at[c]
        )
        for c in range(CHUNKS)
    ]
    for copy in copies:
        copy.start()
    for copy in copies:
        copy.wait()


def hold(blocks, after):
    return pl.pallas_call(
        hold_kernel,
        out_shape=jax.ShapeDtypeStruct((JB, KS * 64, TB), BF16),
        in_specs=[pl.BlockSpec(memory_space=pl.ANY), pl.BlockSpec(memory_space=pl.ANY)],
        out_specs=vmem(),
        scratch_shapes=[pltpu.SemaphoreType.DMA((CHUNKS,))],
        compiler_params=params(46),
        cost_estimate=cost(2.5),
        name="hold_blocks",
    )(blocks, after)


def project_kernel(
    base_ref,
    slab_ref,
    keys_ref,
    weights_ref,
    before_ref,
    three_ref,
    minus_ref,
    half_a_ref,
    half_b_ref,
    measured_ref,
    held,
    out_ref,
    rows,
    shard,
    lhs,
    total,
):
    acc = before_ref[...]
    keys, weights = keys_ref[...], weights_ref[...]
    for i, refs in enumerate(((three_ref,), (minus_ref,), (half_a_ref, half_b_ref))):
        planes_to_rows(refs, rows.at[i], shard.at[i])
        acc = add_gathered(acc, keys, weights, base_ref[5 + i], shard[i])
    low = lower_half(JB)
    for m in range(2):
        cols = slice(128 * m, 128 * m + 128)
        for q in range(3):
            one = acc[2 * q * JB : (2 * q + 1) * JB, cols]
            if q < 2:
                two = acc[(2 * q + 1) * JB : (2 * q + 2) * JB, cols]
                even, odd = pair_halves(one, two, low)
            else:
                even, odd = one, swapped(one)
            lhs[q, pl.ds(2 * m, JB, stride=4), :] = even
            lhs[q, pl.ds(2 * m + 1, JB, stride=4), :] = odd
    upper = lax.broadcasted_iota(I32, (8, TB), 0) < 4
    for p in range(JB // 2):
        at = slice(8 * p, 8 * p + 8)
        left = jnp.concatenate([lhs[0, at], lhs[1, at], lhs[2, at, 0:64]], axis=1).astype(BF16)
        both = jnp.concatenate([held[2 * p], held[2 * p + 1]], axis=1)
        got = jnp.dot(left, both, preferred_element_type=F32)
        total[8 * p : 8 * p + 8, :] = jnp.where(upper, got[:, :TB], got[:, TB:])
    mine = pl.ds(pl.multiple_of(slab_ref[0] * 8, 8), 8)
    total[mine, :] = total[mine, :] - measured_ref[...]
    out_ref[...] = total[...].astype(BF16)


def project(base, slab, keys, weights, before, rest, measured, held):
    return pl.pallas_call(
        project_kernel,
        out_shape=jax.ShapeDtypeStruct((JB * NB, TB), BF16),
        in_specs=[smem(), smem()] + [vmem()] * 9,
        out_specs=vmem(),
        scratch_shapes=[
            pltpu.VMEM((3, 4, 128, 128), F32),
            pltpu.VMEM((3, OWN, 256), BF16),
            pltpu.VMEM((3, JB * NB, 128), F32),
            pltpu.VMEM((JB * NB, TB), F32),
        ],
        compiler_params=params(16),
        cost_estimate=cost(4.0),
        name="project",
    )(base, slab, keys, weights, before, *rest, measured, held)


def adjoint_kernel(
    own_ref, one_ref, two_ref, three_ref, weights_ref, ids_ref, held, out_ref, resid, back
):
    back[2] = jnp.zeros((JB * NB, 128), F32)
    total = own_ref[...].astype(F32) + one_ref[...].astype(F32)
    total = total + two_ref[...].astype(F32) + three_ref[...].astype(F32)
    resid[...] = total.astype(BF16).astype(F32)
    upper = lax.broadcasted_iota(I32, (8, KS * 64), 0) < 4
    dims = (((1,), (1,)), ((), ()))
    for p in range(JB // 2):
        left = resid[8 * p : 8 * p + 8, :].astype(BF16)
        a = lax.dot_general(left, held[2 * p], dims, preferred_element_type=F32)
        b = lax.dot_general(left, held[2 * p + 1], dims, preferred_element_type=F32)
        got = jnp.where(upper, a, b)
        at = slice(8 * p, 8 * p + 8)
        back[0, at, :] = got[:, 0:128]
        back[1, at, :] = got[:, 128:256]
        back[2, at, 0:64] = got[:, 256 : KS * 64]
    low = lower_half(JB)
    for m in range(2):
        for q in range(3):
            one = back[q, pl.ds(2 * m, JB, stride=4), :]
            two = back[q, pl.ds(2 * m + 1, JB, stride=4), :]
            even, odd = pair_halves(one, two, low)
            for k, part in ((2 * q, even), (2 * q + 1, odd)):
                if k < KS:
                    scaled = part * weights_ref[k * JB : (k + 1) * JB, :]
                    out_ref[k * JB : (k + 1) * JB, 128 * m : 128 * m + 128] = scaled.astype(BF16)
    out_ref[SLOTS:SENT, :] = ids_ref[...]


def adjoint(parts, weights, id_rows, held):
    return pl.pallas_call(
        adjoint_kernel,
        out_shape=jax.ShapeDtypeStruct((SENT, 256), BF16),
        in_specs=[vmem()] * 7,
        out_specs=vmem(),
        scratch_shapes=[
            pltpu.VMEM((JB * NB, TB), F32),
            pltpu.VMEM((3, JB * NB, 128), F32),
        ],
        compiler_params=params(16),
        cost_estimate=cost(3.0),
        name="adjoint",
    )(*parts, weights, id_rows, held)


def rows_to_planes(rows, out_ref):
    low = lower_half(48)
    for m in range(2):
        for q in range(4):
            one = rows[96 * q : 96 * q + 48, 128 * m : 128 * m + 128]
            two = rows[96 * q + 48 : 96 * q + 96, 128 * m : 128 * m + 128]
            even, odd = pair_halves(one, two, low)
            out_ref[2 * m, q] = even
            out_ref[2 * m + 1, q] = odd


def edge_rows(planes_ref, place, z):
    for n in range(NB):
        for q in range(4):
            rows = planes_ref[n, q, pl.ds(z, 6, stride=8), :]
            place[n * 6 : n * 6 + 6, 128 * q : 128 * q + 128] = rows


def images_kernel(
    pos_ref, own_ref, plus_ref, minus_ref, planes_ref, low_ref, high_ref, rows
):
    sensor, last = pos_ref[0], pos_ref[1]
    keep_low = jnp.where(sensor > 0, 1.0, 0.0).astype(F32)
    keep_high = jnp.where(sensor < last, 1.0, 0.0).astype(F32)
    for h in range(8):
        block = slice(32 * h, 32 * h + 32)
        rows[48 * h : 48 * h + 8, :] = plus_ref[block, :].astype(F32)[24:32] * keep_low
        rows[48 * h + 8 : 48 * h + 40, :] = own_ref[block, :].astype(F32)
        rows[48 * h + 40 : 48 * h + 48, :] = minus_ref[block, :].astype(F32)[0:8] * keep_high
    rows_to_planes(rows, planes_ref)
    edge_rows(planes_ref, low_ref, 0)
    edge_rows(planes_ref, high_ref, 7)


def images(pos, shards):
    return pl.pallas_call(
        images_kernel,
        out_shape=[
            jax.ShapeDtypeStruct((NB, 4, 48, 128), F32),
            jax.ShapeDtypeStruct((24, 512), F32),
            jax.ShapeDtypeStruct((24, 512), F32),
        ],
        in_specs=[smem()] + [vmem()] * len(shards),
        out_specs=[vmem()] * 3,
        scratch_shapes=[pltpu.VMEM((384, 256), F32)],
        compiler_params=params(16),
        cost_estimate=cost(0.7),
        name="images_to_planes",
    )(pos, *shards)


def add_scattered(acc, sensor, contrib):
    coded = contrib[SLOTS:SENT, :].astype(F32)
    ids = (coded[0:2] * 16.0 + coded[2:4]).astype(I32)
    x = (ids >> 6) - 4 * sensor + 1
    index = (ids & 7) * 48 + x * 8 + ((ids >> 3) & 7)
    index = jnp.where((x >= 0) & (x < 6), index, -1)
    first = lax.broadcasted_iota(I32, (384, 256), 0)
    second = lax.broadcasted_iota(I32, (384, SLOTS - 256), 0)
    hot = jnp.where(first == index[0:1, :], 1.0, 0.0).astype(BF16)
    more = jnp.where(second == index[1:2, 0 : SLOTS - 256], 1.0, 0.0).astype(BF16)
    acc = acc + jnp.dot(hot, contrib[0:256, :], preferred_element_type=F32)
    return acc + jnp.dot(more, contrib[256:SLOTS, :], preferred_element_type=F32)


def scatter_kernel(pos_ref, *refs):
    contribs, out_ref = refs[:-1], refs[-1]
    acc = jnp.zeros((384, 256), F32)
    for contrib in contribs:
        acc = add_scattered(acc, pos_ref[0], contrib)
    out_ref[...] = acc


def scatter_first(pos, contribs):
    return pl.pallas_call(
        scatter_kernel,
        out_shape=jax.ShapeDtypeStruct((384, 256), F32),
        in_specs=[smem()] + [vmem()] * len(contribs),
        out_specs=vmem(),
        compiler_params=params(16),
        cost_estimate=cost(0.7),
        name="scatter_first",
    )(pos, *contribs)


def gradient_kernel(
    pos_ref,
    before_ref,
    three_ref,
    minus_ref,
    half_a_ref,
    half_b_ref,
    image_low_ref,
    image_high_ref,
    planes_ref,
    inner_ref,
    outer_ref,
    far,
    rows,
    low,
    high,
):
    far[0:SENT_SPLIT, :] = half_a_ref[...]
    far[SENT_SPLIT:SENT, :] = half_b_ref[...]
    acc = before_ref[...]
    for contrib in (three_ref, minus_ref, far):
        acc = add_scattered(acc, pos_ref[0], contrib)
    rows[...] = acc
    rows_to_planes(rows, planes_ref)
    low[0:24, :] = image_low_ref[...]
    high[0:24, :] = image_high_ref[...]
    edge_rows(planes_ref, low.at[pl.ds(24, 24)], 0)
    edge_rows(planes_ref, high.at[pl.ds(24, 24)], 7)
    first_core = pos_ref[2] == 0
    inner_ref[...] = jnp.where(first_core, high[...], low[...]).astype(BF16)
    outer_ref[...] = jnp.where(first_core, low[...], high[...]).astype(BF16)


def gradient_planes(pos, before, rest, image_low, image_high):
    return pl.pallas_call(
        gradient_kernel,
        out_shape=[
            jax.ShapeDtypeStruct((NB, 4, 48, 128), F32),
            jax.ShapeDtypeStruct((48, 512), BF16),
            jax.ShapeDtypeStruct((48, 512), BF16),
        ],
        in_specs=[smem()] + [vmem()] * 7,
        out_specs=[vmem()] * 3,
        scratch_shapes=[
            pltpu.VMEM((SENT, 256), BF16),
            pltpu.VMEM((384, 256), F32),
            pltpu.VMEM((48, 512), F32),
            pltpu.VMEM((48, 512), F32),
        ],
        compiler_params=params(16),
        cost_estimate=cost(1.0),
        name="gradient_planes",
    )(pos, before, *rest, image_low, image_high)


def shifted_rows(rows, e):
    if e == 1:
        return rows
    y = lax.broadcasted_iota(I32, rows.shape, 1)
    if e == 0:
        return jnp.where(y == 0, 0.0, pltpu.roll(rows, 1, axis=1))
    return jnp.where(y == 511, 0.0, pltpu.roll(rows, 511, axis=1))


def conv_kernel(
    pos_ref, image_ref, grad_ref, inner_ref, outer_ref, matrix_ref, out_w_ref, out_ref,
    body, ends, done,
):
    first_core = pos_ref[2] == 0
    inner, outer = inner_ref[...].astype(F32), outer_ref[...].astype(F32)
    below, above = jnp.where(first_core, outer, inner), jnp.where(first_core, inner, outer)
    for kind, (edge, start) in enumerate(((below, 0), (above, 0), (below, 24), (above, 24))):
        rows = edge[start : start + 24]
        for e in range(3):
            moved = shifted_rows(rows, e)
            for q in range(4):
                ends[q, pl.ds(kind + 4 * e, 24, stride=16), :] = moved[:, 128 * q : 128 * q + 128]
    for q in range(4):
        ends[q, pl.ds(12, 24, stride=16), :] = jnp.ones((24, 128), F32)
        for r in range(13, 16):
            ends[q, pl.ds(r, 24, stride=16), :] = jnp.zeros((24, 128), F32)
    for n in range(NB):
        for x in range(6):
            rows = jnp.concatenate(
                [
                    jnp.concatenate([ref[n, q, 8 * x : 8 * x + 8, :] for q in range(4)], axis=1)
                    for ref in (image_ref, grad_ref)
                ],
                axis=0,
            )
            for e in range(3):
                body[e, n * 6 + x] = shifted_rows(rows, e).astype(BF16)

    def one_x(x, carry):
        for n in range(NB):
            for half in range(2):
                cols = slice(256 * half, 256 * half + 256)
                tiles = [body[e, n * 6 + x + a, :, cols] for a in range(3) for e in range(3)]
                for a in range(3):
                    at = pl.multiple_of((n * 6 + x + a) * 16, 16)
                    pair = [ends[2 * half + q, pl.ds(at, 16), :] for q in range(2)]
                    tiles.append(jnp.concatenate(pair, axis=1).astype(BF16))
                stack = jnp.concatenate(tiles, axis=0)
                hidden = jnp.dot(matrix_ref[0], stack, preferred_element_type=F32)
                hidden = hidden + jnp.dot(matrix_ref[1], stack, preferred_element_type=F32)
                at = pl.multiple_of(8 * x + 8, 8)
                pair = [image_ref[n, 2 * half + q, pl.ds(at, 8), :] for q in range(2)]
                total = jnp.concatenate(pair, axis=1)
                for c in range(CHAN):
                    total = total + jnp.maximum(hidden[8 * c : 8 * c + 8], 0.0) * out_w_ref[c]
                for q in range(2):
                    part = total[:, 128 * q : 128 * q + 128]
                    done[2 * half + q, pl.ds(n, 8, stride=4), :] = part
        for z in range(8):
            for q in range(4):
                out_ref[x, z, :, 128 * q : 128 * q + 128] = done[q, 4 * z : 4 * z + 4, :]
        return carry

    lax.fori_loop(0, 4, one_x, 0)


def convolve(pos, image, grad, inner, outer, matrix, out_w):
    return pl.pallas_call(
        conv_kernel,
        out_shape=jax.ShapeDtypeStruct((4, 8, NB, 512), F32),
        in_specs=[smem()] + [vmem()] * 5 + [smem()],
        out_specs=vmem(),
        scratch_shapes=[
            pltpu.VMEM((3, 24, 16, 512), BF16),
            pltpu.VMEM((4, 384, 128), F32),
            pltpu.VMEM((4, 32, 128), F32),
        ],
        compiler_params=params(32),
        cost_estimate=cost(5.0),
        name="convolutions",
    )(pos, image, grad, inner, outer, matrix, out_w)


def tap_choice():
    choice = np.zeros((55, 8, TAPS), np.float32)
    for z in range(8):
        for a in range(3):
            for e in range(3):
                for i in range(2):
                    for plane in range(-1, 9):
                        b = plane - z + 1
                        if not 0 <= b <= 2:
                            continue
                        if 0 <= plane < 8:
                            column = (a * 3 + e) * 16 + i * 8 + plane
                        else:
                            column = 144 + a * 16 + i * 2 + (plane > 0) + 4 * e
                        choice[i * 27 + (a * 3 + b) * 3 + e, z, column] = 1.0
        choice[54, z, 144 + 12] = 1.0
    return choice


def conv_matrix(conv_in, conv_bias):
    table = jnp.concatenate([conv_in.reshape(CHAN, 54), conv_bias[:, None]], axis=1)
    high = lax.reduce_precision(table, 8, 7)
    parts = jnp.concatenate([high, table - high], axis=0).astype(BF16)
    choice = jnp.asarray(tap_choice().reshape(55, 8 * TAPS), BF16)
    spread = jnp.dot(parts, choice, preferred_element_type=F32).astype(BF16)
    return spread.reshape(2, CHAN * 8, TAPS)


def ring(distance, count):
    return [(i, (i + distance) % count) for i in range(count)]


def slab_perm(dy, dx, core):
    def index(y, x, c):
        return (y % 4 * 4 + x % 4) * 2 + c

    return [
        (index(y, x, c), index(y + dy, x + dx, c ^ core))
        for y in range(4)
        for x in range(4)
        for c in range(2)
    ]


def from_sensor(block, distance):
    return lax.ppermute(block, "sensor", ring(distance, 8))


def spread_far(plus, minus, split):
    return [
        from_sensor(plus, 1),
        from_sensor(minus, -1),
        from_sensor(plus[:split], 2),
        from_sensor(minus[split:], -2),
    ]


def chip_sum(partial):
    other = lax.ppermute(partial, "slab", slab_perm(0, 0, 1))
    total = partial.astype(F32) + other.astype(F32)
    return total.astype(BF16)


def slab_sum_parts(total):
    moved = [lax.ppermute(total, "slab", slab_perm(0, d, 0)) for d in (1, 3, 2)]
    row = total.astype(F32) + moved[0].astype(F32) + moved[1].astype(F32) + moved[2].astype(F32)
    row = row.astype(BF16)
    return [row] + [lax.ppermute(row, "slab", slab_perm(d, 0, 0)) for d in (1, 3, 2)]


def slot_weights(live_slots, exponents):
    slot_iota = lax.broadcasted_iota(I32, exponents.shape, 1)
    scaled = jnp.exp2(exponents.astype(F32))
    return jnp.where(slot_iota < live_slots[:, None], scaled, jnp.zeros_like(scaled))


def on_device(volume, measured, blocks, voxel_ids, counts, exponents, conv_in, conv_bias, conv_out):
    sensor = lax.axis_index("sensor").astype(I32)
    slab = lax.axis_index("slab").astype(I32)
    steps = jnp.array([0, -1, 1, -2, 2, -3, 3, 4], I32)
    base = ((sensor + steps) % 8) * OWN
    pos = jnp.stack([sensor, jnp.full_like(sensor, 7), slab % 2])
    ids = voxel_ids.T.reshape(SLOTS)
    padded = jnp.pad(ids, (0, 512 - SLOTS), constant_values=4080).reshape(2, 256)
    id_rows = jnp.concatenate([padded >> 4, padded & 15, jnp.zeros((12, 256), I32)], axis=0)
    keys = (ids & ~255) | ((ids & 7) << 5) | ((ids >> 3) & 31)
    keys = keys.reshape(SLOTS, 1)
    weights = slot_weights(counts[:, 0], exponents).T.reshape(SLOTS, 1)
    stacked = blocks.reshape(JB, KS * 64, TB)

    plus, minus = from_sensor(volume, 1), from_sensor(volume, -1)
    two, back = from_sensor(volume, 2), from_sensor(volume, -2)
    far = spread_far(two, back, 2)
    held = hold(stacked, two)
    before, *near = gather_first(base, keys, weights, [volume, plus, minus, two, back])
    partial = project(
        base, slab.reshape(1), keys, weights, before, far,
        measured.reshape(8, TB).astype(F32), held,
    )
    chip = chip_sum(partial)
    held = hold(stacked, chip)
    parts = slab_sum_parts(chip)
    matrix = conv_matrix(conv_in, conv_bias)
    image, image_low, image_high = images(pos, near)
    contrib = adjoint(parts, weights, id_rows.astype(BF16), held)
    two_c, back_c = from_sensor(contrib, 2), from_sensor(contrib, -2)
    near_c = [contrib, from_sensor(contrib, 1), from_sensor(contrib, -1)]
    far_c = spread_far(two_c, back_c, SENT_SPLIT)
    sums = scatter_first(pos, [*near_c, two_c, back_c])
    grad, inner, outer = gradient_planes(pos, sums, far_c, image_low, image_high)
    inner = lax.ppermute(inner, "slab", slab_perm(0, 0, 1))
    pairs = [(2 * i + 1, 2 * i + 2) for i in range(15)]
    outer = lax.ppermute(outer, "slab", pairs + [(b, a) for a, b in pairs])
    return convolve(pos, image, grad, inner, outer, matrix, conv_out)


def solution(mesh):
    in_specs = (
        P("sensor", "slab", None, None),
        P(("sensor", "slab"), None, None),
        P("sensor", "slab", None, None),
        P("sensor", "slab"),
        P("sensor", "slab"),
        P("sensor", "slab"),
        P(),
        P(),
        P(),
    )
    out_specs = P("sensor", "slab", None, None)
    return jax.shard_map(
        on_device, mesh=mesh, in_specs=in_specs, out_specs=out_specs, check_vma=False
    )
```

time: 99.5 us -> 86.6 us (0.87); the launches traced: 99.1 us -> 84.9 us
  waiting for transfers between devices: 25.2 us -> 16.5 us
  local copies, waits for them, and re-layouts: 5.11 us -> 1.08 us
  starting transfers between devices: 48.5 us -> 45.7 us
  Pallas kernels: 16.8 us -> 18.1 us
    ppermute x16, waiting for transfers between devices: 13 us -> 8.48 us  [from_sensor(): return lax.ppermute(block, 'sensor', ring(distance, 8))]
    unnamed x15 -> x13, local copies, waits for them, and re-layouts: 3.51 us -> 0.13 us
    pallas_call x3 -> x4, Pallas kernels: 5.56 us -> 8.26 us  [the longest x2 5.11 us: hold(): pl.pallas_call(hold_kernel, out_shape=jax.ShapeDtypeStruct((JB, KS * 64,...]
    pallas_call x1, Pallas kernels: 4.57 us -> 2.08 us  [project(): pl.pallas_call(project_kernel, out_shape=jax.ShapeDtypeStruct((JB * NB, T...]
    ppermute x3, waiting for transfers between devices: 3.25 us -> 1.17 us  [slab_sum_parts(): lax.ppermute(row, 'slab', slab_perm(d, 0, 0))]
    ppermute x3, waiting for transfers between devices: 6.05 us -> 3.99 us  [the longest x1 3.16 us: on_device(): outer = lax.ppermute(outer, 'slab', pairs + [(b, a) for a, b in pairs])]
    ppermute x16, starting transfers between devices: 28 us -> 26.8 us  [from_sensor(): return lax.ppermute(block, 'sensor', ring(distance, 8))]
  transfers between devices with their start and end apart: 25 -> 25, of which waited for: 10 -> 10; matrix products, arithmetic and copies ran while one was open for 4% -> 5% of each run, Pallas kernels for 2% -> 10%
where the time goes in v1:
time: 86.6 us; the launch traced here: 84.9 us
  starting transfers between devices  45.7 us (53%)
  Pallas kernels  18.1 us (21%)
  waiting for transfers between devices  16.5 us (19%)
  other arithmetic  3.04 us (4%)
  local copies, waits for them, and re-layouts  1.08 us (1%)
    ppermute x16, starting transfers between devices, from_sensor(): return lax.ppermute(block, 'sensor', ring(distance, 8))  26.8 us
    ppermute x16, waiting for transfers between devices, from_sensor(): return lax.ppermute(block, 'sensor', ring(distance, 8))  8.48 us
    pallas_call x2, Pallas kernels, hold(): pl.pallas_call(hold_kernel, out_shape=jax.ShapeDtypeStruct((JB, KS * 64,...  5.11 us
    ppermute x1, starting transfers between devices, on_device(): inner = lax.ppermute(inner, 'slab', slab_perm(0, 0, 1))  4.81 us
    pallas_call x1, Pallas kernels, convolve(): pl.pallas_call(conv_kernel, out_shape=jax.ShapeDtypeStruct((4, 8, NB, 512...  4.72 us
    ppermute x3, starting transfers between devices, slab_sum_parts(): lax.ppermute(row, 'slab', slab_perm(d, 0, 0))  4.46 us
    ppermute x1, starting transfers between devices, on_device(): outer = lax.ppermute(outer, 'slab', pairs + [(b, a) for a, b in pairs])  3.89 us
    ppermute x3, starting transfers between devices, slab_sum_parts(): moved = [lax.ppermute(total, 'slab', slab_perm(0, d, 0)) for d in (1, 3, 2)]  3.27 us
  transfers between devices with their start and end apart: 25, of which 10 were waited for; matrix products, arithmetic and copies ran while one was open for 5% of the time, Pallas kernels for 10%

profile of v1, /device:TPU:7, one launch (start us, length us, event | category | flops | bytes accessed | tf_op | source)
XLA Modules:
  0.0 84.9 jit_solution(23679049532193455)
XLA Ops:
  0.0 3.0 %collective-permute-start.2 = (bf16[4,8,4,512]{3,2,1,0:T(4,128)(2,1)}, bf16[4,8,4,512]{3,2,1,0:T(4,128)(2,1)S(1)}, u32[]{:S(2)}, u32[]{:S(2)}) collective-permute-start(bf16[4,8,4,512]{3,2,1,0:T(4,128)(2,1)} %own_ref.1), channel_id=1, source_target_pairs={{0,64},{32,96},{64,128},{96,160},{128,192},{160,224},{192,0},{224,... | collective-permute-start | bytes 393224 | tf_op jit(solution)/shard_map/ppermute | solution.py:520
  3.0 3.0 %collective-permute-start.3 = (bf16[4,8,4,512]{3,2,1,0:T(4,128)(2,1)}, bf16[4,8,4,512]{3,2,1,0:T(4,128)(2,1)S(1)}, u32[]{:S(2)}, u32[]{:S(2)}) collective-permute-start(bf16[4,8,4,512]{3,2,1,0:T(4,128)(2,1)} %own_ref.1), channel_id=1, source_target_pairs={{0,192},{32,224},{64,0},{96,32},{128,64},{160,96},{192,128},{224,1... | collective-permute-start | bytes 393224 | tf_op jit(solution)/shard_map/ppermute | solution.py:520
  6.8 1.9 %collective-permute-start.1 = (bf16[4,8,4,512]{3,2,1,0:T(4,128)(2,1)}, bf16[4,8,4,512]{3,2,1,0:T(4,128)(2,1)S(1)}, u32[]{:S(2)}, u32[]{:S(2)}) collective-permute-start(bf16[4,8,4,512]{3,2,1,0:T(4,128)(2,1)} %own_ref.1), channel_id=1, source_target_pairs={{0,224},{32,0},{64,32},{96,64},{128,96},{160,128},{192,160},{224,1... | collective-permute-start | bytes 393224 | tf_op jit(solution)/shard_map/ppermute | solution.py:520
  10.1 3.0 %collective-permute-start.6 = (bf16[2,8,4,512]{3,2,1,0:T(4,128)(2,1)S(1)}, bf16[2,8,4,512]{3,2,1,0:T(4,128)(2,1)S(1)}, u32[]{:S(2)}, u32[]{:S(2)}) collective-permute-start(bf16[2,8,4,512]{3,2,1,0:T(4,128)(2,1)S(1)} %slice.16), channel_id=1, source_target_pairs={{0,64},{32,96},{64,128},{96,160},{128,192},{160,224},{192,0},{224,... | collective-permute-start | bytes 196616 | tf_op jit(solution)/shard_map/ppermute | solution.py:520
  13.8 2.4 %collective-permute-start.7 = (bf16[2,8,4,512]{3,2,1,0:T(4,128)(2,1)S(1)}, bf16[2,8,4,512]{3,2,1,0:T(4,128)(2,1)S(1)}, u32[]{:S(2)}, u32[]{:S(2)}) collective-permute-start(bf16[2,8,4,512]{3,2,1,0:T(4,128)(2,1)S(1)} %slice.17), channel_id=1, source_target_pairs={{0,192},{32,224},{64,0},{96,32},{128,64},{160,96},{192,128},{224,1... | collective-permute-start | bytes 196616 | tf_op jit(solution)/shard_map/ppermute | solution.py:520
  17.1 1.8 %collective-permute-start.5 = (bf16[4,8,4,512]{3,2,1,0:T(4,128)(2,1)S(1)}, bf16[4,8,4,512]{3,2,1,0:T(4,128)(2,1)S(1)}, u32[]{:S(2)}, u32[]{:S(2)}) collective-permute-start(bf16[4,8,4,512]{3,2,1,0:T(4,128)(2,1)S(1)} %collective-permute-done.3.back_ref), channel_id=1, source_target_pairs={{0,224},{32,0},{64,32},{96,64},{128,96},{160,128},{192,160},{224,1... | collective-permute-start | bytes 393224 | tf_op jit(solution)/shard_map/ppermute | solution.py:520
  20.5 2.6 %hold_blocks.2.held = bf16[64,320,128]{2,1,0:T(8,128)(2,1)S(1)} custom-call(bf16[64,320,128]{2,1,0:T(8,128)(2,1)} %bitcast.13, bf16[4,8,4,512]{3,2,1,0:T(4,128)(2,1)S(1)} %collective-permute-done.2.two_ref.after_ref), custom_call_target="tpu_custom_call" | custom-call | bytes 7500000 | tf_op jit(solution)/shard_map/hold_blocks/pallas_call | solution.py:128
  23.1 1.3 %gather_first.1 = (f32[320,256]{1,0:T(8,128)S(1)}, bf16[256,256]{1,0:T(8,128)(2,1)S(1)}, bf16[256,256]{1,0:T(8,128)(2,1)S(1)}, bf16[256,256]{1,0:T(8,128)(2,1)S(1)}) custom-call(s32[8]{0:T(128)S(1)} %fusion.5.base_ref, s32[320,1]{1,0:T(8,128)S(1)} %or.27.keys_ref, f32[320,1]{1,0:T(8,128)S(1)} %reshape.88.weights_ref, bf16[4,8,4,512]{3,2,1,0:T(4,128)(2,1)S(1)} %copy-done, ...), custom_call_target="tpu_custom_call" | custom-call | bytes 4500000 | tf_op jit(solution)/shard_map/gather_first/pallas_call | solution.py:94
  24.5 2.1 %project.1 = bf16[256,128]{1,0:T(8,128)(2,1)S(1)} custom-call(s32[8]{0:T(128)S(1)} %fusion.5.base_ref, s32[1]{0:T(128)} %bitcast.5.slab_ref, s32[320,1]{1,0:T(8,128)S(1)} %or.27.keys_ref, f32[320,1]{1,0:T(8,128)S(1)} %reshape.88.weights_ref, f32[320,256]{1,0:T(8,128)S(1)} %get-tuple-element.19.before_ref, ...), custom_call_target="tpu_custom_call" | custom-call | bytes 12000000 | tf_op jit(solution)/shard_map/project/pallas_call | solution.py:188
  26.6 2.5 %collective-permute-start.8 = (bf16[256,128]{1,0:T(8,128)(2,1)S(1)}, bf16[256,128]{1,0:T(8,128)(2,1)S(1)}, u32[]{:S(2)}, u32[]{:S(2)}) collective-permute-start(bf16[256,128]{1,0:T(8,128)(2,1)S(1)} %project.1), channel_id=1, source_target_pairs={{0,1},{1,0},{2,3},{3,2},{4,5},{5,4},{6,7},{7,6},{8,9},{9,8},{10,11... | collective-permute-start | bytes 196616 | tf_op jit(solution)/shard_map/ppermute | solution.py:533
  31.5 1.8 %collective-permute-start.9 = (bf16[256,128]{1,0:T(8,128)(2,1)S(1)}, bf16[256,128]{1,0:T(8,128)(2,1)S(1)}, u32[]{:S(2)}, u32[]{:S(2)}) collective-permute-start(bf16[256,128]{1,0:T(8,128)(2,1)S(1)} %add_convert_fusion.1.after_ref), channel_id=1, source_target_pairs={{0,2},{1,3},{2,4},{3,5},{4,6},{5,7},{6,0},{7,1},{8,10},{9,11},{10,... | collective-permute-start | bytes 196616 | tf_op jit(solution)/shard_map/ppermute | solution.py:539
  33.4 1.0 %collective-permute-done.10 = bf16[256,128]{1,0:T(8,128)(2,1)S(1)} collective-permute-done((bf16[256,128]{1,0:T(8,128)(2,1)S(1)}, bf16[256,128]{1,0:T(8,128)(2,1)S(1)}, u32[]{:S(2)}, u32[]{:S(2)}) %collective-permute-start.10) | collective-permute-done | bytes 65568 | tf_op jit(solution)/shard_map/ppermute | solution.py:539
  34.4 0.9 %collective-permute-done.11 = bf16[256,128]{1,0:T(8,128)(2,1)S(1)} collective-permute-done((bf16[256,128]{1,0:T(8,128)(2,1)S(1)}, bf16[256,128]{1,0:T(8,128)(2,1)S(1)}, u32[]{:S(2)}, u32[]{:S(2)}) %collective-permute-start.11) | collective-permute-done | bytes 65568 | tf_op jit(solution)/shard_map/ppermute | solution.py:539
  36.3 1.4 %collective-permute-start.12 = (bf16[256,128]{1,0:T(8,128)(2,1)S(1)}, bf16[256,128]{1,0:T(8,128)(2,1)S(1)}, u32[]{:S(2)}, u32[]{:S(2)}) collective-permute-start(bf16[256,128]{1,0:T(8,128)(2,1)S(1)} %add_convert_fusion.own_ref), channel_id=1, source_target_pairs={{0,8},{1,9},{2,10},{3,11},{4,12},{5,13},{6,14},{7,15},{8,16},{9,17... | collective-permute-start | bytes 196616 | tf_op jit(solution)/shard_map/ppermute | solution.py:542
  37.7 1.7 %collective-permute-start.13 = (bf16[256,128]{1,0:T(8,128)(2,1)S(1)}, bf16[256,128]{1,0:T(8,128)(2,1)S(1)}, u32[]{:S(2)}, u32[]{:S(2)}) collective-permute-start(bf16[256,128]{1,0:T(8,128)(2,1)S(1)} %add_convert_fusion.own_ref), channel_id=1, source_target_pairs={{0,24},{1,25},{2,26},{3,27},{4,28},{5,29},{6,30},{7,31},{8,0},{9,1... | collective-permute-start | bytes 196616 | tf_op jit(solution)/shard_map/ppermute | solution.py:542
  39.4 1.4 %collective-permute-start.14 = (bf16[256,128]{1,0:T(8,128)(2,1)S(1)}, bf16[256,128]{1,0:T(8,128)(2,1)S(1)}, u32[]{:S(2)}, u32[]{:S(2)}) collective-permute-start(bf16[256,128]{1,0:T(8,128)(2,1)S(1)} %add_convert_fusion.own_ref), channel_id=1, source_target_pairs={{0,16},{1,17},{2,18},{3,19},{4,20},{5,21},{6,22},{7,23},{8,24},{9,... | collective-permute-start | bytes 196616 | tf_op jit(solution)/shard_map/ppermute | solution.py:542
  40.9 2.5 %hold_blocks.3.held = bf16[64,320,128]{2,1,0:T(8,128)(2,1)S(1)} custom-call(bf16[64,320,128]{2,1,0:T(8,128)(2,1)} %bitcast.14, bf16[256,128]{1,0:T(8,128)(2,1)S(1)} %add_convert_fusion.1.after_ref), custom_call_target="tpu_custom_call" | custom-call | bytes 7500000 | tf_op jit(solution)/shard_map/hold_blocks/pallas_call | solution.py:128
  43.5 1.2 %collective-permute-done.14.three_ref = bf16[256,128]{1,0:T(8,128)(2,1)S(1)} collective-permute-done((bf16[256,128]{1,0:T(8,128)(2,1)S(1)}, bf16[256,128]{1,0:T(8,128)(2,1)S(1)}, u32[]{:S(2)}, u32[]{:S(2)}) %collective-permute-start.14) | collective-permute-done | bytes 65568 | tf_op jit(solution)/shard_map/ppermute | solution.py:542
  44.6 1.9 %adjoint.1.refs_0_ = bf16[336,256]{1,0:T(8,128)(2,1)S(1)} custom-call(bf16[256,128]{1,0:T(8,128)(2,1)S(1)} %add_convert_fusion.own_ref, bf16[256,128]{1,0:T(8,128)(2,1)S(1)} %collective-permute-done.12.one_ref, bf16[256,128]{1,0:T(8,128)(2,1)S(1)} %collective-permute-done.13.two_ref, bf16[256,128]{1,0:T(8,128)(2,1)S(1)} %collective-permute-done.14.three_ref, ...), custom_call_target="tpu_custom_call" | custom-call | bytes 9000000 | tf_op jit(solution)/shard_map/adjoint/pallas_call | solution.py:237
  47.0 3.1 %collective-permute-start.18 = (bf16[336,256]{1,0:T(8,128)(2,1)S(1)}, bf16[336,256]{1,0:T(8,128)(2,1)S(1)}, u32[]{:S(2)}, u32[]{:S(2)}) collective-permute-start(bf16[336,256]{1,0:T(8,128)(2,1)S(1)} %adjoint.1.refs_0_), channel_id=1, source_target_pairs={{0,192},{32,224},{64,0},{96,32},{128,64},{160,96},{192,128},{224,1... | collective-permute-start | bytes 516104 | tf_op jit(solution)/shard_map/ppermute | solution.py:520
  50.4 2.7 %collective-permute-start.16 = (bf16[336,256]{1,0:T(8,128)(2,1)S(1)}, bf16[336,256]{1,0:T(8,128)(2,1)S(1)}, u32[]{:S(2)}, u32[]{:S(2)}) collective-permute-start(bf16[336,256]{1,0:T(8,128)(2,1)S(1)} %adjoint.1.refs_0_), channel_id=1, source_target_pairs={{0,224},{32,0},{64,32},{96,64},{128,96},{160,128},{192,160},{224,1... | collective-permute-start | bytes 516104 | tf_op jit(solution)/shard_map/ppermute | solution.py:520
  53.1 2.0 %collective-permute-done.17.refs_3_ = bf16[336,256]{1,0:T(8,128)(2,1)S(1)} collective-permute-done((bf16[336,256]{1,0:T(8,128)(2,1)S(1)}, bf16[336,256]{1,0:T(8,128)(2,1)S(1)}, u32[]{:S(2)}, u32[]{:S(2)}) %collective-permute-start.17) | collective-permute-done | bytes 172064 | tf_op jit(solution)/shard_map/ppermute | solution.py:520
  55.1 3.3 %collective-permute-done.18.refs_4_ = bf16[336,256]{1,0:T(8,128)(2,1)S(1)} collective-permute-done((bf16[336,256]{1,0:T(8,128)(2,1)S(1)}, bf16[336,256]{1,0:T(8,128)(2,1)S(1)}, u32[]{:S(2)}, u32[]{:S(2)}) %collective-permute-start.18) | collective-permute-done | bytes 172064 | tf_op jit(solution)/shard_map/ppermute | solution.py:520
  58.5 1.7 %collective-permute-start.21 = (bf16[176,256]{1,0:T(8,128)(2,1)S(1)}, bf16[176,256]{1,0:T(8,128)(2,1)S(1)}, u32[]{:S(2)}, u32[]{:S(2)}) collective-permute-start(bf16[176,256]{1,0:T(8,128)(2,1)S(1)} %slice.18), channel_id=1, source_target_pairs={{0,64},{32,96},{64,128},{96,160},{128,192},{160,224},{192,0},{224,... | collective-permute-start | bytes 270344 | tf_op jit(solution)/shard_map/ppermute | solution.py:520
  60.2 2.0 %collective-permute-start.22 = (bf16[160,256]{1,0:T(8,128)(2,1)S(1)}, bf16[160,256]{1,0:T(8,128)(2,1)S(1)}, u32[]{:S(2)}, u32[]{:S(2)}) collective-permute-start(bf16[160,256]{1,0:T(8,128)(2,1)S(1)} %slice.19), channel_id=1, source_target_pairs={{0,192},{32,224},{64,0},{96,32},{128,64},{160,96},{192,128},{224,1... | collective-permute-start | bytes 245768 | tf_op jit(solution)/shard_map/ppermute | solution.py:520
  63.0 1.2 %scatter_first.1.before_ref = f32[384,256]{1,0:T(8,128)S(1)} custom-call(s32[3]{0:T(128)S(1)} %pad_add_fusion.pos_ref, bf16[336,256]{1,0:T(8,128)(2,1)S(1)} %adjoint.1.refs_0_, bf16[336,256]{1,0:T(8,128)(2,1)S(1)} %collective-permute-done.15.refs_1_, bf16[336,256]{1,0:T(8,128)(2,1)S(1)} %collective-permute-done.16.refs_2_, ...), custom_call_target="tpu_custom_call" | custom-call | bytes 2100000 | tf_op jit(solution)/shard_map/scatter_first/pallas_call | solution.py:326
  64.2 2.5 %collective-permute-done.22.half_b_ref = bf16[160,256]{1,0:T(8,128)(2,1)S(1)} collective-permute-done((bf16[160,256]{1,0:T(8,128)(2,1)S(1)}, bf16[160,256]{1,0:T(8,128)(2,1)S(1)}, u32[]{:S(2)}, u32[]{:S(2)}) %collective-permute-start.22) | collective-permute-done | bytes 81952 | tf_op jit(solution)/shard_map/ppermute | solution.py:520
  66.8 1.1 %gradient_planes.1 = (f32[4,4,48,128]{3,2,1,0:T(8,128)S(1)}, bf16[48,512]{1,0:T(8,128)(2,1)S(1)}, bf16[48,512]{1,0:T(8,128)(2,1)S(1)}) custom-call(s32[3]{0:T(128)S(1)} %pad_add_fusion.pos_ref, f32[384,256]{1,0:T(8,128)S(1)} %scatter_first.1.before_ref, bf16[336,256]{1,0:T(8,128)(2,1)S(1)} %collective-permute-done.19.three_ref, ...), custom_call_target="tpu_custom_call" | custom-call | bytes 3000000 | tf_op jit(solution)/shard_map/gradient_planes/pallas_call | solution.py:371
  67.9 4.8 %collective-permute-start.23 = (bf16[48,512]{1,0:T(8,128)(2,1)S(1)}, bf16[48,512]{1,0:T(8,128)(2,1)S(1)}, u32[]{:S(2)}, u32[]{:S(2)}) collective-permute-start(bf16[48,512]{1,0:T(8,128)(2,1)S(1)} %get-tuple-element.23), channel_id=1, source_target_pairs={{0,1},{1,0},{2,3},{3,2},{4,5},{5,4},{6,7},{7,6},{8,9},{9,8},{10,11... | collective-permute-start | bytes 147464 | tf_op jit(solution)/shard_map/ppermute | solution.py:585
  72.7 3.9 %collective-permute-start.24 = (bf16[48,512]{1,0:T(8,128)(2,1)S(1)}, bf16[48,512]{1,0:T(8,128)(2,1)S(1)}, u32[]{:S(2)}, u32[]{:S(2)}) collective-permute-start(bf16[48,512]{1,0:T(8,128)(2,1)S(1)} %get-tuple-element.24), channel_id=1, source_target_pairs={{1,2},{3,4},{5,6},{7,8},{9,10},{11,12},{13,14},{15,16},{17,18},{19... | collective-permute-start | bytes 147464 | tf_op jit(solution)/shard_map/ppermute | solution.py:587
  77.0 3.2 %collective-permute-done.24.outer_ref = bf16[48,512]{1,0:T(8,128)(2,1)S(1)} collective-permute-done((bf16[48,512]{1,0:T(8,128)(2,1)S(1)}, bf16[48,512]{1,0:T(8,128)(2,1)S(1)}, u32[]{:S(2)}, u32[]{:S(2)}) %collective-permute-start.24) | collective-permute-done | bytes 49184 | tf_op jit(solution)/shard_map/ppermute | solution.py:587
  80.2 4.7 %convolutions.1 = f32[4,8,4,512]{3,2,1,0:T(4,128)} custom-call(s32[3]{0:T(128)S(1)} %pad_add_fusion.pos_ref, f32[4,4,48,128]{3,2,1,0:T(8,128)S(1)} %get-tuple-element.18.image_ref, f32[4,4,48,128]{3,2,1,0:T(8,128)S(1)} %get-tuple-element.22.grad_ref, bf16[48,512]{1,0:T(8,128)(2,1)S(1)} %collective-permute-done.23.inner_ref, ...), custom_call_target="tpu_custom_call" | custom-call | bytes 15000000 | tf_op jit(solution)/shard_map/convolutions/pallas_call | solution.py:459
  (65 shorter events, 11.1 us)
Async XLA Ops:
  0.0 10.1 %collective-permute-start.2 = (bf16[4,8,4,512]{3,2,1,0:T(4,128)(2,1)}, bf16[4,8,4,512]{3,2,1,0:T(4,128)(2,1)S(1)}, u32[]{:S(2)}, u32[]{:S(2)}) collective-permute-start(bf16[4,8,4,512]{3,2,1,0:T(4,128)(2,1)} %own_ref.1), channel_id=1, source_target_pairs={{0,64},{32,96},{64,128},{96,160},{128,192},{160,224},{192,0},{224,... | collective-permute-start | bytes 393224 | tf_op jit(solution)/shard_map/ppermute | solution.py:520
  3.0 10.8 %collective-permute-start.3 = (bf16[4,8,4,512]{3,2,1,0:T(4,128)(2,1)}, bf16[4,8,4,512]{3,2,1,0:T(4,128)(2,1)S(1)}, u32[]{:S(2)}, u32[]{:S(2)}) collective-permute-start(bf16[4,8,4,512]{3,2,1,0:T(4,128)(2,1)} %own_ref.1), channel_id=1, source_target_pairs={{0,192},{32,224},{64,0},{96,32},{128,64},{160,96},{192,128},{224,1... | collective-permute-start | bytes 393224 | tf_op jit(solution)/shard_map/ppermute | solution.py:520
  6.0 11.1 %collective-permute-start = (bf16[4,8,4,512]{3,2,1,0:T(4,128)(2,1)}, bf16[4,8,4,512]{3,2,1,0:T(4,128)(2,1)S(1)}, u32[]{:S(2)}, u32[]{:S(2)}) collective-permute-start(bf16[4,8,4,512]{3,2,1,0:T(4,128)(2,1)} %own_ref.1), channel_id=1, source_target_pairs={{0,32},{32,64},{64,96},{96,128},{128,160},{160,192},{192,224},{224... | collective-permute-start | bytes 393224 | tf_op jit(solution)/shard_map/ppermute | solution.py:520
  6.8 16.4 %collective-permute-start.1 = (bf16[4,8,4,512]{3,2,1,0:T(4,128)(2,1)}, bf16[4,8,4,512]{3,2,1,0:T(4,128)(2,1)S(1)}, u32[]{:S(2)}, u32[]{:S(2)}) collective-permute-start(bf16[4,8,4,512]{3,2,1,0:T(4,128)(2,1)} %own_ref.1), channel_id=1, source_target_pairs={{0,224},{32,0},{64,32},{96,64},{128,96},{160,128},{192,160},{224,1... | collective-permute-start | bytes 393224 | tf_op jit(solution)/shard_map/ppermute | solution.py:520
  10.1 14.3 %collective-permute-start.6 = (bf16[2,8,4,512]{3,2,1,0:T(4,128)(2,1)S(1)}, bf16[2,8,4,512]{3,2,1,0:T(4,128)(2,1)S(1)}, u32[]{:S(2)}, u32[]{:S(2)}) collective-permute-start(bf16[2,8,4,512]{3,2,1,0:T(4,128)(2,1)S(1)} %slice.16), channel_id=1, source_target_pairs={{0,64},{32,96},{64,128},{96,160},{128,192},{160,224},{192,0},{224,... | collective-permute-start | bytes 196616 | tf_op jit(solution)/shard_map/ppermute | solution.py:520
  13.8 10.7 %collective-permute-start.7 = (bf16[2,8,4,512]{3,2,1,0:T(4,128)(2,1)S(1)}, bf16[2,8,4,512]{3,2,1,0:T(4,128)(2,1)S(1)}, u32[]{:S(2)}, u32[]{:S(2)}) collective-permute-start(bf16[2,8,4,512]{3,2,1,0:T(4,128)(2,1)S(1)} %slice.17), channel_id=1, source_target_pairs={{0,192},{32,224},{64,0},{96,32},{128,64},{160,96},{192,128},{224,1... | collective-permute-start | bytes 196616 | tf_op jit(solution)/shard_map/ppermute | solution.py:520
  16.2 8.3 %collective-permute-start.4 = (bf16[4,8,4,512]{3,2,1,0:T(4,128)(2,1)S(1)}, bf16[4,8,4,512]{3,2,1,0:T(4,128)(2,1)S(1)}, u32[]{:S(2)}, u32[]{:S(2)}) collective-permute-start(bf16[4,8,4,512]{3,2,1,0:T(4,128)(2,1)S(1)} %collective-permute-done.2.two_ref.after_ref), channel_id=1, source_target_pairs={{0,32},{32,64},{64,96},{96,128},{128,160},{160,192},{192,224},{224... | collective-permute-start | bytes 393224 | tf_op jit(solution)/shard_map/ppermute | solution.py:520
  17.1 7.4 %collective-permute-start.5 = (bf16[4,8,4,512]{3,2,1,0:T(4,128)(2,1)S(1)}, bf16[4,8,4,512]{3,2,1,0:T(4,128)(2,1)S(1)}, u32[]{:S(2)}, u32[]{:S(2)}) collective-permute-start(bf16[4,8,4,512]{3,2,1,0:T(4,128)(2,1)S(1)} %collective-permute-done.3.back_ref), channel_id=1, source_target_pairs={{0,224},{32,0},{64,32},{96,64},{128,96},{160,128},{192,160},{224,1... | collective-permute-start | bytes 393224 | tf_op jit(solution)/shard_map/ppermute | solution.py:520
  20.5 2.6 %copy-start = (bf16[4,8,4,512]{3,2,1,0:T(4,128)(2,1)S(1)}, bf16[4,8,4,512]{3,2,1,0:T(4,128)(2,1)}, u32[]{:S(2)}) copy-start(bf16[4,8,4,512]{3,2,1,0:T(4,128)(2,1)} %own_ref.1) | copy-start | bytes 393220
  23.1 6.0 %copy-start.4 = (s32[64,5]{0,1:T(8,128)S(1)}, s32[64,5]{0,1:T(8,128)}, u32[]{:S(2)}) copy-start(s32[64,5]{0,1:T(8,128)} %param.14) | copy-start | bytes 3844
  26.6 3.4 %collective-permute-start.8 = (bf16[256,128]{1,0:T(8,128)(2,1)S(1)}, bf16[256,128]{1,0:T(8,128)(2,1)S(1)}, u32[]{:S(2)}, u32[]{:S(2)}) collective-permute-start(bf16[256,128]{1,0:T(8,128)(2,1)S(1)} %project.1), channel_id=1, source_target_pairs={{0,1},{1,0},{2,3},{3,2},{4,5},{5,4},{6,7},{7,6},{8,9},{9,8},{10,11... | collective-permute-start | bytes 196616 | tf_op jit(solution)/shard_map/ppermute | solution.py:533
  30.0 4.4 %collective-permute-start.10 = (bf16[256,128]{1,0:T(8,128)(2,1)S(1)}, bf16[256,128]{1,0:T(8,128)(2,1)S(1)}, u32[]{:S(2)}, u32[]{:S(2)}) collective-permute-start(bf16[256,128]{1,0:T(8,128)(2,1)S(1)} %add_convert_fusion.1.after_ref), channel_id=1, source_target_pairs={{0,6},{1,7},{2,0},{3,1},{4,2},{5,3},{6,4},{7,5},{8,14},{9,15},{10,... | collective-permute-start | bytes 196616 | tf_op jit(solution)/shard_map/ppermute | solution.py:539
  30.6 4.7 %collective-permute-start.11 = (bf16[256,128]{1,0:T(8,128)(2,1)S(1)}, bf16[256,128]{1,0:T(8,128)(2,1)S(1)}, u32[]{:S(2)}, u32[]{:S(2)}) collective-permute-start(bf16[256,128]{1,0:T(8,128)(2,1)S(1)} %add_convert_fusion.1.after_ref), channel_id=1, source_target_pairs={{0,4},{1,5},{2,6},{3,7},{4,0},{5,1},{6,2},{7,3},{8,12},{9,13},{10,... | collective-permute-start | bytes 196616 | tf_op jit(solution)/shard_map/ppermute | solution.py:539
  31.5 4.8 %collective-permute-start.9 = (bf16[256,128]{1,0:T(8,128)(2,1)S(1)}, bf16[256,128]{1,0:T(8,128)(2,1)S(1)}, u32[]{:S(2)}, u32[]{:S(2)}) collective-permute-start(bf16[256,128]{1,0:T(8,128)(2,1)S(1)} %add_convert_fusion.1.after_ref), channel_id=1, source_target_pairs={{0,2},{1,3},{2,4},{3,5},{4,6},{5,7},{6,0},{7,1},{8,10},{9,11},{10,... | collective-permute-start | bytes 196616 | tf_op jit(solution)/shard_map/ppermute | solution.py:539
  36.3 7.1 %collective-permute-start.12 = (bf16[256,128]{1,0:T(8,128)(2,1)S(1)}, bf16[256,128]{1,0:T(8,128)(2,1)S(1)}, u32[]{:S(2)}, u32[]{:S(2)}) collective-permute-start(bf16[256,128]{1,0:T(8,128)(2,1)S(1)} %add_convert_fusion.own_ref), channel_id=1, source_target_pairs={{0,8},{1,9},{2,10},{3,11},{4,12},{5,13},{6,14},{7,15},{8,16},{9,17... | collective-permute-start | bytes 196616 | tf_op jit(solution)/shard_map/ppermute | solution.py:542
  37.7 5.8 %collective-permute-start.13 = (bf16[256,128]{1,0:T(8,128)(2,1)S(1)}, bf16[256,128]{1,0:T(8,128)(2,1)S(1)}, u32[]{:S(2)}, u32[]{:S(2)}) collective-permute-start(bf16[256,128]{1,0:T(8,128)(2,1)S(1)} %add_convert_fusion.own_ref), channel_id=1, source_target_pairs={{0,24},{1,25},{2,26},{3,27},{4,28},{5,29},{6,30},{7,31},{8,0},{9,1... | collective-permute-start | bytes 196616 | tf_op jit(solution)/shard_map/ppermute | solution.py:542
  39.4 5.2 %collective-permute-start.14 = (bf16[256,128]{1,0:T(8,128)(2,1)S(1)}, bf16[256,128]{1,0:T(8,128)(2,1)S(1)}, u32[]{:S(2)}, u32[]{:S(2)}) collective-permute-start(bf16[256,128]{1,0:T(8,128)(2,1)S(1)} %add_convert_fusion.own_ref), channel_id=1, source_target_pairs={{0,16},{1,17},{2,18},{3,19},{4,20},{5,21},{6,22},{7,23},{8,24},{9,... | collective-permute-start | bytes 196616 | tf_op jit(solution)/shard_map/ppermute | solution.py:542
  43.4 6.7 %copy-start.3 = (f32[32,2,27]{0,1,2:T(2,128)S(1)}, f32[32,2,27]{0,1,2:T(2,128)}, u32[]{:S(2)}) copy-start(f32[32,2,27]{0,1,2:T(2,128)} %param.17) | copy-start | bytes 20740
  43.4 6.9 %copy-start.5 = (f32[32]{0:T(128)S(1)}, f32[32]{0:T(128)}, u32[]{:S(2)}) copy-start(f32[32]{0:T(128)} %param.18) | copy-start | bytes 388
  43.4 33.2 %copy-start.2 = (bf16[55,1536]{1,0:T(8,128)(2,1)S(1)}, bf16[55,1536]{1,0:T(8,128)(2,1)}, u32[]{:S(2)}) copy-start(bf16[55,1536]{1,0:T(8,128)(2,1)} %constant.67.clone) | copy-start | bytes 506884
  43.4 36.8 %copy-start.1 = (f32[32]{0:T(128)S(1)}, f32[32]{0:T(128)}, u32[]{:S(2)}) copy-start(f32[32]{0:T(128)} %out_w_ref.1) | copy-start | bytes 388
  46.5 8.6 %collective-permute-start.17 = (bf16[336,256]{1,0:T(8,128)(2,1)S(1)}, bf16[336,256]{1,0:T(8,128)(2,1)S(1)}, u32[]{:S(2)}, u32[]{:S(2)}) collective-permute-start(bf16[336,256]{1,0:T(8,128)(2,1)S(1)} %adjoint.1.refs_0_), channel_id=1, source_target_pairs={{0,64},{32,96},{64,128},{96,160},{128,192},{160,224},{192,0},{224,... | collective-permute-start | bytes 516104 | tf_op jit(solution)/shard_map/ppermute | solution.py:520
  47.0 11.4 %collective-permute-start.18 = (bf16[336,256]{1,0:T(8,128)(2,1)S(1)}, bf16[336,256]{1,0:T(8,128)(2,1)S(1)}, u32[]{:S(2)}, u32[]{:S(2)}) collective-permute-start(bf16[336,256]{1,0:T(8,128)(2,1)S(1)} %adjoint.1.refs_0_), channel_id=1, source_target_pairs={{0,192},{32,224},{64,0},{96,32},{128,64},{160,96},{192,128},{224,1... | collective-permute-start | bytes 516104 | tf_op jit(solution)/shard_map/ppermute | solution.py:520
  50.1 10.1 %collective-permute-start.15 = (bf16[336,256]{1,0:T(8,128)(2,1)S(1)}, bf16[336,256]{1,0:T(8,128)(2,1)S(1)}, u32[]{:S(2)}, u32[]{:S(2)}) collective-permute-start(bf16[336,256]{1,0:T(8,128)(2,1)S(1)} %adjoint.1.refs_0_), channel_id=1, source_target_pairs={{0,32},{32,64},{64,96},{96,128},{128,160},{160,192},{192,224},{224... | collective-permute-start | bytes 516104 | tf_op jit(solution)/shard_map/ppermute | solution.py:520
  50.4 12.6 %collective-permute-start.16 = (bf16[336,256]{1,0:T(8,128)(2,1)S(1)}, bf16[336,256]{1,0:T(8,128)(2,1)S(1)}, u32[]{:S(2)}, u32[]{:S(2)}) collective-permute-start(bf16[336,256]{1,0:T(8,128)(2,1)S(1)} %adjoint.1.refs_0_), channel_id=1, source_target_pairs={{0,224},{32,0},{64,32},{96,64},{128,96},{160,128},{192,160},{224,1... | collective-permute-start | bytes 516104 | tf_op jit(solution)/shard_map/ppermute | solution.py:520
  55.1 11.6 %collective-permute-start.19 = (bf16[336,256]{1,0:T(8,128)(2,1)S(1)}, bf16[336,256]{1,0:T(8,128)(2,1)S(1)}, u32[]{:S(2)}, u32[]{:S(2)}) collective-permute-start(bf16[336,256]{1,0:T(8,128)(2,1)S(1)} %collective-permute-done.17.refs_3_), channel_id=1, source_target_pairs={{0,32},{32,64},{64,96},{96,128},{128,160},{160,192},{192,224},{224... | collective-permute-start | bytes 516104 | tf_op jit(solution)/shard_map/ppermute | solution.py:520
  58.4 8.4 %collective-permute-start.20 = (bf16[336,256]{1,0:T(8,128)(2,1)S(1)}, bf16[336,256]{1,0:T(8,128)(2,1)S(1)}, u32[]{:S(2)}, u32[]{:S(2)}) collective-permute-start(bf16[336,256]{1,0:T(8,128)(2,1)S(1)} %collective-permute-done.18.refs_4_), channel_id=1, source_target_pairs={{0,224},{32,0},{64,32},{96,64},{128,96},{160,128},{192,160},{224,1... | collective-permute-start | bytes 516104 | tf_op jit(solution)/shard_map/ppermute | solution.py:520
  58.5 8.3 %collective-permute-start.21 = (bf16[176,256]{1,0:T(8,128)(2,1)S(1)}, bf16[176,256]{1,0:T(8,128)(2,1)S(1)}, u32[]{:S(2)}, u32[]{:S(2)}) collective-permute-start(bf16[176,256]{1,0:T(8,128)(2,1)S(1)} %slice.18), channel_id=1, source_target_pairs={{0,64},{32,96},{64,128},{96,160},{128,192},{160,224},{192,0},{224,... | collective-permute-start | bytes 270344 | tf_op jit(solution)/shard_map/ppermute | solution.py:520
  60.2 6.5 %collective-permute-start.22 = (bf16[160,256]{1,0:T(8,128)(2,1)S(1)}, bf16[160,256]{1,0:T(8,128)(2,1)S(1)}, u32[]{:S(2)}, u32[]{:S(2)}) collective-permute-start(bf16[160,256]{1,0:T(8,128)(2,1)S(1)} %slice.19), channel_id=1, source_target_pairs={{0,192},{32,224},{64,0},{96,32},{128,64},{160,96},{192,128},{224,1... | collective-permute-start | bytes 245768 | tf_op jit(solution)/shard_map/ppermute | solution.py:520
  67.9 9.1 %collective-permute-start.23 = (bf16[48,512]{1,0:T(8,128)(2,1)S(1)}, bf16[48,512]{1,0:T(8,128)(2,1)S(1)}, u32[]{:S(2)}, u32[]{:S(2)}) collective-permute-start(bf16[48,512]{1,0:T(8,128)(2,1)S(1)} %get-tuple-element.23), channel_id=1, source_target_pairs={{0,1},{1,0},{2,3},{3,2},{4,5},{5,4},{6,7},{7,6},{8,9},{9,8},{10,11... | collective-permute-start | bytes 147464 | tf_op jit(solution)/shard_map/ppermute | solution.py:585
  72.7 7.5 %collective-permute-start.24 = (bf16[48,512]{1,0:T(8,128)(2,1)S(1)}, bf16[48,512]{1,0:T(8,128)(2,1)S(1)}, u32[]{:S(2)}, u32[]{:S(2)}) collective-permute-start(bf16[48,512]{1,0:T(8,128)(2,1)S(1)} %get-tuple-element.24), channel_id=1, source_target_pairs={{1,2},{3,4},{5,6},{7,8},{9,10},{11,12},{13,14},{15,16},{17,18},{19... | collective-permute-start | bytes 147464 | tf_op jit(solution)/shard_map/ppermute | solution.py:587

commit v2 on v1

--- a/solution.py
+++ b/solution.py
@@ -18,10 +18,19 @@
 NB = 4
 TB = 128
 OWN = 256
+CAP = 80
+PACKED = CAP + 16
 SENT = SLOTS + 16
 SENT_SPLIT = 176
 CHAN = 32
 TAPS = 192
+
+
+def owner_base(step):
+    return lax.rem(lax.axis_index("sensor") + (step + 8), 8) * OWN
+
+
+STEPS = (0, -1, 1, -2, 2, -3, 3, 4)
 
 
 def vmem():
@@ -78,7 +87,7 @@
 
 
 def gather_kernel(
-    base_ref, keys_ref, weights_ref, own_ref, plus_ref, minus_ref, two_ref, back_ref,
+    keys_ref, weights_ref, own_ref, plus_ref, minus_ref, two_ref, back_ref,
     out_ref, own_rows, plus_rows, minus_rows, rows, shard,
 ):
     acc = jnp.zeros((SLOTS, 256), F32)
@@ -86,16 +95,16 @@
     shards = (own_rows, plus_rows, minus_rows, shard.at[0], shard.at[1])
     for i, ref in enumerate((own_ref, plus_ref, minus_ref, two_ref, back_ref)):
         planes_to_rows([ref], rows.at[i], shards[i])
-        acc = add_gathered(acc, keys, weights, base_ref[i], shards[i][...])
+        acc = add_gathered(acc, keys, weights, owner_base(STEPS[i]), shards[i][...])
     out_ref[...] = acc
 
 
-def gather_first(base, keys, weights, shards):
+def gather_first(keys, weights, shards):
     return pl.pallas_call(
         gather_kernel,
         out_shape=[jax.ShapeDtypeStruct((SLOTS, 256), F32)]
         + [jax.ShapeDtypeStruct((OWN, 256), BF16)] * 3,
-        in_specs=[smem()] + [vmem()] * (2 + len(shards)),
+        in_specs=[vmem()] * (2 + len(shards)),
         out_specs=[vmem()] * 4,
         scratch_shapes=[
             pltpu.VMEM((5, 4, 128, 128), F32),
@@ -104,17 +113,19 @@
         compiler_params=params(16),
         cost_estimate=cost(1.5),
         name="gather_first",
-    )(base, keys, weights, *shards)
+    )(keys, weights, *shards)
 
 
 CHUNKS = 8
 
 
-def hold_kernel(blocks_ref, after_ref, held_ref, sems):
-    step = JB // CHUNKS
+def hold_kernel(start, blocks_ref, after_ref, held_ref, sems):
+    step = held_ref.shape[0] // CHUNKS
     copies = [
         pltpu.make_async_copy(
-            blocks_ref.at[pl.ds(c * step, step)], held_ref.at[pl.ds(c * step, step)], sems.at[c]
+            blocks_ref.at[pl.ds(start + c * step, step)],
+            held_ref.at[pl.ds(c * step, step)],
+            sems.at[c],
         )
         for c in range(CHUNKS)
     ]
@@ -124,22 +135,20 @@
         copy.wait()
 
 
-def hold(blocks, after):
-    return pl.pallas_call(
-        hold_kernel,
-        out_shape=jax.ShapeDtypeStruct((JB, KS * 64, TB), BF16),
+def hold(blocks, after, start=0, count=JB):
+    return pl.pallas_call(
+        functools.partial(hold_kernel, start),
+        out_shape=jax.ShapeDtypeStruct((count, KS * 64, TB), BF16),
         in_specs=[pl.BlockSpec(memory_space=pl.ANY), pl.BlockSpec(memory_space=pl.ANY)],
         out_specs=vmem(),
         scratch_shapes=[pltpu.SemaphoreType.DMA((CHUNKS,))],
         compiler_params=params(46),
-        cost_estimate=cost(2.5),
+        cost_estimate=cost(2.5 * count / JB),
         name="hold_blocks",
     )(blocks, after)
 
 
 def project_kernel(
-    base_ref,
-    slab_ref,
     keys_ref,
     weights_ref,
     before_ref,
@@ -159,7 +168,7 @@
     keys, weights = keys_ref[...], weights_ref[...]
     for i, refs in enumerate(((three_ref,), (minus_ref,), (half_a_ref, half_b_ref))):
         planes_to_rows(refs, rows.at[i], shard.at[i])
-        acc = add_gathered(acc, keys, weights, base_ref[5 + i], shard[i])
+        acc = add_gathered(acc, keys, weights, owner_base(STEPS[5 + i]), shard[i])
     low = lower_half(JB)
     for m in range(2):
         cols = slice(128 * m, 128 * m + 128)
@@ -179,16 +188,17 @@
         both = jnp.concatenate([held[2 * p], held[2 * p + 1]], axis=1)
         got = jnp.dot(left, both, preferred_element_type=F32)
         total[8 * p : 8 * p + 8, :] = jnp.where(upper, got[:, :TB], got[:, TB:])
-    mine = pl.ds(pl.multiple_of(slab_ref[0] * 8, 8), 8)
-    total[mine, :] = total[mine, :] - measured_ref[...]
+    mine = pl.ds(pl.multiple_of(lax.axis_index("slab") * 8, 8), 8)
+    own = jnp.concatenate([measured_ref[0].astype(F32), measured_ref[1].astype(F32)], axis=0)
+    total[mine, :] = total[mine, :] - own
     out_ref[...] = total[...].astype(BF16)
 
 
-def project(base, slab, keys, weights, before, rest, measured, held):
+def project(keys, weights, before, rest, measured, held):
     return pl.pallas_call(
         project_kernel,
         out_shape=jax.ShapeDtypeStruct((JB * NB, TB), BF16),
-        in_specs=[smem(), smem()] + [vmem()] * 9,
+        in_specs=[vmem()] * 9,
         out_specs=vmem(),
         scratch_shapes=[
             pltpu.VMEM((3, 4, 128, 128), F32),
@@ -199,12 +209,64 @@
         compiler_params=params(16),
         cost_estimate=cost(4.0),
         name="project",
-    )(base, slab, keys, weights, before, *rest, measured, held)
+    )(keys, weights, before, *rest, measured, held)
+
+
+def plan_kernel(ids_ref, weights_ref, choice_ref, places_ref):
+    sensor = lax.axis_index("sensor")
+    ids = jnp.broadcast_to(ids_ref[...], (8, SLOTS))
+    live = jnp.broadcast_to(weights_ref[...], (8, SLOTS)) > 0.0
+    step = lax.broadcasted_iota(I32, (8, SLOTS), 0)
+    owner = lax.rem(sensor + step, 8)
+    x = (ids >> 6) - 4 * owner + 1
+    needed = live & (x >= 0) & (x < 6)
+    place = (ids & 7) * 48 + x * 8 + ((ids >> 3) & 7)
+    flags = jnp.where(needed, 1.0, 0.0)
+    row = lax.broadcasted_iota(I32, (SLOTS, SLOTS), 0)
+    column = lax.broadcasted_iota(I32, (SLOTS, SLOTS), 1)
+    before = jnp.where(row < column, 1.0, 0.0).astype(BF16)
+    rank = jnp.dot(flags.astype(BF16), before, preferred_element_type=F32)
+    high = (place >> 4).astype(F32)
+    low = (place & 15).astype(F32)
+    most = jnp.max(jnp.sum(flags, axis=1, keepdims=True), axis=0, keepdims=True)
+    over = jnp.where(most > CAP, 1.0, 0.0)
+    want = lax.broadcasted_iota(I32, (CAP, SLOTS), 0).astype(F32)
+    fill = jnp.zeros((4, SLOTS), F32)
+    for d in range(8):
+        at = slice(d, d + 1)
+        rank_d = jnp.where(flags[at] > 0.0, rank[at], -1.0)
+        hot = jnp.where(want == rank_d, 1.0, 0.0).astype(BF16)
+        choice_ref[d * CAP : (d + 1) * CAP, :] = hot
+        values = jnp.concatenate([high[at], low[at], flags[at], flags[at], fill], axis=0)
+        coded = lax.dot_general(
+            values.astype(BF16), hot, (((1,), (1,)), ((), ())), preferred_element_type=F32
+        )
+        coded = jnp.concatenate([coded, jnp.zeros((8, CAP), F32) + over], axis=0)
+        wide = jnp.concatenate([coded, jnp.zeros((16, 128 - CAP), F32)], axis=1)
+        wide = jnp.concatenate([wide, jnp.zeros((16, 128), F32)], axis=1)
+        places_ref[d] = wide.astype(BF16)
+
+
+def plan(ids, weights):
+    return pl.pallas_call(
+        plan_kernel,
+        out_shape=[
+            jax.ShapeDtypeStruct((8 * CAP, SLOTS), BF16),
+            jax.ShapeDtypeStruct((8, 16, 256), BF16),
+        ],
+        in_specs=[vmem()] * 2,
+        out_specs=[vmem()] * 2,
+        compiler_params=params(16),
+        cost_estimate=cost(1.5),
+        name="plan_sends",
+    )(ids, weights)
 
 
 def adjoint_kernel(
-    own_ref, one_ref, two_ref, three_ref, weights_ref, ids_ref, held, out_ref, resid, back
+    own_ref, one_ref, two_ref, three_ref, weights_ref, ids_ref, choice_ref, places_ref, held,
+    out_ref, *refs,
 ):
+    packed_refs, (resid, back) = refs[:8], refs[8:]
     back[2] = jnp.zeros((JB * NB, 128), F32)
     total = own_ref[...].astype(F32) + one_ref[...].astype(F32)
     total = total + two_ref[...].astype(F32) + three_ref[...].astype(F32)
@@ -231,14 +293,20 @@
                     scaled = part * weights_ref[k * JB : (k + 1) * JB, :]
                     out_ref[k * JB : (k + 1) * JB, 128 * m : 128 * m + 128] = scaled.astype(BF16)
     out_ref[SLOTS:SENT, :] = ids_ref[...]
-
-
-def adjoint(parts, weights, id_rows, held):
+    rows = out_ref[0:SLOTS, :]
+    packed = jnp.dot(choice_ref[...], rows, preferred_element_type=F32).astype(BF16)
+    for d, packed_ref in enumerate(packed_refs):
+        packed_ref[0:CAP, :] = packed[d * CAP : (d + 1) * CAP]
+        packed_ref[CAP:PACKED, :] = places_ref[d]
+
+
+def adjoint(parts, weights, id_rows, choice, places, held):
     return pl.pallas_call(
         adjoint_kernel,
-        out_shape=jax.ShapeDtypeStruct((SENT, 256), BF16),
-        in_specs=[vmem()] * 7,
-        out_specs=vmem(),
+        out_shape=[jax.ShapeDtypeStruct((SENT, 256), BF16)]
+        + [jax.ShapeDtypeStruct((PACKED, 256), BF16)] * 8,
+        in_specs=[vmem()] * 9,
+        out_specs=[vmem()] * 9,
         scratch_shapes=[
             pltpu.VMEM((JB * NB, TB), F32),
             pltpu.VMEM((3, JB * NB, 128), F32),
@@ -246,7 +314,7 @@
         compiler_params=params(16),
         cost_estimate=cost(3.0),
         name="adjoint",
-    )(*parts, weights, id_rows, held)
+    )(*parts, weights, id_rows, choice, places, held)
 
 
 def rows_to_planes(rows, out_ref):
@@ -268,9 +336,9 @@
 
 
 def images_kernel(
-    pos_ref, own_ref, plus_ref, minus_ref, planes_ref, low_ref, high_ref, rows
+    own_ref, plus_ref, minus_ref, planes_ref, low_ref, high_ref, rows
 ):
-    sensor, last = pos_ref[0], pos_ref[1]
+    sensor, last = lax.axis_index("sensor"), 7
     keep_low = jnp.where(sensor > 0, 1.0, 0.0).astype(F32)
     keep_high = jnp.where(sensor < last, 1.0, 0.0).astype(F32)
     for h in range(8):
@@ -283,7 +351,7 @@
     edge_rows(planes_ref, high_ref, 7)
 
 
-def images(pos, shards):
+def images(shards):
     return pl.pallas_call(
         images_kernel,
         out_shape=[
@@ -291,19 +359,19 @@
             jax.ShapeDtypeStruct((24, 512), F32),
             jax.ShapeDtypeStruct((24, 512), F32),
         ],
-        in_specs=[smem()] + [vmem()] * len(shards),
+        in_specs=[vmem()] * len(shards),
         out_specs=[vmem()] * 3,
         scratch_shapes=[pltpu.VMEM((384, 256), F32)],
         compiler_params=params(16),
         cost_estimate=cost(0.7),
         name="images_to_planes",
-    )(pos, *shards)
-
-
-def add_scattered(acc, sensor, contrib):
+    )(*shards)
+
+
+def add_scattered(acc, contrib):
     coded = contrib[SLOTS:SENT, :].astype(F32)
     ids = (coded[0:2] * 16.0 + coded[2:4]).astype(I32)
-    x = (ids >> 6) - 4 * sensor + 1
+    x = (ids >> 6) - 4 * lax.axis_index("sensor") + 1
     index = (ids & 7) * 48 + x * 8 + ((ids >> 3) & 7)
     index = jnp.where((x >= 0) & (x < 6), index, -1)
     first = lax.broadcasted_iota(I32, (384, 256), 0)
@@ -314,79 +382,84 @@
     return acc + jnp.dot(more, contrib[256:SLOTS, :], preferred_element_type=F32)
 
 
-def scatter_kernel(pos_ref, *refs):
-    contribs, out_ref = refs[:-1], refs[-1]
-    acc = jnp.zeros((384, 256), F32)
-    for contrib in contribs:
-        acc = add_scattered(acc, pos_ref[0], contrib)
-    out_ref[...] = acc
-
-
-def scatter_first(pos, contribs):
-    return pl.pallas_call(
-        scatter_kernel,
-        out_shape=jax.ShapeDtypeStruct((384, 256), F32),
-        in_specs=[smem()] + [vmem()] * len(contribs),
-        out_specs=vmem(),
-        compiler_params=params(16),
-        cost_estimate=cost(0.7),
-        name="scatter_first",
-    )(pos, *contribs)
-
-
-def gradient_kernel(
-    pos_ref,
-    before_ref,
-    three_ref,
-    minus_ref,
-    half_a_ref,
-    half_b_ref,
-    image_low_ref,
-    image_high_ref,
-    planes_ref,
-    inner_ref,
-    outer_ref,
-    far,
-    rows,
-    low,
-    high,
-):
-    far[0:SENT_SPLIT, :] = half_a_ref[...]
-    far[SENT_SPLIT:SENT, :] = half_b_ref[...]
-    acc = before_ref[...]
-    for contrib in (three_ref, minus_ref, far):
-        acc = add_scattered(acc, pos_ref[0], contrib)
+def write_planes(acc, image_low_ref, image_high_ref, planes_ref, inner_ref, outer_ref, rows, low, high):
     rows[...] = acc
     rows_to_planes(rows, planes_ref)
     low[0:24, :] = image_low_ref[...]
     high[0:24, :] = image_high_ref[...]
     edge_rows(planes_ref, low.at[pl.ds(24, 24)], 0)
     edge_rows(planes_ref, high.at[pl.ds(24, 24)], 7)
-    first_core = pos_ref[2] == 0
+    first_core = lax.rem(lax.axis_index("slab"), 2) == 0
     inner_ref[...] = jnp.where(first_core, high[...], low[...]).astype(BF16)
     outer_ref[...] = jnp.where(first_core, low[...], high[...]).astype(BF16)
 
 
-def gradient_planes(pos, before, rest, image_low, image_high):
-    return pl.pallas_call(
-        gradient_kernel,
-        out_shape=[
-            jax.ShapeDtypeStruct((NB, 4, 48, 128), F32),
-            jax.ShapeDtypeStruct((48, 512), BF16),
-            jax.ShapeDtypeStruct((48, 512), BF16),
-        ],
-        in_specs=[smem()] + [vmem()] * 7,
+PLANES = [
+    jax.ShapeDtypeStruct((NB, 4, 48, 128), F32),
+    jax.ShapeDtypeStruct((48, 512), BF16),
+    jax.ShapeDtypeStruct((48, 512), BF16),
+]
+PLANE_SCRATCH = [
+    pltpu.VMEM((384, 256), F32),
+    pltpu.VMEM((48, 512), F32),
+    pltpu.VMEM((48, 512), F32),
+]
+
+
+def packed_kernel(*refs):
+    packed, (low_in, high_in, planes_ref, inner_ref, outer_ref, over_ref) = refs[:8], refs[8:14]
+    acc = jnp.zeros((384, 256), F32)
+    row = lax.broadcasted_iota(I32, (384, CAP), 0)
+    over = jnp.zeros((8, 256), F32)
+    for ref in packed:
+        coded = ref[CAP:PACKED, :].astype(F32)
+        over = jnp.maximum(over, coded[8:16])
+        place = (coded[0:1] * 16.0 + coded[1:2]).astype(I32)
+        place = jnp.where(coded[2:3] > 0.0, place, -1)[:, 0:CAP]
+        hot = jnp.where(row == place, 1.0, 0.0).astype(BF16)
+        acc = acc + jnp.dot(hot, ref[0:CAP, :], preferred_element_type=F32)
+    over_ref[...] = over[0:1, 0:1].astype(I32)
+    write_planes(acc, low_in, high_in, planes_ref, inner_ref, outer_ref, *refs[14:])
+
+
+def packed_planes(packed, image_low, image_high):
+    return pl.pallas_call(
+        packed_kernel,
+        out_shape=[*PLANES, jax.ShapeDtypeStruct((1, 1), I32)],
+        in_specs=[vmem()] * 10,
+        out_specs=[vmem()] * 4,
+        scratch_shapes=PLANE_SCRATCH,
+        compiler_params=params(16),
+        cost_estimate=cost(1.5),
+        name="gradient_planes",
+    )(*packed, image_low, image_high)
+
+
+def whole_kernel(*refs):
+    whole, (half_a_ref, half_b_ref, low_in, high_in) = refs[:7], refs[7:11]
+    (planes_ref, inner_ref, outer_ref), far, scratch = refs[11:14], refs[14], refs[15:]
+    far[0:SENT_SPLIT, :] = half_a_ref[...]
+    far[SENT_SPLIT:SENT, :] = half_b_ref[...]
+    acc = jnp.zeros((384, 256), F32)
+    for contrib in (*whole, far):
+        acc = add_scattered(acc, contrib)
+    write_planes(acc, low_in, high_in, planes_ref, inner_ref, outer_ref, *scratch)
+
+
+def whole_planes(contrib, image_low, image_high):
+    two, back = from_sensor(contrib, 2), from_sensor(contrib, -2)
+    near = [contrib, from_sensor(contrib, 1), from_sensor(contrib, -1), two, back]
+    far = spread_far(two, back, SENT_SPLIT)
+    return pl.pallas_call(
+        whole_kernel,
+        out_shape=PLANES,
+        in_specs=[vmem()] * 11,
         out_specs=[vmem()] * 3,
-        scratch_shapes=[
-            pltpu.VMEM((SENT, 256), BF16),
-            pltpu.VMEM((384, 256), F32),
-            pltpu.VMEM((48, 512), F32),
-            pltpu.VMEM((48, 512), F32),
-        ],
+        scratch_shapes=[pltpu.VMEM((SENT, 256), BF16), *PLANE_SCRATCH],
         compiler_params=params(16),
-        cost_estimate=cost(1.0),
-        name="gradient_planes",
-    )(pos, before, *rest, image_low, image_high)
+        cost_estimate=cost(2.0),
+        name="gradient_planes_whole",
+    )(*near, *far, image_low, image_high)
 
 
 def shifted_rows(rows, e):
@@ -399,10 +472,10 @@
 
 
 def conv_kernel(
-    pos_ref, image_ref, grad_ref, inner_ref, outer_ref, matrix_ref, out_w_ref, out_ref,
+    image_ref, grad_ref, inner_ref, outer_ref, matrix_ref, out_w_ref, out_ref,
     body, ends, done,
 ):
-    first_core = pos_ref[2] == 0
+    first_core = lax.rem(lax.axis_index("slab"), 2) == 0
     inner, outer = inner_ref[...].astype(F32), outer_ref[...].astype(F32)
     below, above = jnp.where(first_core, outer, inner), jnp.where(first_core, inner, outer)
     for kind, (edge, start) in enumerate(((below, 0), (above, 0), (below, 24), (above, 24))):
@@ -455,11 +528,11 @@
     lax.fori_loop(0, 4, one_x, 0)
 
 
-def convolve(pos, image, grad, inner, outer, matrix, out_w):
+def convolve(image, grad, inner, outer, matrix, out_w):
     return pl.pallas_call(
         conv_kernel,
         out_shape=jax.ShapeDtypeStruct((4, 8, NB, 512), F32),
-        in_specs=[smem()] + [vmem()] * 5 + [smem()],
+        in_specs=[vmem()] * 5 + [smem()],
         out_specs=vmem(),
         scratch_shapes=[
             pltpu.VMEM((3, 24, 16, 512), BF16),
@@ -469,7 +542,7 @@
         compiler_params=params(32),
         cost_estimate=cost(5.0),
         name="convolutions",
-    )(pos, image, grad, inner, outer, matrix, out_w)
+    )(image, grad, inner, outer, matrix, out_w)
 
 
 def tap_choice():
@@ -549,11 +622,6 @@
 
 
 def on_device(volume, measured, blocks, voxel_ids, counts, exponents, conv_in, conv_bias, conv_out):
-    sensor = lax.axis_index("sensor").astype(I32)
-    slab = lax.axis_index("slab").astype(I32)
-    steps = jnp.array([0, -1, 1, -2, 2, -3, 3, 4], I32)
-    base = ((sensor + steps) % 8) * OWN
-    pos = jnp.stack([sensor, jnp.full_like(sensor, 7), slab % 2])
     ids = voxel_ids.T.reshape(SLOTS)
     padded = jnp.pad(ids, (0, 512 - SLOTS), constant_values=4080).reshape(2, 256)
     id_rows = jnp.concatenate([padded >> 4, padded & 15, jnp.zeros((12, 256), I32)], axis=0)
@@ -566,26 +634,29 @@
     two, back = from_sensor(volume, 2), from_sensor(volume, -2)
     far = spread_far(two, back, 2)
     held = hold(stacked, two)
-    before, *near = gather_first(base, keys, weights, [volume, plus, minus, two, back])
+    before, *near = gather_first(keys, weights, [volume, plus, minus, two, back])
     partial = project(
-        base, slab.reshape(1), keys, weights, before, far,
-        measured.reshape(8, TB).astype(F32), held,
+        keys, weights, before, far, measured, held
     )
     chip = chip_sum(partial)
     held = hold(stacked, chip)
     parts = slab_sum_parts(chip)
     matrix = conv_matrix(conv_in, conv_bias)
-    image, image_low, image_high = images(pos, near)
-    contrib = adjoint(parts, weights, id_rows.astype(BF16), held)
-    two_c, back_c = from_sensor(contrib, 2), from_sensor(contrib, -2)
-    near_c = [contrib, from_sensor(contrib, 1), from_sensor(contrib, -1)]
-    far_c = spread_far(two_c, back_c, SENT_SPLIT)
-    sums = scatter_first(pos, [*near_c, two_c, back_c])
-    grad, inner, outer = gradient_planes(pos, sums, far_c, image_low, image_high)
+    image, image_low, image_high = images(near)
+    live_row = weights.reshape(1, SLOTS)
+    choice, places = plan(ids.reshape(1, SLOTS), live_row)
+    contrib, *packed = adjoint(parts, weights, id_rows.astype(BF16), choice, places, held)
+    moved = [packed[0]] + [from_sensor(packed[d % 8], d) for d in (4, 3, -3, 2, -2, 1, -1)]
+    grad, inner, outer, over = packed_planes(moved, image_low, image_high)
+    grad, inner, outer = lax.cond(
+        over[0, 0] > 0,
+        lambda: tuple(whole_planes(contrib, image_low, image_high)),
+        lambda: (grad, inner, outer),
+    )
     inner = lax.ppermute(inner, "slab", slab_perm(0, 0, 1))
     pairs = [(2 * i + 1, 2 * i + 2) for i in range(15)]
     outer = lax.ppermute(outer, "slab", pairs + [(b, a) for a, b in pairs])
-    return convolve(pos, image, grad, inner, outer, matrix, conv_out)
+    return convolve(image, grad, inner, outer, matrix, conv_out)
 
 
 def solution(mesh):

time: 86.6 us -> 82.4 us (0.952); the launches traced: 84.9 us -> 82.2 us
  waiting for transfers between devices: 16.5 us -> 11.3 us
  starting transfers between devices: 45.7 us -> 50.7 us
  Pallas kernels: 18.1 us -> 16 us
  other arithmetic: 3.04 us -> 1.61 us
    ppermute x16 -> x15, waiting for transfers between devices: 8.48 us -> 2.53 us  [from_sensor(): return lax.ppermute(block, 'sensor', ring(distance, 8))]
    ppermute x16 -> x15, starting transfers between devices: 26.8 us -> 32.5 us  [from_sensor(): return lax.ppermute(block, 'sensor', ring(distance, 8))]
    ppermute x1, waiting for transfers between devices: 3.16 us -> 4.08 us  [on_device(): outer = lax.ppermute(outer, 'slab', pairs + [(b, a) for a, b in pairs])]
    ppermute x1, starting transfers between devices: 3.89 us -> 2.97 us  [on_device(): outer = lax.ppermute(outer, 'slab', pairs + [(b, a) for a, b in pairs])]
  transfers between devices with their start and end apart: 25 -> 24, of which waited for: 10 -> 9; matrix products, arithmetic and copies ran while one was open for 5% -> 4% of each run, Pallas kernels for 10% -> 8%
where the time goes in v2:
time: 82.4 us; the launch traced here: 82.2 us
  starting transfers between devices  50.7 us (62%)
  Pallas kernels  16 us (19%)
  waiting for transfers between devices  11.3 us (14%)
  other arithmetic  1.61 us (2%)
  local copies, waits for them, and re-layouts  1.23 us (1%)
  between operations  0.95 us (1%)
    ppermute x15, starting transfers between devices, from_sensor(): return lax.ppermute(block, 'sensor', ring(distance, 8))  32.5 us
    ppermute x1, starting transfers between devices, on_device(): inner = lax.ppermute(inner, 'slab', slab_perm(0, 0, 1))  5.59 us
    pallas_call x2, Pallas kernels, hold(): pl.pallas_call(functools.partial(hold_kernel, start), out_shape=jax.Shape...  5.13 us
    pallas_call x1, Pallas kernels, convolve(): pl.pallas_call(conv_kernel, out_shape=jax.ShapeDtypeStruct((4, 8, NB, 512...  4.73 us
    ppermute x3, starting transfers between devices, slab_sum_parts(): lax.ppermute(row, 'slab', slab_perm(d, 0, 0))  4.46 us
    ppermute x1, waiting for transfers between devices, on_device(): outer = lax.ppermute(outer, 'slab', pairs + [(b, a) for a, b in pairs])  4.08 us
    ppermute x3, waiting for transfers between devices, slab_sum_parts(): moved = [lax.ppermute(total, 'slab', slab_perm(0, d, 0)) for d in (1, 3, 2)]  3.47 us
    ppermute x1, starting transfers between devices, on_device(): outer = lax.ppermute(outer, 'slab', pairs + [(b, a) for a, b in pairs])  2.97 us
  transfers between devices with their start and end apart: 24, of which 9 were waited for; matrix products, arithmetic and copies ran while one was open for 4% of the time, Pallas kernels for 8%

profile of v2, /device:TPU:7, one launch (start us, length us, event | category | flops | bytes accessed | tf_op | source)
XLA Modules:
  0.0 82.2 jit_solution(1507901672721975141)
XLA Ops:
  0.0 3.0 %collective-permute-start.10 = (bf16[4,8,4,512]{3,2,1,0:T(4,128)(2,1)}, bf16[4,8,4,512]{3,2,1,0:T(4,128)(2,1)S(1)}, u32[]{:S(2)}, u32[]{:S(2)}) collective-permute-start(bf16[4,8,4,512]{3,2,1,0:T(4,128)(2,1)} %own_ref.1), channel_id=1, source_target_pairs={{0,64},{32,96},{64,128},{96,160},{128,192},{160,224},{192,0},{224,... | collective-permute-start | bytes 393224 | tf_op jit(solution)/shard_map/ppermute | solution.py:593
  3.0 3.0 %collective-permute-start.11 = (bf16[4,8,4,512]{3,2,1,0:T(4,128)(2,1)}, bf16[4,8,4,512]{3,2,1,0:T(4,128)(2,1)S(1)}, u32[]{:S(2)}, u32[]{:S(2)}) collective-permute-start(bf16[4,8,4,512]{3,2,1,0:T(4,128)(2,1)} %own_ref.1), channel_id=1, source_target_pairs={{0,192},{32,224},{64,0},{96,32},{128,64},{160,96},{192,128},{224,1... | collective-permute-start | bytes 393224 | tf_op jit(solution)/shard_map/ppermute | solution.py:593
  6.0 0.7 collective-permute-start.8
  6.8 1.9 %collective-permute-start.9 = (bf16[4,8,4,512]{3,2,1,0:T(4,128)(2,1)}, bf16[4,8,4,512]{3,2,1,0:T(4,128)(2,1)S(1)}, u32[]{:S(2)}, u32[]{:S(2)}) collective-permute-start(bf16[4,8,4,512]{3,2,1,0:T(4,128)(2,1)} %own_ref.1), channel_id=1, source_target_pairs={{0,224},{32,0},{64,32},{96,64},{128,96},{160,128},{192,160},{224,1... | collective-permute-start | bytes 393224 | tf_op jit(solution)/shard_map/ppermute | solution.py:593
  10.1 3.0 %collective-permute-start.14 = (bf16[2,8,4,512]{3,2,1,0:T(4,128)(2,1)S(1)}, bf16[2,8,4,512]{3,2,1,0:T(4,128)(2,1)S(1)}, u32[]{:S(2)}, u32[]{:S(2)}) collective-permute-start(bf16[2,8,4,512]{3,2,1,0:T(4,128)(2,1)S(1)} %slice.16), channel_id=1, source_target_pairs={{0,64},{32,96},{64,128},{96,160},{128,192},{160,224},{192,0},{224,... | collective-permute-start | bytes 196616 | tf_op jit(solution)/shard_map/ppermute | solution.py:593
  13.8 2.4 %collective-permute-start.15 = (bf16[2,8,4,512]{3,2,1,0:T(4,128)(2,1)S(1)}, bf16[2,8,4,512]{3,2,1,0:T(4,128)(2,1)S(1)}, u32[]{:S(2)}, u32[]{:S(2)}) collective-permute-start(bf16[2,8,4,512]{3,2,1,0:T(4,128)(2,1)S(1)} %slice.17), channel_id=1, source_target_pairs={{0,192},{32,224},{64,0},{96,32},{128,64},{160,96},{192,128},{224,1... | collective-permute-start | bytes 196616 | tf_op jit(solution)/shard_map/ppermute | solution.py:593
  16.2 0.9 %collective-permute-start.12 = (bf16[4,8,4,512]{3,2,1,0:T(4,128)(2,1)S(1)}, bf16[4,8,4,512]{3,2,1,0:T(4,128)(2,1)S(1)}, u32[]{:S(2)}, u32[]{:S(2)}) collective-permute-start(bf16[4,8,4,512]{3,2,1,0:T(4,128)(2,1)S(1)} %collective-permute-done.10.two_ref.after_ref), channel_id=1, source_target_pairs={{0,32},{32,64},{64,96},{96,128},{128,160},{160,192},{192,224},{224... | collective-permute-start | bytes 393224 | tf_op jit(solution)/shard_map/ppermute | solution.py:593
  17.1 1.8 %collective-permute-start.13 = (bf16[4,8,4,512]{3,2,1,0:T(4,128)(2,1)S(1)}, bf16[4,8,4,512]{3,2,1,0:T(4,128)(2,1)S(1)}, u32[]{:S(2)}, u32[]{:S(2)}) collective-permute-start(bf16[4,8,4,512]{3,2,1,0:T(4,128)(2,1)S(1)} %collective-permute-done.11.back_ref), channel_id=1, source_target_pairs={{0,224},{32,0},{64,32},{96,64},{128,96},{160,128},{192,160},{224,1... | collective-permute-start | bytes 393224 | tf_op jit(solution)/shard_map/ppermute | solution.py:593
  19.9 2.6 %hold_blocks.2.held = bf16[64,320,128]{2,1,0:T(8,128)(2,1)S(1)} custom-call(bf16[64,320,128]{2,1,0:T(8,128)(2,1)} %bitcast.9, bf16[4,8,4,512]{3,2,1,0:T(4,128)(2,1)S(1)} %collective-permute-done.10.two_ref.after_ref), custom_call_target="tpu_custom_call" | custom-call | bytes 7500000 | tf_op jit(solution)/shard_map/hold_blocks/pallas_call | solution.py:139
  22.5 0.8 gather_first.1
  23.3 1.5 %project.1 = bf16[256,128]{1,0:T(8,128)(2,1)S(1)} custom-call(s32[320,1]{1,0:T(8,128)S(1)} %or.27.keys_ref, f32[320,1]{1,0:T(8,128)S(1)} %reshape.85.weights_ref, f32[320,256]{1,0:T(8,128)S(1)} %get-tuple-element.49.before_ref, bf16[4,8,4,512]{3,2,1,0:T(4,128)(2,1)S(1)} %collective-permute-done.12.three_ref, ...), custom_call_target="tpu_custom_call" | custom-call | bytes 12000000 | tf_op jit(solution)/shard_map/project/pallas_call | solution.py:198
  24.9 2.5 %collective-permute-start.16 = (bf16[256,128]{1,0:T(8,128)(2,1)S(1)}, bf16[256,128]{1,0:T(8,128)(2,1)S(1)}, u32[]{:S(2)}, u32[]{:S(2)}) collective-permute-start(bf16[256,128]{1,0:T(8,128)(2,1)S(1)} %project.1), channel_id=1, source_target_pairs={{0,1},{1,0},{2,3},{3,2},{4,5},{5,4},{6,7},{7,6},{8,9},{9,8},{10,11... | collective-permute-start | bytes 196616 | tf_op jit(solution)/shard_map/ppermute | solution.py:606
  27.4 0.8 %collective-permute-done.16 = bf16[256,128]{1,0:T(8,128)(2,1)S(1)} collective-permute-done((bf16[256,128]{1,0:T(8,128)(2,1)S(1)}, bf16[256,128]{1,0:T(8,128)(2,1)S(1)}, u32[]{:S(2)}, u32[]{:S(2)}) %collective-permute-start.16) | collective-permute-done | bytes 65568 | tf_op jit(solution)/shard_map/ppermute | solution.py:606
  28.6 1.3 %collective-permute-start.18 = (bf16[256,128]{1,0:T(8,128)(2,1)S(1)}, bf16[256,128]{1,0:T(8,128)(2,1)S(1)}, u32[]{:S(2)}, u32[]{:S(2)}) collective-permute-start(bf16[256,128]{1,0:T(8,128)(2,1)S(1)} %add_convert_fusion.1.after_ref), channel_id=1, source_target_pairs={{0,6},{1,7},{2,0},{3,1},{4,2},{5,3},{6,4},{7,5},{8,14},{9,15},{10,... | collective-permute-start | bytes 196616 | tf_op jit(solution)/shard_map/ppermute | solution.py:612
  29.8 1.1 %collective-permute-start.19 = (bf16[256,128]{1,0:T(8,128)(2,1)S(1)}, bf16[256,128]{1,0:T(8,128)(2,1)S(1)}, u32[]{:S(2)}, u32[]{:S(2)}) collective-permute-start(bf16[256,128]{1,0:T(8,128)(2,1)S(1)} %add_convert_fusion.1.after_ref), channel_id=1, source_target_pairs={{0,4},{1,5},{2,6},{3,7},{4,0},{5,1},{6,2},{7,3},{8,12},{9,13},{10,... | collective-permute-start | bytes 196616 | tf_op jit(solution)/shard_map/ppermute | solution.py:612
  31.5 1.4 %collective-permute-done.18 = bf16[256,128]{1,0:T(8,128)(2,1)S(1)} collective-permute-done((bf16[256,128]{1,0:T(8,128)(2,1)S(1)}, bf16[256,128]{1,0:T(8,128)(2,1)S(1)}, u32[]{:S(2)}, u32[]{:S(2)}) %collective-permute-start.18) | collective-permute-done | bytes 65568 | tf_op jit(solution)/shard_map/ppermute | solution.py:612
  32.9 1.7 %collective-permute-done.19 = bf16[256,128]{1,0:T(8,128)(2,1)S(1)} collective-permute-done((bf16[256,128]{1,0:T(8,128)(2,1)S(1)}, bf16[256,128]{1,0:T(8,128)(2,1)S(1)}, u32[]{:S(2)}, u32[]{:S(2)}) %collective-permute-start.19) | collective-permute-done | bytes 65568 | tf_op jit(solution)/shard_map/ppermute | solution.py:612
  34.6 1.4 %collective-permute-start.20 = (bf16[256,128]{1,0:T(8,128)(2,1)S(1)}, bf16[256,128]{1,0:T(8,128)(2,1)S(1)}, u32[]{:S(2)}, u32[]{:S(2)}) collective-permute-start(bf16[256,128]{1,0:T(8,128)(2,1)S(1)} %add_convert_fusion.own_ref), channel_id=1, source_target_pairs={{0,8},{1,9},{2,10},{3,11},{4,12},{5,13},{6,14},{7,15},{8,16},{9,17... | collective-permute-start | bytes 196616 | tf_op jit(solution)/shard_map/ppermute | solution.py:615
  36.0 1.7 %collective-permute-start.21 = (bf16[256,128]{1,0:T(8,128)(2,1)S(1)}, bf16[256,128]{1,0:T(8,128)(2,1)S(1)}, u32[]{:S(2)}, u32[]{:S(2)}) collective-permute-start(bf16[256,128]{1,0:T(8,128)(2,1)S(1)} %add_convert_fusion.own_ref), channel_id=1, source_target_pairs={{0,24},{1,25},{2,26},{3,27},{4,28},{5,29},{6,30},{7,31},{8,0},{9,1... | collective-permute-start | bytes 196616 | tf_op jit(solution)/shard_map/ppermute | solution.py:615
  37.7 1.4 %collective-permute-start.22 = (bf16[256,128]{1,0:T(8,128)(2,1)S(1)}, bf16[256,128]{1,0:T(8,128)(2,1)S(1)}, u32[]{:S(2)}, u32[]{:S(2)}) collective-permute-start(bf16[256,128]{1,0:T(8,128)(2,1)S(1)} %add_convert_fusion.own_ref), channel_id=1, source_target_pairs={{0,16},{1,17},{2,18},{3,19},{4,20},{5,21},{6,22},{7,23},{8,24},{9,... | collective-permute-start | bytes 196616 | tf_op jit(solution)/shard_map/ppermute | solution.py:615
  39.7 2.6 %hold_blocks.3.held = bf16[64,320,128]{2,1,0:T(8,128)(2,1)S(1)} custom-call(bf16[64,320,128]{2,1,0:T(8,128)(2,1)} %bitcast.10, bf16[256,128]{1,0:T(8,128)(2,1)S(1)} %add_convert_fusion.1.after_ref), custom_call_target="tpu_custom_call" | custom-call | bytes 7500000 | tf_op jit(solution)/shard_map/hold_blocks/pallas_call | solution.py:139
  42.8 2.2 %adjoint.1 = (bf16[336,256]{1,0:T(8,128)(2,1)S(1)}, bf16[96,256]{1,0:T(8,128)(2,1)S(1)}, bf16[96,256]{1,0:T(8,128)(2,1)S(1)}, bf16[96,256]{1,0:T(8,128)(2,1)S(1)...) custom-call(bf16[256,128]{1,0:T(8,128)(2,1)S(1)} %add_convert_fusion, ...), custom_call_target="tpu_custom_call" | custom-call | bytes 9000000 | tf_op jit(solution)/shard_map/adjoint/pallas_call | solution.py:304
  44.9 5.0 %collective-permute-start.23 = (bf16[96,256]{1,0:T(8,128)(2,1)S(1)}, bf16[96,256]{1,0:T(8,128)(2,1)S(1)}, u32[]{:S(2)}, u32[]{:S(2)}) collective-permute-start(bf16[96,256]{1,0:T(8,128)(2,1)S(1)} %get-tuple-element.53), channel_id=1, source_target_pairs={{0,128},{32,160},{64,192},{96,224},{128,0},{160,32},{192,64},{224,... | collective-permute-start | bytes 147464 | tf_op jit(solution)/shard_map/ppermute | solution.py:593
  50.2 4.5 %collective-permute-start.25 = (bf16[96,256]{1,0:T(8,128)(2,1)S(1)}, bf16[96,256]{1,0:T(8,128)(2,1)S(1)}, u32[]{:S(2)}, u32[]{:S(2)}) collective-permute-start(bf16[96,256]{1,0:T(8,128)(2,1)S(1)} %get-tuple-element.55), channel_id=1, source_target_pairs={{0,160},{32,192},{64,224},{96,0},{128,32},{160,64},{192,96},{224,1... | collective-permute-start | bytes 147464 | tf_op jit(solution)/shard_map/ppermute | solution.py:593
  54.7 3.6 %collective-permute-start.27 = (bf16[96,256]{1,0:T(8,128)(2,1)S(1)}, bf16[96,256]{1,0:T(8,128)(2,1)S(1)}, u32[]{:S(2)}, u32[]{:S(2)}) collective-permute-start(bf16[96,256]{1,0:T(8,128)(2,1)S(1)} %get-tuple-element.57), channel_id=1, source_target_pairs={{0,192},{32,224},{64,0},{96,32},{128,64},{160,96},{192,128},{224,1... | collective-permute-start | bytes 147464 | tf_op jit(solution)/shard_map/ppermute | solution.py:593
  58.2 2.7 %collective-permute-start.29 = (bf16[96,256]{1,0:T(8,128)(2,1)S(1)}, bf16[96,256]{1,0:T(8,128)(2,1)S(1)}, u32[]{:S(2)}, u32[]{:S(2)}) collective-permute-start(bf16[96,256]{1,0:T(8,128)(2,1)S(1)} %get-tuple-element.59), channel_id=1, source_target_pairs={{0,224},{32,0},{64,32},{96,64},{128,96},{160,128},{192,160},{224,1... | collective-permute-start | bytes 147464 | tf_op jit(solution)/shard_map/ppermute | solution.py:593
  61.2 1.2 %collective-permute-done.28.refs_6_ = bf16[96,256]{1,0:T(8,128)(2,1)S(1)} collective-permute-done((bf16[96,256]{1,0:T(8,128)(2,1)S(1)}, bf16[96,256]{1,0:T(8,128)(2,1)S(1)}, u32[]{:S(2)}, u32[]{:S(2)}) %collective-permute-start.28) | collective-permute-done | bytes 49184 | tf_op jit(solution)/shard_map/ppermute | solution.py:593
  62.4 1.1 %gradient_planes.1 = (f32[4,4,48,128]{3,2,1,0:T(8,128)S(1)}, bf16[48,512]{1,0:T(8,128)(2,1)S(1)}, bf16[48,512]{1,0:T(8,128)(2,1)S(1)}, s32[1,1]{1,0:T(1,128)}) custom-call(bf16[96,256]{1,0:T(8,128)(2,1)S(1)} %get-tuple-element.52.refs_0_, bf16[96,256]{1,0:T(8,128)(2,1)S(1)} %collective-permute-done.23.refs_1_, ...), custom_call_target="tpu_custom_call" | custom-call | bytes 4500000 | tf_op jit(solution)/shard_map/gradient_planes/pallas_call | solution.py:426
  64.4 5.6 %collective-permute-start.30 = (bf16[48,512]{1,0:T(8,128)(2,1)S(1)}, bf16[48,512]{1,0:T(8,128)(2,1)S(1)}, u32[]{:S(2)}, u32[]{:S(2)}) collective-permute-start(bf16[48,512]{1,0:T(8,128)(2,1)S(1)} %get-tuple-element.68), channel_id=1, source_target_pairs={{0,1},{1,0},{2,3},{3,2},{4,5},{5,4},{6,7},{7,6},{8,9},{9,8},{10,11... | collective-permute-start | bytes 147464 | tf_op jit(solution)/shard_map/ppermute | solution.py:656
  70.0 3.0 %collective-permute-start.31 = (bf16[48,512]{1,0:T(8,128)(2,1)S(1)}, bf16[48,512]{1,0:T(8,128)(2,1)S(1)}, u32[]{:S(2)}, u32[]{:S(2)}) collective-permute-start(bf16[48,512]{1,0:T(8,128)(2,1)S(1)} %get-tuple-element.69), channel_id=1, source_target_pairs={{1,2},{3,4},{5,6},{7,8},{9,10},{11,12},{13,14},{15,16},{17,18},{19... | collective-permute-start | bytes 147464 | tf_op jit(solution)/shard_map/ppermute | solution.py:658
  73.4 4.1 %collective-permute-done.31.outer_ref = bf16[48,512]{1,0:T(8,128)(2,1)S(1)} collective-permute-done((bf16[48,512]{1,0:T(8,128)(2,1)S(1)}, bf16[48,512]{1,0:T(8,128)(2,1)S(1)}, u32[]{:S(2)}, u32[]{:S(2)}) %collective-permute-start.31) | collective-permute-done | bytes 49184 | tf_op jit(solution)/shard_map/ppermute | solution.py:658
  77.5 4.7 %convolutions.1 = f32[4,8,4,512]{3,2,1,0:T(4,128)} custom-call(f32[4,4,48,128]{3,2,1,0:T(8,128)S(1)} %get-tuple-element.48.image_ref, f32[4,4,48,128]{3,2,1,0:T(8,128)S(1)} %get-tuple-element.67.grad_ref, bf16[48,512]{1,0:T(8,128)(2,1)S(1)} %collective-permute-done.30.inner_ref, bf16[48,512]{1,0:T(8,128)(2,1)S(1)} %collective-permute-done.31.outer_ref, ...), custom_call_target="tpu_custom_call" | custom-call | bytes 15000000 | tf_op jit(solution)/shard_map/convolutions/pallas_call | solution.py:532
  (63 shorter events, 6.3 us)
Async XLA Ops:
  0.0 10.0 %collective-permute-start.10 = (bf16[4,8,4,512]{3,2,1,0:T(4,128)(2,1)}, bf16[4,8,4,512]{3,2,1,0:T(4,128)(2,1)S(1)}, u32[]{:S(2)}, u32[]{:S(2)}) collective-permute-start(bf16[4,8,4,512]{3,2,1,0:T(4,128)(2,1)} %own_ref.1), channel_id=1, source_target_pairs={{0,64},{32,96},{64,128},{96,160},{128,192},{160,224},{192,0},{224,... | collective-permute-start | bytes 393224 | tf_op jit(solution)/shard_map/ppermute | solution.py:593
  3.0 10.8 %collective-permute-start.11 = (bf16[4,8,4,512]{3,2,1,0:T(4,128)(2,1)}, bf16[4,8,4,512]{3,2,1,0:T(4,128)(2,1)S(1)}, u32[]{:S(2)}, u32[]{:S(2)}) collective-permute-start(bf16[4,8,4,512]{3,2,1,0:T(4,128)(2,1)} %own_ref.1), channel_id=1, source_target_pairs={{0,192},{32,224},{64,0},{96,32},{128,64},{160,96},{192,128},{224,1... | collective-permute-start | bytes 393224 | tf_op jit(solution)/shard_map/ppermute | solution.py:593
  6.0 11.1 %collective-permute-start.8 = (bf16[4,8,4,512]{3,2,1,0:T(4,128)(2,1)}, bf16[4,8,4,512]{3,2,1,0:T(4,128)(2,1)S(1)}, u32[]{:S(2)}, u32[]{:S(2)}) collective-permute-start(bf16[4,8,4,512]{3,2,1,0:T(4,128)(2,1)} %own_ref.1), channel_id=1, source_target_pairs={{0,32},{32,64},{64,96},{96,128},{128,160},{160,192},{192,224},{224... | collective-permute-start | bytes 393224 | tf_op jit(solution)/shard_map/ppermute | solution.py:593
  6.8 15.7 %collective-permute-start.9 = (bf16[4,8,4,512]{3,2,1,0:T(4,128)(2,1)}, bf16[4,8,4,512]{3,2,1,0:T(4,128)(2,1)S(1)}, u32[]{:S(2)}, u32[]{:S(2)}) collective-permute-start(bf16[4,8,4,512]{3,2,1,0:T(4,128)(2,1)} %own_ref.1), channel_id=1, source_target_pairs={{0,224},{32,0},{64,32},{96,64},{128,96},{160,128},{192,160},{224,1... | collective-permute-start | bytes 393224 | tf_op jit(solution)/shard_map/ppermute | solution.py:593
  10.1 13.2 %collective-permute-start.14 = (bf16[2,8,4,512]{3,2,1,0:T(4,128)(2,1)S(1)}, bf16[2,8,4,512]{3,2,1,0:T(4,128)(2,1)S(1)}, u32[]{:S(2)}, u32[]{:S(2)}) collective-permute-start(bf16[2,8,4,512]{3,2,1,0:T(4,128)(2,1)S(1)} %slice.16), channel_id=1, source_target_pairs={{0,64},{32,96},{64,128},{96,160},{128,192},{160,224},{192,0},{224,... | collective-permute-start | bytes 196616 | tf_op jit(solution)/shard_map/ppermute | solution.py:593
  13.8 9.5 %collective-permute-start.15 = (bf16[2,8,4,512]{3,2,1,0:T(4,128)(2,1)S(1)}, bf16[2,8,4,512]{3,2,1,0:T(4,128)(2,1)S(1)}, u32[]{:S(2)}, u32[]{:S(2)}) collective-permute-start(bf16[2,8,4,512]{3,2,1,0:T(4,128)(2,1)S(1)} %slice.17), channel_id=1, source_target_pairs={{0,192},{32,224},{64,0},{96,32},{128,64},{160,96},{192,128},{224,1... | collective-permute-start | bytes 196616 | tf_op jit(solution)/shard_map/ppermute | solution.py:593
  16.2 7.1 %collective-permute-start.12 = (bf16[4,8,4,512]{3,2,1,0:T(4,128)(2,1)S(1)}, bf16[4,8,4,512]{3,2,1,0:T(4,128)(2,1)S(1)}, u32[]{:S(2)}, u32[]{:S(2)}) collective-permute-start(bf16[4,8,4,512]{3,2,1,0:T(4,128)(2,1)S(1)} %collective-permute-done.10.two_ref.after_ref), channel_id=1, source_target_pairs={{0,32},{32,64},{64,96},{96,128},{128,160},{160,192},{192,224},{224... | collective-permute-start | bytes 393224 | tf_op jit(solution)/shard_map/ppermute | solution.py:593
  17.1 6.2 %collective-permute-start.13 = (bf16[4,8,4,512]{3,2,1,0:T(4,128)(2,1)S(1)}, bf16[4,8,4,512]{3,2,1,0:T(4,128)(2,1)S(1)}, u32[]{:S(2)}, u32[]{:S(2)}) collective-permute-start(bf16[4,8,4,512]{3,2,1,0:T(4,128)(2,1)S(1)} %collective-permute-done.11.back_ref), channel_id=1, source_target_pairs={{0,224},{32,0},{64,32},{96,64},{128,96},{160,128},{192,160},{224,1... | collective-permute-start | bytes 393224 | tf_op jit(solution)/shard_map/ppermute | solution.py:593
  19.9 2.6 %copy-start = (bf16[4,8,4,512]{3,2,1,0:T(4,128)(2,1)S(1)}, bf16[4,8,4,512]{3,2,1,0:T(4,128)(2,1)}, u32[]{:S(2)}) copy-start(bf16[4,8,4,512]{3,2,1,0:T(4,128)(2,1)} %own_ref.1) | copy-start | bytes 393220
  19.9 3.4 %copy-start.1 = (bf16[2,4,128]{2,1,0:T(4,128)(2,1)S(1)}, bf16[2,4,128]{2,1,0:T(4,128)(2,1)}, u32[]{:S(2)}) copy-start(bf16[2,4,128]{2,1,0:T(4,128)(2,1)} %measured_ref.1) | copy-start | bytes 6148
  22.5 4.9 %copy-start.4 = (s32[64,5]{0,1:T(8,128)S(1)}, s32[64,5]{0,1:T(8,128)}, u32[]{:S(2)}) copy-start(s32[64,5]{0,1:T(8,128)} %param.15) | copy-start | bytes 3844
  24.9 3.4 %collective-permute-start.16 = (bf16[256,128]{1,0:T(8,128)(2,1)S(1)}, bf16[256,128]{1,0:T(8,128)(2,1)S(1)}, u32[]{:S(2)}, u32[]{:S(2)}) collective-permute-start(bf16[256,128]{1,0:T(8,128)(2,1)S(1)} %project.1), channel_id=1, source_target_pairs={{0,1},{1,0},{2,3},{3,2},{4,5},{5,4},{6,7},{7,6},{8,9},{9,8},{10,11... | collective-permute-start | bytes 196616 | tf_op jit(solution)/shard_map/ppermute | solution.py:606
  28.3 3.2 %collective-permute-start.17 = (bf16[256,128]{1,0:T(8,128)(2,1)S(1)}, bf16[256,128]{1,0:T(8,128)(2,1)S(1)}, u32[]{:S(2)}, u32[]{:S(2)}) collective-permute-start(bf16[256,128]{1,0:T(8,128)(2,1)S(1)} %add_convert_fusion.1.after_ref), channel_id=1, source_target_pairs={{0,2},{1,3},{2,4},{3,5},{4,6},{5,7},{6,0},{7,1},{8,10},{9,11},{10,... | collective-permute-start | bytes 196616 | tf_op jit(solution)/shard_map/ppermute | solution.py:612
  28.6 4.3 %collective-permute-start.18 = (bf16[256,128]{1,0:T(8,128)(2,1)S(1)}, bf16[256,128]{1,0:T(8,128)(2,1)S(1)}, u32[]{:S(2)}, u32[]{:S(2)}) collective-permute-start(bf16[256,128]{1,0:T(8,128)(2,1)S(1)} %add_convert_fusion.1.after_ref), channel_id=1, source_target_pairs={{0,6},{1,7},{2,0},{3,1},{4,2},{5,3},{6,4},{7,5},{8,14},{9,15},{10,... | collective-permute-start | bytes 196616 | tf_op jit(solution)/shard_map/ppermute | solution.py:612
  29.8 4.7 %collective-permute-start.19 = (bf16[256,128]{1,0:T(8,128)(2,1)S(1)}, bf16[256,128]{1,0:T(8,128)(2,1)S(1)}, u32[]{:S(2)}, u32[]{:S(2)}) collective-permute-start(bf16[256,128]{1,0:T(8,128)(2,1)S(1)} %add_convert_fusion.1.after_ref), channel_id=1, source_target_pairs={{0,4},{1,5},{2,6},{3,7},{4,0},{5,1},{6,2},{7,3},{8,12},{9,13},{10,... | collective-permute-start | bytes 196616 | tf_op jit(solution)/shard_map/ppermute | solution.py:612
  34.6 7.7 %collective-permute-start.20 = (bf16[256,128]{1,0:T(8,128)(2,1)S(1)}, bf16[256,128]{1,0:T(8,128)(2,1)S(1)}, u32[]{:S(2)}, u32[]{:S(2)}) collective-permute-start(bf16[256,128]{1,0:T(8,128)(2,1)S(1)} %add_convert_fusion.own_ref), channel_id=1, source_target_pairs={{0,8},{1,9},{2,10},{3,11},{4,12},{5,13},{6,14},{7,15},{8,16},{9,17... | collective-permute-start | bytes 196616 | tf_op jit(solution)/shard_map/ppermute | solution.py:615
  36.0 6.4 %collective-permute-start.21 = (bf16[256,128]{1,0:T(8,128)(2,1)S(1)}, bf16[256,128]{1,0:T(8,128)(2,1)S(1)}, u32[]{:S(2)}, u32[]{:S(2)}) collective-permute-start(bf16[256,128]{1,0:T(8,128)(2,1)S(1)} %add_convert_fusion.own_ref), channel_id=1, source_target_pairs={{0,24},{1,25},{2,26},{3,27},{4,28},{5,29},{6,30},{7,31},{8,0},{9,1... | collective-permute-start | bytes 196616 | tf_op jit(solution)/shard_map/ppermute | solution.py:615
  37.7 5.1 %collective-permute-start.22 = (bf16[256,128]{1,0:T(8,128)(2,1)S(1)}, bf16[256,128]{1,0:T(8,128)(2,1)S(1)}, u32[]{:S(2)}, u32[]{:S(2)}) collective-permute-start(bf16[256,128]{1,0:T(8,128)(2,1)S(1)} %add_convert_fusion.own_ref), channel_id=1, source_target_pairs={{0,16},{1,17},{2,18},{3,19},{4,20},{5,21},{6,22},{7,23},{8,24},{9,... | collective-permute-start | bytes 196616 | tf_op jit(solution)/shard_map/ppermute | solution.py:615
  42.3 7.6 %copy-start.5 = (f32[32,2,27]{0,1,2:T(2,128)S(1)}, f32[32,2,27]{0,1,2:T(2,128)}, u32[]{:S(2)}) copy-start(f32[32,2,27]{0,1,2:T(2,128)} %param.18) | copy-start | bytes 20740
  42.3 7.8 %copy-start.6 = (f32[32]{0:T(128)S(1)}, f32[32]{0:T(128)}, u32[]{:S(2)}) copy-start(f32[32]{0:T(128)} %param.19) | copy-start | bytes 388
  42.3 30.6 %copy-start.3 = (bf16[55,1536]{1,0:T(8,128)(2,1)S(1)}, bf16[55,1536]{1,0:T(8,128)(2,1)}, u32[]{:S(2)}) copy-start(bf16[55,1536]{1,0:T(8,128)(2,1)} %constant.28.clone) | copy-start | bytes 506884
  42.3 35.2 %copy-start.2 = (f32[32]{0:T(128)S(1)}, f32[32]{0:T(128)}, u32[]{:S(2)}) copy-start(f32[32]{0:T(128)} %out_w_ref.1) | copy-start | bytes 388
  44.9 13.3 %collective-permute-start.23 = (bf16[96,256]{1,0:T(8,128)(2,1)S(1)}, bf16[96,256]{1,0:T(8,128)(2,1)S(1)}, u32[]{:S(2)}, u32[]{:S(2)}) collective-permute-start(bf16[96,256]{1,0:T(8,128)(2,1)S(1)} %get-tuple-element.53), channel_id=1, source_target_pairs={{0,128},{32,160},{64,192},{96,224},{128,0},{160,32},{192,64},{224,... | collective-permute-start | bytes 147464 | tf_op jit(solution)/shard_map/ppermute | solution.py:593
  49.9 8.3 %collective-permute-start.24 = (bf16[96,256]{1,0:T(8,128)(2,1)S(1)}, bf16[96,256]{1,0:T(8,128)(2,1)S(1)}, u32[]{:S(2)}, u32[]{:S(2)}) collective-permute-start(bf16[96,256]{1,0:T(8,128)(2,1)S(1)} %get-tuple-element.54), channel_id=1, source_target_pairs={{0,96},{32,128},{64,160},{96,192},{128,224},{160,0},{192,32},{224,... | collective-permute-start | bytes 147464 | tf_op jit(solution)/shard_map/ppermute | solution.py:593
  50.2 11.0 %collective-permute-start.25 = (bf16[96,256]{1,0:T(8,128)(2,1)S(1)}, bf16[96,256]{1,0:T(8,128)(2,1)S(1)}, u32[]{:S(2)}, u32[]{:S(2)}) collective-permute-start(bf16[96,256]{1,0:T(8,128)(2,1)S(1)} %get-tuple-element.55), channel_id=1, source_target_pairs={{0,160},{32,192},{64,224},{96,0},{128,32},{160,64},{192,96},{224,1... | collective-permute-start | bytes 147464 | tf_op jit(solution)/shard_map/ppermute | solution.py:593
  54.6 6.5 %collective-permute-start.26 = (bf16[96,256]{1,0:T(8,128)(2,1)S(1)}, bf16[96,256]{1,0:T(8,128)(2,1)S(1)}, u32[]{:S(2)}, u32[]{:S(2)}) collective-permute-start(bf16[96,256]{1,0:T(8,128)(2,1)S(1)} %get-tuple-element.56), channel_id=1, source_target_pairs={{0,64},{32,96},{64,128},{96,160},{128,192},{160,224},{192,0},{224,... | collective-permute-start | bytes 147464 | tf_op jit(solution)/shard_map/ppermute | solution.py:593
  54.7 6.5 %collective-permute-start.27 = (bf16[96,256]{1,0:T(8,128)(2,1)S(1)}, bf16[96,256]{1,0:T(8,128)(2,1)S(1)}, u32[]{:S(2)}, u32[]{:S(2)}) collective-permute-start(bf16[96,256]{1,0:T(8,128)(2,1)S(1)} %get-tuple-element.57), channel_id=1, source_target_pairs={{0,192},{32,224},{64,0},{96,32},{128,64},{160,96},{192,128},{224,1... | collective-permute-start | bytes 147464 | tf_op jit(solution)/shard_map/ppermute | solution.py:593
  58.2 4.2 %collective-permute-start.28 = (bf16[96,256]{1,0:T(8,128)(2,1)S(1)}, bf16[96,256]{1,0:T(8,128)(2,1)S(1)}, u32[]{:S(2)}, u32[]{:S(2)}) collective-permute-start(bf16[96,256]{1,0:T(8,128)(2,1)S(1)} %get-tuple-element.58), channel_id=1, source_target_pairs={{0,32},{32,64},{64,96},{96,128},{128,160},{160,192},{192,224},{224... | collective-permute-start | bytes 147464 | tf_op jit(solution)/shard_map/ppermute | solution.py:593
  58.2 4.1 %collective-permute-start.29 = (bf16[96,256]{1,0:T(8,128)(2,1)S(1)}, bf16[96,256]{1,0:T(8,128)(2,1)S(1)}, u32[]{:S(2)}, u32[]{:S(2)}) collective-permute-start(bf16[96,256]{1,0:T(8,128)(2,1)S(1)} %get-tuple-element.59), channel_id=1, source_target_pairs={{0,224},{32,0},{64,32},{96,64},{128,96},{160,128},{192,160},{224,1... | collective-permute-start | bytes 147464 | tf_op jit(solution)/shard_map/ppermute | solution.py:593
  64.4 9.0 %collective-permute-start.30 = (bf16[48,512]{1,0:T(8,128)(2,1)S(1)}, bf16[48,512]{1,0:T(8,128)(2,1)S(1)}, u32[]{:S(2)}, u32[]{:S(2)}) collective-permute-start(bf16[48,512]{1,0:T(8,128)(2,1)S(1)} %get-tuple-element.68), channel_id=1, source_target_pairs={{0,1},{1,0},{2,3},{3,2},{4,5},{5,4},{6,7},{7,6},{8,9},{9,8},{10,11... | collective-permute-start | bytes 147464 | tf_op jit(solution)/shard_map/ppermute | solution.py:656
  70.0 7.5 %collective-permute-start.31 = (bf16[48,512]{1,0:T(8,128)(2,1)S(1)}, bf16[48,512]{1,0:T(8,128)(2,1)S(1)}, u32[]{:S(2)}, u32[]{:S(2)}) collective-permute-start(bf16[48,512]{1,0:T(8,128)(2,1)S(1)} %get-tuple-element.69), channel_id=1, source_target_pairs={{1,2},{3,4},{5,6},{7,8},{9,10},{11,12},{13,14},{15,16},{17,18},{19... | collective-permute-start | bytes 147464 | tf_op jit(solution)/shard_map/ppermute | solution.py:658

commit v3 on v2

--- a/solution.py
+++ b/solution.py
@@ -525,7 +525,7 @@
                 out_ref[x, z, :, 128 * q : 128 * q + 128] = done[q, 4 * z : 4 * z + 4, :]
         return carry
 
-    lax.fori_loop(0, 4, one_x, 0)
+    lax.fori_loop(0, 4, one_x, 0, unroll=True)
 
 
 def convolve(image, grad, inner, outer, matrix, out_w):

time: 82.4 us -> 81.6 us (level)
  no operation moved by 1% of the time
where the time goes in v3:
time: 81.6 us; the launch traced here: 81.4 us
  starting transfers between devices  50.7 us (62%)
  Pallas kernels  15.2 us (19%)
  waiting for transfers between devices  11.3 us (14%)
  other arithmetic  1.61 us (2%)
  local copies, waits for them, and re-layouts  1.23 us (2%)
  between operations  0.95 us (1%)
    ppermute x15, starting transfers between devices, from_sensor(): return lax.ppermute(block, 'sensor', ring(distance, 8))  32.5 us
    ppermute x1, starting transfers between devices, on_device(): inner = lax.ppermute(inner, 'slab', slab_perm(0, 0, 1))  5.59 us
    pallas_call x2, Pallas kernels, hold(): pl.pallas_call(functools.partial(hold_kernel, start), out_shape=jax.Shape...  5.13 us
    ppermute x3, starting transfers between devices, slab_sum_parts(): lax.ppermute(row, 'slab', slab_perm(d, 0, 0))  4.46 us
    ppermute x1, waiting for transfers between devices, on_device(): outer = lax.ppermute(outer, 'slab', pairs + [(b, a) for a, b in pairs])  4.08 us
    pallas_call x1, Pallas kernels, convolve(): pl.pallas_call(conv_kernel, out_shape=jax.ShapeDtypeStruct((4, 8, NB, 512...  3.91 us
    ppermute x3, waiting for transfers between devices, slab_sum_parts(): moved = [lax.ppermute(total, 'slab', slab_perm(0, d, 0)) for d in (1, 3, 2)]  3.47 us
    ppermute x1, starting transfers between devices, on_device(): outer = lax.ppermute(outer, 'slab', pairs + [(b, a) for a, b in pairs])  2.97 us
  transfers between devices with their start and end apart: 24, of which 9 were waited for; matrix products, arithmetic and copies ran while one was open for 4% of the time, Pallas kernels for 8%

profile of v3, /device:TPU:7, one launch (start us, length us, event | category | flops | bytes accessed | tf_op | source)
XLA Modules:
  0.0 81.4 jit_solution(4511668092514486661)
XLA Ops:
  0.0 3.0 %collective-permute-start.10 = (bf16[4,8,4,512]{3,2,1,0:T(4,128)(2,1)}, bf16[4,8,4,512]{3,2,1,0:T(4,128)(2,1)S(1)}, u32[]{:S(2)}, u32[]{:S(2)}) collective-permute-start(bf16[4,8,4,512]{3,2,1,0:T(4,128)(2,1)} %own_ref.1), channel_id=1, source_target_pairs={{0,64},{32,96},{64,128},{96,160},{128,192},{160,224},{192,0},{224,... | collective-permute-start | bytes 393224 | tf_op jit(solution)/shard_map/ppermute | solution.py:593
  3.0 3.0 %collective-permute-start.11 = (bf16[4,8,4,512]{3,2,1,0:T(4,128)(2,1)}, bf16[4,8,4,512]{3,2,1,0:T(4,128)(2,1)S(1)}, u32[]{:S(2)}, u32[]{:S(2)}) collective-permute-start(bf16[4,8,4,512]{3,2,1,0:T(4,128)(2,1)} %own_ref.1), channel_id=1, source_target_pairs={{0,192},{32,224},{64,0},{96,32},{128,64},{160,96},{192,128},{224,1... | collective-permute-start | bytes 393224 | tf_op jit(solution)/shard_map/ppermute | solution.py:593
  6.0 0.7 collective-permute-start.8
  6.8 1.9 %collective-permute-start.9 = (bf16[4,8,4,512]{3,2,1,0:T(4,128)(2,1)}, bf16[4,8,4,512]{3,2,1,0:T(4,128)(2,1)S(1)}, u32[]{:S(2)}, u32[]{:S(2)}) collective-permute-start(bf16[4,8,4,512]{3,2,1,0:T(4,128)(2,1)} %own_ref.1), channel_id=1, source_target_pairs={{0,224},{32,0},{64,32},{96,64},{128,96},{160,128},{192,160},{224,1... | collective-permute-start | bytes 393224 | tf_op jit(solution)/shard_map/ppermute | solution.py:593
  10.1 3.0 %collective-permute-start.14 = (bf16[2,8,4,512]{3,2,1,0:T(4,128)(2,1)S(1)}, bf16[2,8,4,512]{3,2,1,0:T(4,128)(2,1)S(1)}, u32[]{:S(2)}, u32[]{:S(2)}) collective-permute-start(bf16[2,8,4,512]{3,2,1,0:T(4,128)(2,1)S(1)} %slice.16), channel_id=1, source_target_pairs={{0,64},{32,96},{64,128},{96,160},{128,192},{160,224},{192,0},{224,... | collective-permute-start | bytes 196616 | tf_op jit(solution)/shard_map/ppermute | solution.py:593
  13.8 2.4 %collective-permute-start.15 = (bf16[2,8,4,512]{3,2,1,0:T(4,128)(2,1)S(1)}, bf16[2,8,4,512]{3,2,1,0:T(4,128)(2,1)S(1)}, u32[]{:S(2)}, u32[]{:S(2)}) collective-permute-start(bf16[2,8,4,512]{3,2,1,0:T(4,128)(2,1)S(1)} %slice.17), channel_id=1, source_target_pairs={{0,192},{32,224},{64,0},{96,32},{128,64},{160,96},{192,128},{224,1... | collective-permute-start | bytes 196616 | tf_op jit(solution)/shard_map/ppermute | solution.py:593
  16.2 0.9 %collective-permute-start.12 = (bf16[4,8,4,512]{3,2,1,0:T(4,128)(2,1)S(1)}, bf16[4,8,4,512]{3,2,1,0:T(4,128)(2,1)S(1)}, u32[]{:S(2)}, u32[]{:S(2)}) collective-permute-start(bf16[4,8,4,512]{3,2,1,0:T(4,128)(2,1)S(1)} %collective-permute-done.10.two_ref.after_ref), channel_id=1, source_target_pairs={{0,32},{32,64},{64,96},{96,128},{128,160},{160,192},{192,224},{224... | collective-permute-start | bytes 393224 | tf_op jit(solution)/shard_map/ppermute | solution.py:593
  17.1 1.8 %collective-permute-start.13 = (bf16[4,8,4,512]{3,2,1,0:T(4,128)(2,1)S(1)}, bf16[4,8,4,512]{3,2,1,0:T(4,128)(2,1)S(1)}, u32[]{:S(2)}, u32[]{:S(2)}) collective-permute-start(bf16[4,8,4,512]{3,2,1,0:T(4,128)(2,1)S(1)} %collective-permute-done.11.back_ref), channel_id=1, source_target_pairs={{0,224},{32,0},{64,32},{96,64},{128,96},{160,128},{192,160},{224,1... | collective-permute-start | bytes 393224 | tf_op jit(solution)/shard_map/ppermute | solution.py:593
  19.9 2.6 %hold_blocks.2.held = bf16[64,320,128]{2,1,0:T(8,128)(2,1)S(1)} custom-call(bf16[64,320,128]{2,1,0:T(8,128)(2,1)} %bitcast.9, bf16[4,8,4,512]{3,2,1,0:T(4,128)(2,1)S(1)} %collective-permute-done.10.two_ref.after_ref), custom_call_target="tpu_custom_call" | custom-call | bytes 7500000 | tf_op jit(solution)/shard_map/hold_blocks/pallas_call | solution.py:139
  22.5 0.8 gather_first.1
  23.3 1.5 %project.1 = bf16[256,128]{1,0:T(8,128)(2,1)S(1)} custom-call(s32[320,1]{1,0:T(8,128)S(1)} %or.27.keys_ref, f32[320,1]{1,0:T(8,128)S(1)} %reshape.85.weights_ref, f32[320,256]{1,0:T(8,128)S(1)} %get-tuple-element.49.before_ref, bf16[4,8,4,512]{3,2,1,0:T(4,128)(2,1)S(1)} %collective-permute-done.12.three_ref, ...), custom_call_target="tpu_custom_call" | custom-call | bytes 12000000 | tf_op jit(solution)/shard_map/project/pallas_call | solution.py:198
  24.9 2.5 %collective-permute-start.16 = (bf16[256,128]{1,0:T(8,128)(2,1)S(1)}, bf16[256,128]{1,0:T(8,128)(2,1)S(1)}, u32[]{:S(2)}, u32[]{:S(2)}) collective-permute-start(bf16[256,128]{1,0:T(8,128)(2,1)S(1)} %project.1), channel_id=1, source_target_pairs={{0,1},{1,0},{2,3},{3,2},{4,5},{5,4},{6,7},{7,6},{8,9},{9,8},{10,11... | collective-permute-start | bytes 196616 | tf_op jit(solution)/shard_map/ppermute | solution.py:606
  27.4 0.8 %collective-permute-done.16 = bf16[256,128]{1,0:T(8,128)(2,1)S(1)} collective-permute-done((bf16[256,128]{1,0:T(8,128)(2,1)S(1)}, bf16[256,128]{1,0:T(8,128)(2,1)S(1)}, u32[]{:S(2)}, u32[]{:S(2)}) %collective-permute-start.16) | collective-permute-done | bytes 65568 | tf_op jit(solution)/shard_map/ppermute | solution.py:606
  28.6 1.3 %collective-permute-start.18 = (bf16[256,128]{1,0:T(8,128)(2,1)S(1)}, bf16[256,128]{1,0:T(8,128)(2,1)S(1)}, u32[]{:S(2)}, u32[]{:S(2)}) collective-permute-start(bf16[256,128]{1,0:T(8,128)(2,1)S(1)} %add_convert_fusion.1.after_ref), channel_id=1, source_target_pairs={{0,6},{1,7},{2,0},{3,1},{4,2},{5,3},{6,4},{7,5},{8,14},{9,15},{10,... | collective-permute-start | bytes 196616 | tf_op jit(solution)/shard_map/ppermute | solution.py:612
  29.8 1.1 %collective-permute-start.19 = (bf16[256,128]{1,0:T(8,128)(2,1)S(1)}, bf16[256,128]{1,0:T(8,128)(2,1)S(1)}, u32[]{:S(2)}, u32[]{:S(2)}) collective-permute-start(bf16[256,128]{1,0:T(8,128)(2,1)S(1)} %add_convert_fusion.1.after_ref), channel_id=1, source_target_pairs={{0,4},{1,5},{2,6},{3,7},{4,0},{5,1},{6,2},{7,3},{8,12},{9,13},{10,... | collective-permute-start | bytes 196616 | tf_op jit(solution)/shard_map/ppermute | solution.py:612
  31.5 1.4 %collective-permute-done.18 = bf16[256,128]{1,0:T(8,128)(2,1)S(1)} collective-permute-done((bf16[256,128]{1,0:T(8,128)(2,1)S(1)}, bf16[256,128]{1,0:T(8,128)(2,1)S(1)}, u32[]{:S(2)}, u32[]{:S(2)}) %collective-permute-start.18) | collective-permute-done | bytes 65568 | tf_op jit(solution)/shard_map/ppermute | solution.py:612
  32.9 1.7 %collective-permute-done.19 = bf16[256,128]{1,0:T(8,128)(2,1)S(1)} collective-permute-done((bf16[256,128]{1,0:T(8,128)(2,1)S(1)}, bf16[256,128]{1,0:T(8,128)(2,1)S(1)}, u32[]{:S(2)}, u32[]{:S(2)}) %collective-permute-start.19) | collective-permute-done | bytes 65568 | tf_op jit(solution)/shard_map/ppermute | solution.py:612
  34.6 1.4 %collective-permute-start.20 = (bf16[256,128]{1,0:T(8,128)(2,1)S(1)}, bf16[256,128]{1,0:T(8,128)(2,1)S(1)}, u32[]{:S(2)}, u32[]{:S(2)}) collective-permute-start(bf16[256,128]{1,0:T(8,128)(2,1)S(1)} %add_convert_fusion.own_ref), channel_id=1, source_target_pairs={{0,8},{1,9},{2,10},{3,11},{4,12},{5,13},{6,14},{7,15},{8,16},{9,17... | collective-permute-start | bytes 196616 | tf_op jit(solution)/shard_map/ppermute | solution.py:615
  36.0 1.7 %collective-permute-start.21 = (bf16[256,128]{1,0:T(8,128)(2,1)S(1)}, bf16[256,128]{1,0:T(8,128)(2,1)S(1)}, u32[]{:S(2)}, u32[]{:S(2)}) collective-permute-start(bf16[256,128]{1,0:T(8,128)(2,1)S(1)} %add_convert_fusion.own_ref), channel_id=1, source_target_pairs={{0,24},{1,25},{2,26},{3,27},{4,28},{5,29},{6,30},{7,31},{8,0},{9,1... | collective-permute-start | bytes 196616 | tf_op jit(solution)/shard_map/ppermute | solution.py:615
  37.7 1.4 %collective-permute-start.22 = (bf16[256,128]{1,0:T(8,128)(2,1)S(1)}, bf16[256,128]{1,0:T(8,128)(2,1)S(1)}, u32[]{:S(2)}, u32[]{:S(2)}) collective-permute-start(bf16[256,128]{1,0:T(8,128)(2,1)S(1)} %add_convert_fusion.own_ref), channel_id=1, source_target_pairs={{0,16},{1,17},{2,18},{3,19},{4,20},{5,21},{6,22},{7,23},{8,24},{9,... | collective-permute-start | bytes 196616 | tf_op jit(solution)/shard_map/ppermute | solution.py:615
  39.7 2.6 %hold_blocks.3.held = bf16[64,320,128]{2,1,0:T(8,128)(2,1)S(1)} custom-call(bf16[64,320,128]{2,1,0:T(8,128)(2,1)} %bitcast.10, bf16[256,128]{1,0:T(8,128)(2,1)S(1)} %add_convert_fusion.1.after_ref), custom_call_target="tpu_custom_call" | custom-call | bytes 7500000 | tf_op jit(solution)/shard_map/hold_blocks/pallas_call | solution.py:139
  42.8 2.2 %adjoint.1 = (bf16[336,256]{1,0:T(8,128)(2,1)S(1)}, bf16[96,256]{1,0:T(8,128)(2,1)S(1)}, bf16[96,256]{1,0:T(8,128)(2,1)S(1)}, bf16[96,256]{1,0:T(8,128)(2,1)S(1)...) custom-call(bf16[256,128]{1,0:T(8,128)(2,1)S(1)} %add_convert_fusion, ...), custom_call_target="tpu_custom_call" | custom-call | bytes 9000000 | tf_op jit(solution)/shard_map/adjoint/pallas_call | solution.py:304
  44.9 5.0 %collective-permute-start.23 = (bf16[96,256]{1,0:T(8,128)(2,1)S(1)}, bf16[96,256]{1,0:T(8,128)(2,1)S(1)}, u32[]{:S(2)}, u32[]{:S(2)}) collective-permute-start(bf16[96,256]{1,0:T(8,128)(2,1)S(1)} %get-tuple-element.53), channel_id=1, source_target_pairs={{0,128},{32,160},{64,192},{96,224},{128,0},{160,32},{192,64},{224,... | collective-permute-start | bytes 147464 | tf_op jit(solution)/shard_map/ppermute | solution.py:593
  50.2 4.5 %collective-permute-start.25 = (bf16[96,256]{1,0:T(8,128)(2,1)S(1)}, bf16[96,256]{1,0:T(8,128)(2,1)S(1)}, u32[]{:S(2)}, u32[]{:S(2)}) collective-permute-start(bf16[96,256]{1,0:T(8,128)(2,1)S(1)} %get-tuple-element.55), channel_id=1, source_target_pairs={{0,160},{32,192},{64,224},{96,0},{128,32},{160,64},{192,96},{224,1... | collective-permute-start | bytes 147464 | tf_op jit(solution)/shard_map/ppermute | solution.py:593
  54.7 3.6 %collective-permute-start.27 = (bf16[96,256]{1,0:T(8,128)(2,1)S(1)}, bf16[96,256]{1,0:T(8,128)(2,1)S(1)}, u32[]{:S(2)}, u32[]{:S(2)}) collective-permute-start(bf16[96,256]{1,0:T(8,128)(2,1)S(1)} %get-tuple-element.57), channel_id=1, source_target_pairs={{0,192},{32,224},{64,0},{96,32},{128,64},{160,96},{192,128},{224,1... | collective-permute-start | bytes 147464 | tf_op jit(solution)/shard_map/ppermute | solution.py:593
  58.2 2.7 %collective-permute-start.29 = (bf16[96,256]{1,0:T(8,128)(2,1)S(1)}, bf16[96,256]{1,0:T(8,128)(2,1)S(1)}, u32[]{:S(2)}, u32[]{:S(2)}) collective-permute-start(bf16[96,256]{1,0:T(8,128)(2,1)S(1)} %get-tuple-element.59), channel_id=1, source_target_pairs={{0,224},{32,0},{64,32},{96,64},{128,96},{160,128},{192,160},{224,1... | collective-permute-start | bytes 147464 | tf_op jit(solution)/shard_map/ppermute | solution.py:593
  61.2 1.2 %collective-permute-done.28.refs_6_ = bf16[96,256]{1,0:T(8,128)(2,1)S(1)} collective-permute-done((bf16[96,256]{1,0:T(8,128)(2,1)S(1)}, bf16[96,256]{1,0:T(8,128)(2,1)S(1)}, u32[]{:S(2)}, u32[]{:S(2)}) %collective-permute-start.28) | collective-permute-done | bytes 49184 | tf_op jit(solution)/shard_map/ppermute | solution.py:593
  62.4 1.1 %gradient_planes.1 = (f32[4,4,48,128]{3,2,1,0:T(8,128)S(1)}, bf16[48,512]{1,0:T(8,128)(2,1)S(1)}, bf16[48,512]{1,0:T(8,128)(2,1)S(1)}, s32[1,1]{1,0:T(1,128)}) custom-call(bf16[96,256]{1,0:T(8,128)(2,1)S(1)} %get-tuple-element.52.refs_0_, bf16[96,256]{1,0:T(8,128)(2,1)S(1)} %collective-permute-done.23.refs_1_, ...), custom_call_target="tpu_custom_call" | custom-call | bytes 4500000 | tf_op jit(solution)/shard_map/gradient_planes/pallas_call | solution.py:426
  64.4 5.6 %collective-permute-start.30 = (bf16[48,512]{1,0:T(8,128)(2,1)S(1)}, bf16[48,512]{1,0:T(8,128)(2,1)S(1)}, u32[]{:S(2)}, u32[]{:S(2)}) collective-permute-start(bf16[48,512]{1,0:T(8,128)(2,1)S(1)} %get-tuple-element.68), channel_id=1, source_target_pairs={{0,1},{1,0},{2,3},{3,2},{4,5},{5,4},{6,7},{7,6},{8,9},{9,8},{10,11... | collective-permute-start | bytes 147464 | tf_op jit(solution)/shard_map/ppermute | solution.py:656
  70.0 3.0 %collective-permute-start.31 = (bf16[48,512]{1,0:T(8,128)(2,1)S(1)}, bf16[48,512]{1,0:T(8,128)(2,1)S(1)}, u32[]{:S(2)}, u32[]{:S(2)}) collective-permute-start(bf16[48,512]{1,0:T(8,128)(2,1)S(1)} %get-tuple-element.69), channel_id=1, source_target_pairs={{1,2},{3,4},{5,6},{7,8},{9,10},{11,12},{13,14},{15,16},{17,18},{19... | collective-permute-start | bytes 147464 | tf_op jit(solution)/shard_map/ppermute | solution.py:658
  73.4 4.1 %collective-permute-done.31.outer_ref = bf16[48,512]{1,0:T(8,128)(2,1)S(1)} collective-permute-done((bf16[48,512]{1,0:T(8,128)(2,1)S(1)}, bf16[48,512]{1,0:T(8,128)(2,1)S(1)}, u32[]{:S(2)}, u32[]{:S(2)}) %collective-permute-start.31) | collective-permute-done | bytes 49184 | tf_op jit(solution)/shard_map/ppermute | solution.py:658
  77.5 3.9 %convolutions.1 = f32[4,8,4,512]{3,2,1,0:T(4,128)} custom-call(f32[4,4,48,128]{3,2,1,0:T(8,128)S(1)} %get-tuple-element.48.image_ref, f32[4,4,48,128]{3,2,1,0:T(8,128)S(1)} %get-tuple-element.67.grad_ref, bf16[48,512]{1,0:T(8,128)(2,1)S(1)} %collective-permute-done.30.inner_ref, bf16[48,512]{1,0:T(8,128)(2,1)S(1)} %collective-permute-done.31.outer_ref, ...), custom_call_target="tpu_custom_call" | custom-call | bytes 15000000 | tf_op jit(solution)/shard_map/convolutions/pallas_call | solution.py:532
  (63 shorter events, 6.3 us)
Async XLA Ops:
  0.0 10.0 %collective-permute-start.10 = (bf16[4,8,4,512]{3,2,1,0:T(4,128)(2,1)}, bf16[4,8,4,512]{3,2,1,0:T(4,128)(2,1)S(1)}, u32[]{:S(2)}, u32[]{:S(2)}) collective-permute-start(bf16[4,8,4,512]{3,2,1,0:T(4,128)(2,1)} %own_ref.1), channel_id=1, source_target_pairs={{0,64},{32,96},{64,128},{96,160},{128,192},{160,224},{192,0},{224,... | collective-permute-start | bytes 393224 | tf_op jit(solution)/shard_map/ppermute | solution.py:593
  3.0 10.8 %collective-permute-start.11 = (bf16[4,8,4,512]{3,2,1,0:T(4,128)(2,1)}, bf16[4,8,4,512]{3,2,1,0:T(4,128)(2,1)S(1)}, u32[]{:S(2)}, u32[]{:S(2)}) collective-permute-start(bf16[4,8,4,512]{3,2,1,0:T(4,128)(2,1)} %own_ref.1), channel_id=1, source_target_pairs={{0,192},{32,224},{64,0},{96,32},{128,64},{160,96},{192,128},{224,1... | collective-permute-start | bytes 393224 | tf_op jit(solution)/shard_map/ppermute | solution.py:593
  6.0 11.1 %collective-permute-start.8 = (bf16[4,8,4,512]{3,2,1,0:T(4,128)(2,1)}, bf16[4,8,4,512]{3,2,1,0:T(4,128)(2,1)S(1)}, u32[]{:S(2)}, u32[]{:S(2)}) collective-permute-start(bf16[4,8,4,512]{3,2,1,0:T(4,128)(2,1)} %own_ref.1), channel_id=1, source_target_pairs={{0,32},{32,64},{64,96},{96,128},{128,160},{160,192},{192,224},{224... | collective-permute-start | bytes 393224 | tf_op jit(solution)/shard_map/ppermute | solution.py:593
  6.8 15.7 %collective-permute-start.9 = (bf16[4,8,4,512]{3,2,1,0:T(4,128)(2,1)}, bf16[4,8,4,512]{3,2,1,0:T(4,128)(2,1)S(1)}, u32[]{:S(2)}, u32[]{:S(2)}) collective-permute-start(bf16[4,8,4,512]{3,2,1,0:T(4,128)(2,1)} %own_ref.1), channel_id=1, source_target_pairs={{0,224},{32,0},{64,32},{96,64},{128,96},{160,128},{192,160},{224,1... | collective-permute-start | bytes 393224 | tf_op jit(solution)/shard_map/ppermute | solution.py:593
  10.1 13.2 %collective-permute-start.14 = (bf16[2,8,4,512]{3,2,1,0:T(4,128)(2,1)S(1)}, bf16[2,8,4,512]{3,2,1,0:T(4,128)(2,1)S(1)}, u32[]{:S(2)}, u32[]{:S(2)}) collective-permute-start(bf16[2,8,4,512]{3,2,1,0:T(4,128)(2,1)S(1)} %slice.16), channel_id=1, source_target_pairs={{0,64},{32,96},{64,128},{96,160},{128,192},{160,224},{192,0},{224,... | collective-permute-start | bytes 196616 | tf_op jit(solution)/shard_map/ppermute | solution.py:593
  13.8 9.5 %collective-permute-start.15 = (bf16[2,8,4,512]{3,2,1,0:T(4,128)(2,1)S(1)}, bf16[2,8,4,512]{3,2,1,0:T(4,128)(2,1)S(1)}, u32[]{:S(2)}, u32[]{:S(2)}) collective-permute-start(bf16[2,8,4,512]{3,2,1,0:T(4,128)(2,1)S(1)} %slice.17), channel_id=1, source_target_pairs={{0,192},{32,224},{64,0},{96,32},{128,64},{160,96},{192,128},{224,1... | collective-permute-start | bytes 196616 | tf_op jit(solution)/shard_map/ppermute | solution.py:593
  16.2 7.1 %collective-permute-start.12 = (bf16[4,8,4,512]{3,2,1,0:T(4,128)(2,1)S(1)}, bf16[4,8,4,512]{3,2,1,0:T(4,128)(2,1)S(1)}, u32[]{:S(2)}, u32[]{:S(2)}) collective-permute-start(bf16[4,8,4,512]{3,2,1,0:T(4,128)(2,1)S(1)} %collective-permute-done.10.two_ref.after_ref), channel_id=1, source_target_pairs={{0,32},{32,64},{64,96},{96,128},{128,160},{160,192},{192,224},{224... | collective-permute-start | bytes 393224 | tf_op jit(solution)/shard_map/ppermute | solution.py:593
  17.1 6.2 %collective-permute-start.13 = (bf16[4,8,4,512]{3,2,1,0:T(4,128)(2,1)S(1)}, bf16[4,8,4,512]{3,2,1,0:T(4,128)(2,1)S(1)}, u32[]{:S(2)}, u32[]{:S(2)}) collective-permute-start(bf16[4,8,4,512]{3,2,1,0:T(4,128)(2,1)S(1)} %collective-permute-done.11.back_ref), channel_id=1, source_target_pairs={{0,224},{32,0},{64,32},{96,64},{128,96},{160,128},{192,160},{224,1... | collective-permute-start | bytes 393224 | tf_op jit(solution)/shard_map/ppermute | solution.py:593
  19.9 2.6 %copy-start = (bf16[4,8,4,512]{3,2,1,0:T(4,128)(2,1)S(1)}, bf16[4,8,4,512]{3,2,1,0:T(4,128)(2,1)}, u32[]{:S(2)}) copy-start(bf16[4,8,4,512]{3,2,1,0:T(4,128)(2,1)} %own_ref.1) | copy-start | bytes 393220
  19.9 3.4 %copy-start.1 = (bf16[2,4,128]{2,1,0:T(4,128)(2,1)S(1)}, bf16[2,4,128]{2,1,0:T(4,128)(2,1)}, u32[]{:S(2)}) copy-start(bf16[2,4,128]{2,1,0:T(4,128)(2,1)} %measured_ref.1) | copy-start | bytes 6148
  22.5 4.9 %copy-start.4 = (s32[64,5]{0,1:T(8,128)S(1)}, s32[64,5]{0,1:T(8,128)}, u32[]{:S(2)}) copy-start(s32[64,5]{0,1:T(8,128)} %param.15) | copy-start | bytes 3844
  24.9 3.4 %collective-permute-start.16 = (bf16[256,128]{1,0:T(8,128)(2,1)S(1)}, bf16[256,128]{1,0:T(8,128)(2,1)S(1)}, u32[]{:S(2)}, u32[]{:S(2)}) collective-permute-start(bf16[256,128]{1,0:T(8,128)(2,1)S(1)} %project.1), channel_id=1, source_target_pairs={{0,1},{1,0},{2,3},{3,2},{4,5},{5,4},{6,7},{7,6},{8,9},{9,8},{10,11... | collective-permute-start | bytes 196616 | tf_op jit(solution)/shard_map/ppermute | solution.py:606
  28.3 3.2 %collective-permute-start.17 = (bf16[256,128]{1,0:T(8,128)(2,1)S(1)}, bf16[256,128]{1,0:T(8,128)(2,1)S(1)}, u32[]{:S(2)}, u32[]{:S(2)}) collective-permute-start(bf16[256,128]{1,0:T(8,128)(2,1)S(1)} %add_convert_fusion.1.after_ref), channel_id=1, source_target_pairs={{0,2},{1,3},{2,4},{3,5},{4,6},{5,7},{6,0},{7,1},{8,10},{9,11},{10,... | collective-permute-start | bytes 196616 | tf_op jit(solution)/shard_map/ppermute | solution.py:612
  28.6 4.3 %collective-permute-start.18 = (bf16[256,128]{1,0:T(8,128)(2,1)S(1)}, bf16[256,128]{1,0:T(8,128)(2,1)S(1)}, u32[]{:S(2)}, u32[]{:S(2)}) collective-permute-start(bf16[256,128]{1,0:T(8,128)(2,1)S(1)} %add_convert_fusion.1.after_ref), channel_id=1, source_target_pairs={{0,6},{1,7},{2,0},{3,1},{4,2},{5,3},{6,4},{7,5},{8,14},{9,15},{10,... | collective-permute-start | bytes 196616 | tf_op jit(solution)/shard_map/ppermute | solution.py:612
  29.8 4.7 %collective-permute-start.19 = (bf16[256,128]{1,0:T(8,128)(2,1)S(1)}, bf16[256,128]{1,0:T(8,128)(2,1)S(1)}, u32[]{:S(2)}, u32[]{:S(2)}) collective-permute-start(bf16[256,128]{1,0:T(8,128)(2,1)S(1)} %add_convert_fusion.1.after_ref), channel_id=1, source_target_pairs={{0,4},{1,5},{2,6},{3,7},{4,0},{5,1},{6,2},{7,3},{8,12},{9,13},{10,... | collective-permute-start | bytes 196616 | tf_op jit(solution)/shard_map/ppermute | solution.py:612
  34.6 7.7 %collective-permute-start.20 = (bf16[256,128]{1,0:T(8,128)(2,1)S(1)}, bf16[256,128]{1,0:T(8,128)(2,1)S(1)}, u32[]{:S(2)}, u32[]{:S(2)}) collective-permute-start(bf16[256,128]{1,0:T(8,128)(2,1)S(1)} %add_convert_fusion.own_ref), channel_id=1, source_target_pairs={{0,8},{1,9},{2,10},{3,11},{4,12},{5,13},{6,14},{7,15},{8,16},{9,17... | collective-permute-start | bytes 196616 | tf_op jit(solution)/shard_map/ppermute | solution.py:615
  36.0 6.4 %collective-permute-start.21 = (bf16[256,128]{1,0:T(8,128)(2,1)S(1)}, bf16[256,128]{1,0:T(8,128)(2,1)S(1)}, u32[]{:S(2)}, u32[]{:S(2)}) collective-permute-start(bf16[256,128]{1,0:T(8,128)(2,1)S(1)} %add_convert_fusion.own_ref), channel_id=1, source_target_pairs={{0,24},{1,25},{2,26},{3,27},{4,28},{5,29},{6,30},{7,31},{8,0},{9,1... | collective-permute-start | bytes 196616 | tf_op jit(solution)/shard_map/ppermute | solution.py:615
  37.7 5.1 %collective-permute-start.22 = (bf16[256,128]{1,0:T(8,128)(2,1)S(1)}, bf16[256,128]{1,0:T(8,128)(2,1)S(1)}, u32[]{:S(2)}, u32[]{:S(2)}) collective-permute-start(bf16[256,128]{1,0:T(8,128)(2,1)S(1)} %add_convert_fusion.own_ref), channel_id=1, source_target_pairs={{0,16},{1,17},{2,18},{3,19},{4,20},{5,21},{6,22},{7,23},{8,24},{9,... | collective-permute-start | bytes 196616 | tf_op jit(solution)/shard_map/ppermute | solution.py:615
  42.3 7.6 %copy-start.5 = (f32[32,2,27]{0,1,2:T(2,128)S(1)}, f32[32,2,27]{0,1,2:T(2,128)}, u32[]{:S(2)}) copy-start(f32[32,2,27]{0,1,2:T(2,128)} %param.18) | copy-start | bytes 20740
  42.3 7.8 %copy-start.6 = (f32[32]{0:T(128)S(1)}, f32[32]{0:T(128)}, u32[]{:S(2)}) copy-start(f32[32]{0:T(128)} %param.19) | copy-start | bytes 388
  42.3 30.6 %copy-start.3 = (bf16[55,1536]{1,0:T(8,128)(2,1)S(1)}, bf16[55,1536]{1,0:T(8,128)(2,1)}, u32[]{:S(2)}) copy-start(bf16[55,1536]{1,0:T(8,128)(2,1)} %constant.28.clone) | copy-start | bytes 506884
  42.3 35.2 %copy-start.2 = (f32[32]{0:T(128)S(1)}, f32[32]{0:T(128)}, u32[]{:S(2)}) copy-start(f32[32]{0:T(128)} %out_w_ref.1) | copy-start | bytes 388
  44.9 13.3 %collective-permute-start.23 = (bf16[96,256]{1,0:T(8,128)(2,1)S(1)}, bf16[96,256]{1,0:T(8,128)(2,1)S(1)}, u32[]{:S(2)}, u32[]{:S(2)}) collective-permute-start(bf16[96,256]{1,0:T(8,128)(2,1)S(1)} %get-tuple-element.53), channel_id=1, source_target_pairs={{0,128},{32,160},{64,192},{96,224},{128,0},{160,32},{192,64},{224,... | collective-permute-start | bytes 147464 | tf_op jit(solution)/shard_map/ppermute | solution.py:593
  49.9 8.3 %collective-permute-start.24 = (bf16[96,256]{1,0:T(8,128)(2,1)S(1)}, bf16[96,256]{1,0:T(8,128)(2,1)S(1)}, u32[]{:S(2)}, u32[]{:S(2)}) collective-permute-start(bf16[96,256]{1,0:T(8,128)(2,1)S(1)} %get-tuple-element.54), channel_id=1, source_target_pairs={{0,96},{32,128},{64,160},{96,192},{128,224},{160,0},{192,32},{224,... | collective-permute-start | bytes 147464 | tf_op jit(solution)/shard_map/ppermute | solution.py:593
  50.2 11.0 %collective-permute-start.25 = (bf16[96,256]{1,0:T(8,128)(2,1)S(1)}, bf16[96,256]{1,0:T(8,128)(2,1)S(1)}, u32[]{:S(2)}, u32[]{:S(2)}) collective-permute-start(bf16[96,256]{1,0:T(8,128)(2,1)S(1)} %get-tuple-element.55), channel_id=1, source_target_pairs={{0,160},{32,192},{64,224},{96,0},{128,32},{160,64},{192,96},{224,1... | collective-permute-start | bytes 147464 | tf_op jit(solution)/shard_map/ppermute | solution.py:593
  54.6 6.5 %collective-permute-start.26 = (bf16[96,256]{1,0:T(8,128)(2,1)S(1)}, bf16[96,256]{1,0:T(8,128)(2,1)S(1)}, u32[]{:S(2)}, u32[]{:S(2)}) collective-permute-start(bf16[96,256]{1,0:T(8,128)(2,1)S(1)} %get-tuple-element.56), channel_id=1, source_target_pairs={{0,64},{32,96},{64,128},{96,160},{128,192},{160,224},{192,0},{224,... | collective-permute-start | bytes 147464 | tf_op jit(solution)/shard_map/ppermute | solution.py:593
  54.7 6.5 %collective-permute-start.27 = (bf16[96,256]{1,0:T(8,128)(2,1)S(1)}, bf16[96,256]{1,0:T(8,128)(2,1)S(1)}, u32[]{:S(2)}, u32[]{:S(2)}) collective-permute-start(bf16[96,256]{1,0:T(8,128)(2,1)S(1)} %get-tuple-element.57), channel_id=1, source_target_pairs={{0,192},{32,224},{64,0},{96,32},{128,64},{160,96},{192,128},{224,1... | collective-permute-start | bytes 147464 | tf_op jit(solution)/shard_map/ppermute | solution.py:593
  58.2 4.2 %collective-permute-start.28 = (bf16[96,256]{1,0:T(8,128)(2,1)S(1)}, bf16[96,256]{1,0:T(8,128)(2,1)S(1)}, u32[]{:S(2)}, u32[]{:S(2)}) collective-permute-start(bf16[96,256]{1,0:T(8,128)(2,1)S(1)} %get-tuple-element.58), channel_id=1, source_target_pairs={{0,32},{32,64},{64,96},{96,128},{128,160},{160,192},{192,224},{224... | collective-permute-start | bytes 147464 | tf_op jit(solution)/shard_map/ppermute | solution.py:593
  58.2 4.1 %collective-permute-start.29 = (bf16[96,256]{1,0:T(8,128)(2,1)S(1)}, bf16[96,256]{1,0:T(8,128)(2,1)S(1)}, u32[]{:S(2)}, u32[]{:S(2)}) collective-permute-start(bf16[96,256]{1,0:T(8,128)(2,1)S(1)} %get-tuple-element.59), channel_id=1, source_target_pairs={{0,224},{32,0},{64,32},{96,64},{128,96},{160,128},{192,160},{224,1... | collective-permute-start | bytes 147464 | tf_op jit(solution)/shard_map/ppermute | solution.py:593
  64.4 9.0 %collective-permute-start.30 = (bf16[48,512]{1,0:T(8,128)(2,1)S(1)}, bf16[48,512]{1,0:T(8,128)(2,1)S(1)}, u32[]{:S(2)}, u32[]{:S(2)}) collective-permute-start(bf16[48,512]{1,0:T(8,128)(2,1)S(1)} %get-tuple-element.68), channel_id=1, source_target_pairs={{0,1},{1,0},{2,3},{3,2},{4,5},{5,4},{6,7},{7,6},{8,9},{9,8},{10,11... | collective-permute-start | bytes 147464 | tf_op jit(solution)/shard_map/ppermute | solution.py:656
  70.0 7.5 %collective-permute-start.31 = (bf16[48,512]{1,0:T(8,128)(2,1)S(1)}, bf16[48,512]{1,0:T(8,128)(2,1)S(1)}, u32[]{:S(2)}, u32[]{:S(2)}) collective-permute-start(bf16[48,512]{1,0:T(8,128)(2,1)S(1)} %get-tuple-element.69), channel_id=1, source_target_pairs={{1,2},{3,4},{5,6},{7,8},{9,10},{11,12},{13,14},{15,16},{17,18},{19... | collective-permute-start | bytes 147464 | tf_op jit(solution)/shard_map/ppermute | solution.py:658

commit v4 on v3

--- a/solution.py
+++ b/solution.py
@@ -471,9 +471,34 @@
     return jnp.where(y == 511, 0.0, pltpu.roll(rows, 511, axis=1))
 
 
+def stack_kernel(image_ref, grad_ref, body):
+    for n in range(NB):
+        for x in range(6):
+            rows = jnp.concatenate(
+                [
+                    jnp.concatenate([ref[n, q, 8 * x : 8 * x + 8, :] for q in range(4)], axis=1)
+                    for ref in (image_ref, grad_ref)
+                ],
+                axis=0,
+            )
+            for e in range(3):
+                body[e, n * 6 + x] = shifted_rows(rows, e).astype(BF16)
+
+
+def stack_rows(image, grad):
+    return pl.pallas_call(
+        stack_kernel,
+        out_shape=jax.ShapeDtypeStruct((3, 24, 16, 512), BF16),
+        in_specs=[vmem()] * 2,
+        out_specs=vmem(),
+        compiler_params=params(16),
+        cost_estimate=cost(1.0),
+        name="stack_rows",
+    )(image, grad)
+
+
 def conv_kernel(
-    image_ref, grad_ref, inner_ref, outer_ref, matrix_ref, out_w_ref, out_ref,
-    body, ends, done,
+    image_ref, body, inner_ref, outer_ref, matrix_ref, out_w_ref, out_ref, ends, done
 ):
     first_core = lax.rem(lax.axis_index("slab"), 2) == 0
     inner, outer = inner_ref[...].astype(F32), outer_ref[...].astype(F32)
@@ -488,17 +513,6 @@
         ends[q, pl.ds(12, 24, stride=16), :] = jnp.ones((24, 128), F32)
         for r in range(13, 16):
             ends[q, pl.ds(r, 24, stride=16), :] = jnp.zeros((24, 128), F32)
-    for n in range(NB):
-        for x in range(6):
-            rows = jnp.concatenate(
-                [
-                    jnp.concatenate([ref[n, q, 8 * x : 8 * x + 8, :] for q in range(4)], axis=1)
-                    for ref in (image_ref, grad_ref)
-                ],
-                axis=0,
-            )
-            for e in range(3):
-                body[e, n * 6 + x] = shifted_rows(rows, e).astype(BF16)
 
     def one_x(x, carry):
         for n in range(NB):
@@ -528,21 +542,20 @@
     lax.fori_loop(0, 4, one_x, 0, unroll=True)
 
 
-def convolve(image, grad, inner, outer, matrix, out_w):
+def convolve(image, body, inner, outer, matrix, out_w):
     return pl.pallas_call(
         conv_kernel,
         out_shape=jax.ShapeDtypeStruct((4, 8, NB, 512), F32),
         in_specs=[vmem()] * 5 + [smem()],
         out_specs=vmem(),
         scratch_shapes=[
-            pltpu.VMEM((3, 24, 16, 512), BF16),
             pltpu.VMEM((4, 384, 128), F32),
             pltpu.VMEM((4, 32, 128), F32),
         ],
         compiler_params=params(32),
         cost_estimate=cost(5.0),
         name="convolutions",
-    )(image, grad, inner, outer, matrix, out_w)
+    )(image, body, inner, outer, matrix, out_w)
 
 
 def tap_choice():
@@ -656,7 +669,7 @@
     inner = lax.ppermute(inner, "slab", slab_perm(0, 0, 1))
     pairs = [(2 * i + 1, 2 * i + 2) for i in range(15)]
     outer = lax.ppermute(outer, "slab", pairs + [(b, a) for a, b in pairs])
-    return convolve(image, grad, inner, outer, matrix, conv_out)
+    return convolve(image, stack_rows(image, grad), inner, outer, matrix, conv_out)
 
 
 def solution(mesh):

time: 81.6 us -> 81.5 us (level)
  no operation moved by 1% of the time
where the time goes in v4:
time: 81.5 us; the launch traced here: 81.3 us
  starting transfers between devices  50.7 us (62%)
  Pallas kernels  15.4 us (19%)
  waiting for transfers between devices  11 us (13%)
  other arithmetic  1.61 us (2%)
  local copies, waits for them, and re-layouts  1.23 us (2%)
  between operations  0.95 us (1%)
    ppermute x15, starting transfers between devices, from_sensor(): return lax.ppermute(block, 'sensor', ring(distance, 8))  32.5 us
    ppermute x1, starting transfers between devices, on_device(): inner = lax.ppermute(inner, 'slab', slab_perm(0, 0, 1))  5.59 us
    pallas_call x2, Pallas kernels, hold(): pl.pallas_call(functools.partial(hold_kernel, start), out_shape=jax.Shape...  5.13 us
    ppermute x3, starting transfers between devices, slab_sum_parts(): lax.ppermute(row, 'slab', slab_perm(d, 0, 0))  4.46 us
    pallas_call x1, Pallas kernels, convolve(): pl.pallas_call(conv_kernel, out_shape=jax.ShapeDtypeStruct((4, 8, NB, 512...  3.84 us
    ppermute x1, waiting for transfers between devices, on_device(): outer = lax.ppermute(outer, 'slab', pairs + [(b, a) for a, b in pairs])  3.79 us
    ppermute x3, waiting for transfers between devices, slab_sum_parts(): moved = [lax.ppermute(total, 'slab', slab_perm(0, d, 0)) for d in (1, 3, 2)]  3.47 us
    ppermute x1, starting transfers between devices, on_device(): outer = lax.ppermute(outer, 'slab', pairs + [(b, a) for a, b in pairs])  2.97 us
  transfers between devices with their start and end apart: 24, of which 9 were waited for; matrix products, arithmetic and copies ran while one was open for 4% of the time, Pallas kernels for 8%

profile of v4, /device:TPU:7, one launch (start us, length us, event | category | flops | bytes accessed | tf_op | source)
XLA Modules:
  0.0 81.3 jit_solution(7217442589658414943)
XLA Ops:
  0.0 3.0 %collective-permute-start.10 = (bf16[4,8,4,512]{3,2,1,0:T(4,128)(2,1)}, bf16[4,8,4,512]{3,2,1,0:T(4,128)(2,1)S(1)}, u32[]{:S(2)}, u32[]{:S(2)}) collective-permute-start(bf16[4,8,4,512]{3,2,1,0:T(4,128)(2,1)} %own_ref.1), channel_id=1, source_target_pairs={{0,64},{32,96},{64,128},{96,160},{128,192},{160,224},{192,0},{224,... | collective-permute-start | bytes 393224 | tf_op jit(solution)/shard_map/ppermute | solution.py:606
  3.0 3.0 %collective-permute-start.11 = (bf16[4,8,4,512]{3,2,1,0:T(4,128)(2,1)}, bf16[4,8,4,512]{3,2,1,0:T(4,128)(2,1)S(1)}, u32[]{:S(2)}, u32[]{:S(2)}) collective-permute-start(bf16[4,8,4,512]{3,2,1,0:T(4,128)(2,1)} %own_ref.1), channel_id=1, source_target_pairs={{0,192},{32,224},{64,0},{96,32},{128,64},{160,96},{192,128},{224,1... | collective-permute-start | bytes 393224 | tf_op jit(solution)/shard_map/ppermute | solution.py:606
  6.0 0.7 collective-permute-start.8
  6.8 1.9 %collective-permute-start.9 = (bf16[4,8,4,512]{3,2,1,0:T(4,128)(2,1)}, bf16[4,8,4,512]{3,2,1,0:T(4,128)(2,1)S(1)}, u32[]{:S(2)}, u32[]{:S(2)}) collective-permute-start(bf16[4,8,4,512]{3,2,1,0:T(4,128)(2,1)} %own_ref.1), channel_id=1, source_target_pairs={{0,224},{32,0},{64,32},{96,64},{128,96},{160,128},{192,160},{224,1... | collective-permute-start | bytes 393224 | tf_op jit(solution)/shard_map/ppermute | solution.py:606
  10.1 3.0 %collective-permute-start.14 = (bf16[2,8,4,512]{3,2,1,0:T(4,128)(2,1)S(1)}, bf16[2,8,4,512]{3,2,1,0:T(4,128)(2,1)S(1)}, u32[]{:S(2)}, u32[]{:S(2)}) collective-permute-start(bf16[2,8,4,512]{3,2,1,0:T(4,128)(2,1)S(1)} %slice.16), channel_id=1, source_target_pairs={{0,64},{32,96},{64,128},{96,160},{128,192},{160,224},{192,0},{224,... | collective-permute-start | bytes 196616 | tf_op jit(solution)/shard_map/ppermute | solution.py:606
  13.8 2.4 %collective-permute-start.15 = (bf16[2,8,4,512]{3,2,1,0:T(4,128)(2,1)S(1)}, bf16[2,8,4,512]{3,2,1,0:T(4,128)(2,1)S(1)}, u32[]{:S(2)}, u32[]{:S(2)}) collective-permute-start(bf16[2,8,4,512]{3,2,1,0:T(4,128)(2,1)S(1)} %slice.17), channel_id=1, source_target_pairs={{0,192},{32,224},{64,0},{96,32},{128,64},{160,96},{192,128},{224,1... | collective-permute-start | bytes 196616 | tf_op jit(solution)/shard_map/ppermute | solution.py:606
  16.2 0.9 %collective-permute-start.12 = (bf16[4,8,4,512]{3,2,1,0:T(4,128)(2,1)S(1)}, bf16[4,8,4,512]{3,2,1,0:T(4,128)(2,1)S(1)}, u32[]{:S(2)}, u32[]{:S(2)}) collective-permute-start(bf16[4,8,4,512]{3,2,1,0:T(4,128)(2,1)S(1)} %collective-permute-done.10.two_ref.after_ref), channel_id=1, source_target_pairs={{0,32},{32,64},{64,96},{96,128},{128,160},{160,192},{192,224},{224... | collective-permute-start | bytes 393224 | tf_op jit(solution)/shard_map/ppermute | solution.py:606
  17.1 1.8 %collective-permute-start.13 = (bf16[4,8,4,512]{3,2,1,0:T(4,128)(2,1)S(1)}, bf16[4,8,4,512]{3,2,1,0:T(4,128)(2,1)S(1)}, u32[]{:S(2)}, u32[]{:S(2)}) collective-permute-start(bf16[4,8,4,512]{3,2,1,0:T(4,128)(2,1)S(1)} %collective-permute-done.11.back_ref), channel_id=1, source_target_pairs={{0,224},{32,0},{64,32},{96,64},{128,96},{160,128},{192,160},{224,1... | collective-permute-start | bytes 393224 | tf_op jit(solution)/shard_map/ppermute | solution.py:606
  19.9 2.6 %hold_blocks.2.held = bf16[64,320,128]{2,1,0:T(8,128)(2,1)S(1)} custom-call(bf16[64,320,128]{2,1,0:T(8,128)(2,1)} %bitcast.9, bf16[4,8,4,512]{3,2,1,0:T(4,128)(2,1)S(1)} %collective-permute-done.10.two_ref.after_ref), custom_call_target="tpu_custom_call" | custom-call | bytes 7500000 | tf_op jit(solution)/shard_map/hold_blocks/pallas_call | solution.py:139
  22.5 0.8 gather_first.1
  23.3 1.5 %project.1 = bf16[256,128]{1,0:T(8,128)(2,1)S(1)} custom-call(s32[320,1]{1,0:T(8,128)S(1)} %or.27.keys_ref, f32[320,1]{1,0:T(8,128)S(1)} %reshape.85.weights_ref, f32[320,256]{1,0:T(8,128)S(1)} %get-tuple-element.49.before_ref, bf16[4,8,4,512]{3,2,1,0:T(4,128)(2,1)S(1)} %collective-permute-done.12.three_ref, ...), custom_call_target="tpu_custom_call" | custom-call | bytes 12000000 | tf_op jit(solution)/shard_map/project/pallas_call | solution.py:198
  24.9 2.5 %collective-permute-start.16 = (bf16[256,128]{1,0:T(8,128)(2,1)S(1)}, bf16[256,128]{1,0:T(8,128)(2,1)S(1)}, u32[]{:S(2)}, u32[]{:S(2)}) collective-permute-start(bf16[256,128]{1,0:T(8,128)(2,1)S(1)} %project.1), channel_id=1, source_target_pairs={{0,1},{1,0},{2,3},{3,2},{4,5},{5,4},{6,7},{7,6},{8,9},{9,8},{10,11... | collective-permute-start | bytes 196616 | tf_op jit(solution)/shard_map/ppermute | solution.py:619
  27.4 0.8 %collective-permute-done.16 = bf16[256,128]{1,0:T(8,128)(2,1)S(1)} collective-permute-done((bf16[256,128]{1,0:T(8,128)(2,1)S(1)}, bf16[256,128]{1,0:T(8,128)(2,1)S(1)}, u32[]{:S(2)}, u32[]{:S(2)}) %collective-permute-start.16) | collective-permute-done | bytes 65568 | tf_op jit(solution)/shard_map/ppermute | solution.py:619
  28.6 1.3 %collective-permute-start.18 = (bf16[256,128]{1,0:T(8,128)(2,1)S(1)}, bf16[256,128]{1,0:T(8,128)(2,1)S(1)}, u32[]{:S(2)}, u32[]{:S(2)}) collective-permute-start(bf16[256,128]{1,0:T(8,128)(2,1)S(1)} %add_convert_fusion.1.after_ref), channel_id=1, source_target_pairs={{0,6},{1,7},{2,0},{3,1},{4,2},{5,3},{6,4},{7,5},{8,14},{9,15},{10,... | collective-permute-start | bytes 196616 | tf_op jit(solution)/shard_map/ppermute | solution.py:625
  29.8 1.1 %collective-permute-start.19 = (bf16[256,128]{1,0:T(8,128)(2,1)S(1)}, bf16[256,128]{1,0:T(8,128)(2,1)S(1)}, u32[]{:S(2)}, u32[]{:S(2)}) collective-permute-start(bf16[256,128]{1,0:T(8,128)(2,1)S(1)} %add_convert_fusion.1.after_ref), channel_id=1, source_target_pairs={{0,4},{1,5},{2,6},{3,7},{4,0},{5,1},{6,2},{7,3},{8,12},{9,13},{10,... | collective-permute-start | bytes 196616 | tf_op jit(solution)/shard_map/ppermute | solution.py:625
  31.5 1.4 %collective-permute-done.18 = bf16[256,128]{1,0:T(8,128)(2,1)S(1)} collective-permute-done((bf16[256,128]{1,0:T(8,128)(2,1)S(1)}, bf16[256,128]{1,0:T(8,128)(2,1)S(1)}, u32[]{:S(2)}, u32[]{:S(2)}) %collective-permute-start.18) | collective-permute-done | bytes 65568 | tf_op jit(solution)/shard_map/ppermute | solution.py:625
  32.9 1.7 %collective-permute-done.19 = bf16[256,128]{1,0:T(8,128)(2,1)S(1)} collective-permute-done((bf16[256,128]{1,0:T(8,128)(2,1)S(1)}, bf16[256,128]{1,0:T(8,128)(2,1)S(1)}, u32[]{:S(2)}, u32[]{:S(2)}) %collective-permute-start.19) | collective-permute-done | bytes 65568 | tf_op jit(solution)/shard_map/ppermute | solution.py:625
  34.6 1.4 %collective-permute-start.20 = (bf16[256,128]{1,0:T(8,128)(2,1)S(1)}, bf16[256,128]{1,0:T(8,128)(2,1)S(1)}, u32[]{:S(2)}, u32[]{:S(2)}) collective-permute-start(bf16[256,128]{1,0:T(8,128)(2,1)S(1)} %add_convert_fusion.own_ref), channel_id=1, source_target_pairs={{0,8},{1,9},{2,10},{3,11},{4,12},{5,13},{6,14},{7,15},{8,16},{9,17... | collective-permute-start | bytes 196616 | tf_op jit(solution)/shard_map/ppermute | solution.py:628
  36.0 1.7 %collective-permute-start.21 = (bf16[256,128]{1,0:T(8,128)(2,1)S(1)}, bf16[256,128]{1,0:T(8,128)(2,1)S(1)}, u32[]{:S(2)}, u32[]{:S(2)}) collective-permute-start(bf16[256,128]{1,0:T(8,128)(2,1)S(1)} %add_convert_fusion.own_ref), channel_id=1, source_target_pairs={{0,24},{1,25},{2,26},{3,27},{4,28},{5,29},{6,30},{7,31},{8,0},{9,1... | collective-permute-start | bytes 196616 | tf_op jit(solution)/shard_map/ppermute | solution.py:628
  37.7 1.4 %collective-permute-start.22 = (bf16[256,128]{1,0:T(8,128)(2,1)S(1)}, bf16[256,128]{1,0:T(8,128)(2,1)S(1)}, u32[]{:S(2)}, u32[]{:S(2)}) collective-permute-start(bf16[256,128]{1,0:T(8,128)(2,1)S(1)} %add_convert_fusion.own_ref), channel_id=1, source_target_pairs={{0,16},{1,17},{2,18},{3,19},{4,20},{5,21},{6,22},{7,23},{8,24},{9,... | collective-permute-start | bytes 196616 | tf_op jit(solution)/shard_map/ppermute | solution.py:628
  39.7 2.6 %hold_blocks.3.held = bf16[64,320,128]{2,1,0:T(8,128)(2,1)S(1)} custom-call(bf16[64,320,128]{2,1,0:T(8,128)(2,1)} %bitcast.10, bf16[256,128]{1,0:T(8,128)(2,1)S(1)} %add_convert_fusion.1.after_ref), custom_call_target="tpu_custom_call" | custom-call | bytes 7500000 | tf_op jit(solution)/shard_map/hold_blocks/pallas_call | solution.py:139
  42.8 2.2 %adjoint.1 = (bf16[336,256]{1,0:T(8,128)(2,1)S(1)}, bf16[96,256]{1,0:T(8,128)(2,1)S(1)}, bf16[96,256]{1,0:T(8,128)(2,1)S(1)}, bf16[96,256]{1,0:T(8,128)(2,1)S(1)...) custom-call(bf16[256,128]{1,0:T(8,128)(2,1)S(1)} %add_convert_fusion, ...), custom_call_target="tpu_custom_call" | custom-call | bytes 9000000 | tf_op jit(solution)/shard_map/adjoint/pallas_call | solution.py:304
  44.9 5.0 %collective-permute-start.23 = (bf16[96,256]{1,0:T(8,128)(2,1)S(1)}, bf16[96,256]{1,0:T(8,128)(2,1)S(1)}, u32[]{:S(2)}, u32[]{:S(2)}) collective-permute-start(bf16[96,256]{1,0:T(8,128)(2,1)S(1)} %get-tuple-element.53), channel_id=1, source_target_pairs={{0,128},{32,160},{64,192},{96,224},{128,0},{160,32},{192,64},{224,... | collective-permute-start | bytes 147464 | tf_op jit(solution)/shard_map/ppermute | solution.py:606
  50.2 4.5 %collective-permute-start.25 = (bf16[96,256]{1,0:T(8,128)(2,1)S(1)}, bf16[96,256]{1,0:T(8,128)(2,1)S(1)}, u32[]{:S(2)}, u32[]{:S(2)}) collective-permute-start(bf16[96,256]{1,0:T(8,128)(2,1)S(1)} %get-tuple-element.55), channel_id=1, source_target_pairs={{0,160},{32,192},{64,224},{96,0},{128,32},{160,64},{192,96},{224,1... | collective-permute-start | bytes 147464 | tf_op jit(solution)/shard_map/ppermute | solution.py:606
  54.7 3.6 %collective-permute-start.27 = (bf16[96,256]{1,0:T(8,128)(2,1)S(1)}, bf16[96,256]{1,0:T(8,128)(2,1)S(1)}, u32[]{:S(2)}, u32[]{:S(2)}) collective-permute-start(bf16[96,256]{1,0:T(8,128)(2,1)S(1)} %get-tuple-element.57), channel_id=1, source_target_pairs={{0,192},{32,224},{64,0},{96,32},{128,64},{160,96},{192,128},{224,1... | collective-permute-start | bytes 147464 | tf_op jit(solution)/shard_map/ppermute | solution.py:606
  58.2 2.7 %collective-permute-start.29 = (bf16[96,256]{1,0:T(8,128)(2,1)S(1)}, bf16[96,256]{1,0:T(8,128)(2,1)S(1)}, u32[]{:S(2)}, u32[]{:S(2)}) collective-permute-start(bf16[96,256]{1,0:T(8,128)(2,1)S(1)} %get-tuple-element.59), channel_id=1, source_target_pairs={{0,224},{32,0},{64,32},{96,64},{128,96},{160,128},{192,160},{224,1... | collective-permute-start | bytes 147464 | tf_op jit(solution)/shard_map/ppermute | solution.py:606
  61.2 1.2 %collective-permute-done.28.refs_6_ = bf16[96,256]{1,0:T(8,128)(2,1)S(1)} collective-permute-done((bf16[96,256]{1,0:T(8,128)(2,1)S(1)}, bf16[96,256]{1,0:T(8,128)(2,1)S(1)}, u32[]{:S(2)}, u32[]{:S(2)}) %collective-permute-start.28) | collective-permute-done | bytes 49184 | tf_op jit(solution)/shard_map/ppermute | solution.py:606
  62.4 1.1 %gradient_planes.1 = (f32[4,4,48,128]{3,2,1,0:T(8,128)S(1)}, bf16[48,512]{1,0:T(8,128)(2,1)S(1)}, bf16[48,512]{1,0:T(8,128)(2,1)S(1)}, s32[1,1]{1,0:T(1,128)}) custom-call(bf16[96,256]{1,0:T(8,128)(2,1)S(1)} %get-tuple-element.52.refs_0_, bf16[96,256]{1,0:T(8,128)(2,1)S(1)} %collective-permute-done.23.refs_1_, ...), custom_call_target="tpu_custom_call" | custom-call | bytes 4500000 | tf_op jit(solution)/shard_map/gradient_planes/pallas_call | solution.py:426
  64.4 5.6 %collective-permute-start.30 = (bf16[48,512]{1,0:T(8,128)(2,1)S(1)}, bf16[48,512]{1,0:T(8,128)(2,1)S(1)}, u32[]{:S(2)}, u32[]{:S(2)}) collective-permute-start(bf16[48,512]{1,0:T(8,128)(2,1)S(1)} %get-tuple-element.68), channel_id=1, source_target_pairs={{0,1},{1,0},{2,3},{3,2},{4,5},{5,4},{6,7},{7,6},{8,9},{9,8},{10,11... | collective-permute-start | bytes 147464 | tf_op jit(solution)/shard_map/ppermute | solution.py:669
  70.0 3.0 %collective-permute-start.31 = (bf16[48,512]{1,0:T(8,128)(2,1)S(1)}, bf16[48,512]{1,0:T(8,128)(2,1)S(1)}, u32[]{:S(2)}, u32[]{:S(2)}) collective-permute-start(bf16[48,512]{1,0:T(8,128)(2,1)S(1)} %get-tuple-element.69), channel_id=1, source_target_pairs={{1,2},{3,4},{5,6},{7,8},{9,10},{11,12},{13,14},{15,16},{17,18},{19... | collective-permute-start | bytes 147464 | tf_op jit(solution)/shard_map/ppermute | solution.py:671
  73.7 3.8 %collective-permute-done.31.outer_ref = bf16[48,512]{1,0:T(8,128)(2,1)S(1)} collective-permute-done((bf16[48,512]{1,0:T(8,128)(2,1)S(1)}, bf16[48,512]{1,0:T(8,128)(2,1)S(1)}, u32[]{:S(2)}, u32[]{:S(2)}) %collective-permute-start.31) | collective-permute-done | bytes 49184 | tf_op jit(solution)/shard_map/ppermute | solution.py:671
  77.5 3.8 %convolutions.1 = f32[4,8,4,512]{3,2,1,0:T(4,128)} custom-call(f32[4,4,48,128]{3,2,1,0:T(8,128)S(1)} %get-tuple-element.48.image_ref, bf16[3,24,16,512]{3,2,1,0:T(8,128)(2,1)S(1)} %stack_rows.1.body, bf16[48,512]{1,0:T(8,128)(2,1)S(1)} %collective-permute-done.30.inner_ref, bf16[48,512]{1,0:T(8,128)(2,1)S(1)} %collective-permute-done.31.outer_ref, ...), custom_call_target="tpu_custom_call" | custom-call | bytes 15000000 | tf_op jit(solution)/shard_map/convolutions/pallas_call | solution.py:546
  (64 shorter events, 6.6 us)
Async XLA Ops:
  0.0 10.0 %collective-permute-start.10 = (bf16[4,8,4,512]{3,2,1,0:T(4,128)(2,1)}, bf16[4,8,4,512]{3,2,1,0:T(4,128)(2,1)S(1)}, u32[]{:S(2)}, u32[]{:S(2)}) collective-permute-start(bf16[4,8,4,512]{3,2,1,0:T(4,128)(2,1)} %own_ref.1), channel_id=1, source_target_pairs={{0,64},{32,96},{64,128},{96,160},{128,192},{160,224},{192,0},{224,... | collective-permute-start | bytes 393224 | tf_op jit(solution)/shard_map/ppermute | solution.py:606
  3.0 10.8 %collective-permute-start.11 = (bf16[4,8,4,512]{3,2,1,0:T(4,128)(2,1)}, bf16[4,8,4,512]{3,2,1,0:T(4,128)(2,1)S(1)}, u32[]{:S(2)}, u32[]{:S(2)}) collective-permute-start(bf16[4,8,4,512]{3,2,1,0:T(4,128)(2,1)} %own_ref.1), channel_id=1, source_target_pairs={{0,192},{32,224},{64,0},{96,32},{128,64},{160,96},{192,128},{224,1... | collective-permute-start | bytes 393224 | tf_op jit(solution)/shard_map/ppermute | solution.py:606
  6.0 11.1 %collective-permute-start.8 = (bf16[4,8,4,512]{3,2,1,0:T(4,128)(2,1)}, bf16[4,8,4,512]{3,2,1,0:T(4,128)(2,1)S(1)}, u32[]{:S(2)}, u32[]{:S(2)}) collective-permute-start(bf16[4,8,4,512]{3,2,1,0:T(4,128)(2,1)} %own_ref.1), channel_id=1, source_target_pairs={{0,32},{32,64},{64,96},{96,128},{128,160},{160,192},{192,224},{224... | collective-permute-start | bytes 393224 | tf_op jit(solution)/shard_map/ppermute | solution.py:606
  6.8 15.7 %collective-permute-start.9 = (bf16[4,8,4,512]{3,2,1,0:T(4,128)(2,1)}, bf16[4,8,4,512]{3,2,1,0:T(4,128)(2,1)S(1)}, u32[]{:S(2)}, u32[]{:S(2)}) collective-permute-start(bf16[4,8,4,512]{3,2,1,0:T(4,128)(2,1)} %own_ref.1), channel_id=1, source_target_pairs={{0,224},{32,0},{64,32},{96,64},{128,96},{160,128},{192,160},{224,1... | collective-permute-start | bytes 393224 | tf_op jit(solution)/shard_map/ppermute | solution.py:606
  10.1 13.2 %collective-permute-start.14 = (bf16[2,8,4,512]{3,2,1,0:T(4,128)(2,1)S(1)}, bf16[2,8,4,512]{3,2,1,0:T(4,128)(2,1)S(1)}, u32[]{:S(2)}, u32[]{:S(2)}) collective-permute-start(bf16[2,8,4,512]{3,2,1,0:T(4,128)(2,1)S(1)} %slice.16), channel_id=1, source_target_pairs={{0,64},{32,96},{64,128},{96,160},{128,192},{160,224},{192,0},{224,... | collective-permute-start | bytes 196616 | tf_op jit(solution)/shard_map/ppermute | solution.py:606
  13.8 9.5 %collective-permute-start.15 = (bf16[2,8,4,512]{3,2,1,0:T(4,128)(2,1)S(1)}, bf16[2,8,4,512]{3,2,1,0:T(4,128)(2,1)S(1)}, u32[]{:S(2)}, u32[]{:S(2)}) collective-permute-start(bf16[2,8,4,512]{3,2,1,0:T(4,128)(2,1)S(1)} %slice.17), channel_id=1, source_target_pairs={{0,192},{32,224},{64,0},{96,32},{128,64},{160,96},{192,128},{224,1... | collective-permute-start | bytes 196616 | tf_op jit(solution)/shard_map/ppermute | solution.py:606
  16.2 7.1 %collective-permute-start.12 = (bf16[4,8,4,512]{3,2,1,0:T(4,128)(2,1)S(1)}, bf16[4,8,4,512]{3,2,1,0:T(4,128)(2,1)S(1)}, u32[]{:S(2)}, u32[]{:S(2)}) collective-permute-start(bf16[4,8,4,512]{3,2,1,0:T(4,128)(2,1)S(1)} %collective-permute-done.10.two_ref.after_ref), channel_id=1, source_target_pairs={{0,32},{32,64},{64,96},{96,128},{128,160},{160,192},{192,224},{224... | collective-permute-start | bytes 393224 | tf_op jit(solution)/shard_map/ppermute | solution.py:606
  17.1 6.2 %collective-permute-start.13 = (bf16[4,8,4,512]{3,2,1,0:T(4,128)(2,1)S(1)}, bf16[4,8,4,512]{3,2,1,0:T(4,128)(2,1)S(1)}, u32[]{:S(2)}, u32[]{:S(2)}) collective-permute-start(bf16[4,8,4,512]{3,2,1,0:T(4,128)(2,1)S(1)} %collective-permute-done.11.back_ref), channel_id=1, source_target_pairs={{0,224},{32,0},{64,32},{96,64},{128,96},{160,128},{192,160},{224,1... | collective-permute-start | bytes 393224 | tf_op jit(solution)/shard_map/ppermute | solution.py:606
  19.9 2.6 %copy-start = (bf16[4,8,4,512]{3,2,1,0:T(4,128)(2,1)S(1)}, bf16[4,8,4,512]{3,2,1,0:T(4,128)(2,1)}, u32[]{:S(2)}) copy-start(bf16[4,8,4,512]{3,2,1,0:T(4,128)(2,1)} %own_ref.1) | copy-start | bytes 393220
  19.9 3.4 %copy-start.1 = (bf16[2,4,128]{2,1,0:T(4,128)(2,1)S(1)}, bf16[2,4,128]{2,1,0:T(4,128)(2,1)}, u32[]{:S(2)}) copy-start(bf16[2,4,128]{2,1,0:T(4,128)(2,1)} %measured_ref.1) | copy-start | bytes 6148
  22.5 4.9 %copy-start.4 = (s32[64,5]{0,1:T(8,128)S(1)}, s32[64,5]{0,1:T(8,128)}, u32[]{:S(2)}) copy-start(s32[64,5]{0,1:T(8,128)} %param.15) | copy-start | bytes 3844
  24.9 3.4 %collective-permute-start.16 = (bf16[256,128]{1,0:T(8,128)(2,1)S(1)}, bf16[256,128]{1,0:T(8,128)(2,1)S(1)}, u32[]{:S(2)}, u32[]{:S(2)}) collective-permute-start(bf16[256,128]{1,0:T(8,128)(2,1)S(1)} %project.1), channel_id=1, source_target_pairs={{0,1},{1,0},{2,3},{3,2},{4,5},{5,4},{6,7},{7,6},{8,9},{9,8},{10,11... | collective-permute-start | bytes 196616 | tf_op jit(solution)/shard_map/ppermute | solution.py:619
  28.3 3.2 %collective-permute-start.17 = (bf16[256,128]{1,0:T(8,128)(2,1)S(1)}, bf16[256,128]{1,0:T(8,128)(2,1)S(1)}, u32[]{:S(2)}, u32[]{:S(2)}) collective-permute-start(bf16[256,128]{1,0:T(8,128)(2,1)S(1)} %add_convert_fusion.1.after_ref), channel_id=1, source_target_pairs={{0,2},{1,3},{2,4},{3,5},{4,6},{5,7},{6,0},{7,1},{8,10},{9,11},{10,... | collective-permute-start | bytes 196616 | tf_op jit(solution)/shard_map/ppermute | solution.py:625
  28.6 4.3 %collective-permute-start.18 = (bf16[256,128]{1,0:T(8,128)(2,1)S(1)}, bf16[256,128]{1,0:T(8,128)(2,1)S(1)}, u32[]{:S(2)}, u32[]{:S(2)}) collective-permute-start(bf16[256,128]{1,0:T(8,128)(2,1)S(1)} %add_convert_fusion.1.after_ref), channel_id=1, source_target_pairs={{0,6},{1,7},{2,0},{3,1},{4,2},{5,3},{6,4},{7,5},{8,14},{9,15},{10,... | collective-permute-start | bytes 196616 | tf_op jit(solution)/shard_map/ppermute | solution.py:625
  29.8 4.7 %collective-permute-start.19 = (bf16[256,128]{1,0:T(8,128)(2,1)S(1)}, bf16[256,128]{1,0:T(8,128)(2,1)S(1)}, u32[]{:S(2)}, u32[]{:S(2)}) collective-permute-start(bf16[256,128]{1,0:T(8,128)(2,1)S(1)} %add_convert_fusion.1.after_ref), channel_id=1, source_target_pairs={{0,4},{1,5},{2,6},{3,7},{4,0},{5,1},{6,2},{7,3},{8,12},{9,13},{10,... | collective-permute-start | bytes 196616 | tf_op jit(solution)/shard_map/ppermute | solution.py:625
  34.6 7.7 %collective-permute-start.20 = (bf16[256,128]{1,0:T(8,128)(2,1)S(1)}, bf16[256,128]{1,0:T(8,128)(2,1)S(1)}, u32[]{:S(2)}, u32[]{:S(2)}) collective-permute-start(bf16[256,128]{1,0:T(8,128)(2,1)S(1)} %add_convert_fusion.own_ref), channel_id=1, source_target_pairs={{0,8},{1,9},{2,10},{3,11},{4,12},{5,13},{6,14},{7,15},{8,16},{9,17... | collective-permute-start | bytes 196616 | tf_op jit(solution)/shard_map/ppermute | solution.py:628
  36.0 6.4 %collective-permute-start.21 = (bf16[256,128]{1,0:T(8,128)(2,1)S(1)}, bf16[256,128]{1,0:T(8,128)(2,1)S(1)}, u32[]{:S(2)}, u32[]{:S(2)}) collective-permute-start(bf16[256,128]{1,0:T(8,128)(2,1)S(1)} %add_convert_fusion.own_ref), channel_id=1, source_target_pairs={{0,24},{1,25},{2,26},{3,27},{4,28},{5,29},{6,30},{7,31},{8,0},{9,1... | collective-permute-start | bytes 196616 | tf_op jit(solution)/shard_map/ppermute | solution.py:628
  37.7 5.1 %collective-permute-start.22 = (bf16[256,128]{1,0:T(8,128)(2,1)S(1)}, bf16[256,128]{1,0:T(8,128)(2,1)S(1)}, u32[]{:S(2)}, u32[]{:S(2)}) collective-permute-start(bf16[256,128]{1,0:T(8,128)(2,1)S(1)} %add_convert_fusion.own_ref), channel_id=1, source_target_pairs={{0,16},{1,17},{2,18},{3,19},{4,20},{5,21},{6,22},{7,23},{8,24},{9,... | collective-permute-start | bytes 196616 | tf_op jit(solution)/shard_map/ppermute | solution.py:628
  42.3 7.6 %copy-start.5 = (f32[32,2,27]{0,1,2:T(2,128)S(1)}, f32[32,2,27]{0,1,2:T(2,128)}, u32[]{:S(2)}) copy-start(f32[32,2,27]{0,1,2:T(2,128)} %param.18) | copy-start | bytes 20740
  42.3 7.8 %copy-start.6 = (f32[32]{0:T(128)S(1)}, f32[32]{0:T(128)}, u32[]{:S(2)}) copy-start(f32[32]{0:T(128)} %param.19) | copy-start | bytes 388
  42.3 30.6 %copy-start.3 = (bf16[55,1536]{1,0:T(8,128)(2,1)S(1)}, bf16[55,1536]{1,0:T(8,128)(2,1)}, u32[]{:S(2)}) copy-start(bf16[55,1536]{1,0:T(8,128)(2,1)} %constant.28.clone) | copy-start | bytes 506884
  42.8 34.7 %copy-start.2 = (f32[32]{0:T(128)S(1)}, f32[32]{0:T(128)}, u32[]{:S(2)}) copy-start(f32[32]{0:T(128)} %out_w_ref.1) | copy-start | bytes 388
  44.9 13.3 %collective-permute-start.23 = (bf16[96,256]{1,0:T(8,128)(2,1)S(1)}, bf16[96,256]{1,0:T(8,128)(2,1)S(1)}, u32[]{:S(2)}, u32[]{:S(2)}) collective-permute-start(bf16[96,256]{1,0:T(8,128)(2,1)S(1)} %get-tuple-element.53), channel_id=1, source_target_pairs={{0,128},{32,160},{64,192},{96,224},{128,0},{160,32},{192,64},{224,... | collective-permute-start | bytes 147464 | tf_op jit(solution)/shard_map/ppermute | solution.py:606
  49.9 8.3 %collective-permute-start.24 = (bf16[96,256]{1,0:T(8,128)(2,1)S(1)}, bf16[96,256]{1,0:T(8,128)(2,1)S(1)}, u32[]{:S(2)}, u32[]{:S(2)}) collective-permute-start(bf16[96,256]{1,0:T(8,128)(2,1)S(1)} %get-tuple-element.54), channel_id=1, source_target_pairs={{0,96},{32,128},{64,160},{96,192},{128,224},{160,0},{192,32},{224,... | collective-permute-start | bytes 147464 | tf_op jit(solution)/shard_map/ppermute | solution.py:606
  50.2 11.0 %collective-permute-start.25 = (bf16[96,256]{1,0:T(8,128)(2,1)S(1)}, bf16[96,256]{1,0:T(8,128)(2,1)S(1)}, u32[]{:S(2)}, u32[]{:S(2)}) collective-permute-start(bf16[96,256]{1,0:T(8,128)(2,1)S(1)} %get-tuple-element.55), channel_id=1, source_target_pairs={{0,160},{32,192},{64,224},{96,0},{128,32},{160,64},{192,96},{224,1... | collective-permute-start | bytes 147464 | tf_op jit(solution)/shard_map/ppermute | solution.py:606
  54.6 6.5 %collective-permute-start.26 = (bf16[96,256]{1,0:T(8,128)(2,1)S(1)}, bf16[96,256]{1,0:T(8,128)(2,1)S(1)}, u32[]{:S(2)}, u32[]{:S(2)}) collective-permute-start(bf16[96,256]{1,0:T(8,128)(2,1)S(1)} %get-tuple-element.56), channel_id=1, source_target_pairs={{0,64},{32,96},{64,128},{96,160},{128,192},{160,224},{192,0},{224,... | collective-permute-start | bytes 147464 | tf_op jit(solution)/shard_map/ppermute | solution.py:606
  54.7 6.5 %collective-permute-start.27 = (bf16[96,256]{1,0:T(8,128)(2,1)S(1)}, bf16[96,256]{1,0:T(8,128)(2,1)S(1)}, u32[]{:S(2)}, u32[]{:S(2)}) collective-permute-start(bf16[96,256]{1,0:T(8,128)(2,1)S(1)} %get-tuple-element.57), channel_id=1, source_target_pairs={{0,192},{32,224},{64,0},{96,32},{128,64},{160,96},{192,128},{224,1... | collective-permute-start | bytes 147464 | tf_op jit(solution)/shard_map/ppermute | solution.py:606
  58.2 4.2 %collective-permute-start.28 = (bf16[96,256]{1,0:T(8,128)(2,1)S(1)}, bf16[96,256]{1,0:T(8,128)(2,1)S(1)}, u32[]{:S(2)}, u32[]{:S(2)}) collective-permute-start(bf16[96,256]{1,0:T(8,128)(2,1)S(1)} %get-tuple-element.58), channel_id=1, source_target_pairs={{0,32},{32,64},{64,96},{96,128},{128,160},{160,192},{192,224},{224... | collective-permute-start | bytes 147464 | tf_op jit(solution)/shard_map/ppermute | solution.py:606
  58.2 4.1 %collective-permute-start.29 = (bf16[96,256]{1,0:T(8,128)(2,1)S(1)}, bf16[96,256]{1,0:T(8,128)(2,1)S(1)}, u32[]{:S(2)}, u32[]{:S(2)}) collective-permute-start(bf16[96,256]{1,0:T(8,128)(2,1)S(1)} %get-tuple-element.59), channel_id=1, source_target_pairs={{0,224},{32,0},{64,32},{96,64},{128,96},{160,128},{192,160},{224,1... | collective-permute-start | bytes 147464 | tf_op jit(solution)/shard_map/ppermute | solution.py:606
  64.4 9.3 %collective-permute-start.30 = (bf16[48,512]{1,0:T(8,128)(2,1)S(1)}, bf16[48,512]{1,0:T(8,128)(2,1)S(1)}, u32[]{:S(2)}, u32[]{:S(2)}) collective-permute-start(bf16[48,512]{1,0:T(8,128)(2,1)S(1)} %get-tuple-element.68), channel_id=1, source_target_pairs={{0,1},{1,0},{2,3},{3,2},{4,5},{5,4},{6,7},{7,6},{8,9},{9,8},{10,11... | collective-permute-start | bytes 147464 | tf_op jit(solution)/shard_map/ppermute | solution.py:669
  70.0 7.5 %collective-permute-start.31 = (bf16[48,512]{1,0:T(8,128)(2,1)S(1)}, bf16[48,512]{1,0:T(8,128)(2,1)S(1)}, u32[]{:S(2)}, u32[]{:S(2)}) collective-permute-start(bf16[48,512]{1,0:T(8,128)(2,1)S(1)} %get-tuple-element.69), channel_id=1, source_target_pairs={{1,2},{3,4},{5,6},{7,8},{9,10},{11,12},{13,14},{15,16},{17,18},{19... | collective-permute-start | bytes 147464 | tf_op jit(solution)/shard_map/ppermute | solution.py:671
